TPU v7x, 256 devices: a whole 4x4x8 slice. The times are simulated.
256 devices in a mesh: aux: 32 (over z, y), rep: 8 (over x, core).
Axes of the slice: x: 4, y: 4, z: 8, core: 2. Of those that a mesh axis runs over, the one named last changes fastest.
Arguments:
- basis_tensor: bfloat16 [1280, 384, 384], P('aux'), may hold values from -6 to 6
- aux_pattern: int32 [20, 6, 6], replicated, may hold values 0 or 1
- green_pattern: int32 [6, 6], replicated, may hold values 0 or 1
- green_occ: bfloat16 [384, 384], replicated, may hold values from -0.3125 to 0.3125
- green_vir: bfloat16 [384, 384], replicated, may hold values from -0.3125 to 0.3125
Outputs:
- chi: float32 [1280, 1280], P('aux', 'rep')
All inputs are finite; a program needn't handle non-finite values.
Results may differ from a plain program's by a relative error of at most 0.0041.
Values may be sent and summed in bfloat16 or wider, within the bound.
No kernel may reach another device: no remote copies, remote signals or barrier semaphores. Data moves between devices by JAX's collectives and lax.ppermute only.
A program may use at most 128 MiB of HBM per device.

v0:
```python
import jax
import jax.numpy as jnp
from jax import lax
from jax.sharding import PartitionSpec as P

BLOCK = 64
ABLOCK = 64


def widen(pattern, size):
    return jnp.repeat(jnp.repeat(pattern, size, axis=-1), size, axis=-2)


def local(basis_tensor, aux_pattern, green_pattern, green_occ, green_vir):
    local_aux = basis_tensor.shape[0]
    orbitals = basis_tensor.shape[1]
    rep_count = lax.axis_size("rep")
    aux_count = lax.axis_size("aux")
    row_count = orbitals // rep_count
    rep_place = lax.axis_index("rep")
    aux_place = lax.axis_index("aux")
    global_rows = aux_place * local_aux + jnp.arange(local_aux, dtype=jnp.int32)
    block_ids = global_rows // ABLOCK
    selector = (
        block_ids[:, None] == jnp.arange(aux_pattern.shape[0], dtype=jnp.int32)[None, :]
    ).astype(jnp.int32)
    local_pattern = jnp.sum(selector[:, :, None, None] * aux_pattern[None], axis=1)
    masked = basis_tensor * widen(local_pattern, BLOCK).astype(jnp.bfloat16)
    green_mask = widen(green_pattern, BLOCK).astype(jnp.bfloat16)
    occ = green_occ * green_mask
    vir = green_vir * green_mask
    occ_rows = lax.dynamic_slice_in_dim(occ, rep_place * row_count, row_count, 0)
    basis_rows = lax.dynamic_slice_in_dim(masked, rep_place * row_count, row_count, 1)
    first = jnp.einsum("mk,qkn->qmn", occ_rows, masked, preferred_element_type=jnp.float32).astype(
        jnp.bfloat16
    )
    product = jnp.einsum("qmk,kn->qmn", first, vir, preferred_element_type=jnp.float32).astype(
        jnp.bfloat16
    )
    pair_basis, pair_product = (
        lax.all_to_all(basis_rows, "aux", split_axis=2, concat_axis=0, tiled=True),
        lax.all_to_all(product, "aux", split_axis=2, concat_axis=0, tiled=True),
    )
    total_aux = pair_basis.shape[0]
    flat_basis = pair_basis.reshape(total_aux, -1)
    flat_product = pair_product.reshape(total_aux, -1)
    partial_value = lax.dot_general(
        flat_basis, flat_product, (((1,), (1,)), ((), ())), preferred_element_type=jnp.float32
    )
    partial_value = partial_value * (1.0 / orbitals)
    column_count = total_aux // rep_count
    tiles = partial_value.reshape(aux_count, local_aux, rep_count, column_count)
    tiles = jnp.transpose(tiles, (0, 2, 1, 3)).reshape(
        aux_count * rep_count * local_aux, column_count
    )
    return lax.psum_scatter(tiles, ("aux", "rep"), scatter_dimension=0, tiled=True)


def solution(mesh):
    return jax.shard_map(
        local,
        mesh=mesh,
        in_specs=(P("aux", None, None), P(), P(), P(), P()),
        out_specs=P("aux", "rep"),
        check_vma=False,
    )
```

profile of v0, /device:TPU:2, one launch (start us, length us, event | category | flops | bytes accessed | tf_op | source)
XLA Modules:
  0.0 1453.5 jit_solution(14609078557500777313)
XLA Ops:
  6.6 0.9 multiply_reduce_fusion
  7.5 0.1 copy.31
  7.7 0.3 broadcast_in_dim.16
  8.0 0.3 convert_element_type.40
  8.3 6.3 bitcast_multiply_fusion
  14.7 0.0 copy-start
  14.7 4.4 copy-done
  19.1 0.2 constant_dynamic-slice_fusion
  19.2 4.3 copy.33
  23.5 0.0 copy-start.2
  23.5 0.0 copy-start.1
  23.5 8.1 reshape.69
  31.6 11.5 all-to-all-start
  43.1 0.0 copy-done.2
  43.1 0.1 broadcast_in_dim.18
  43.2 0.1 convert_element_type.43
  43.3 0.0 copy-done.1
  43.3 7.5 convolution_convert_fusion.1
  50.8 4.3 copy.35
  55.1 8.1 reshape.71
  63.2 16.9 %all-to-all-done = bf16[32,2,11520]{2,1,0:T(2,128)(2,1)S(1)} async-done(((bf16[32,2,11520]{2,1,0:T(2,128)(2,1)}), bf16[32,2,11520]{2,1,0:T(2,128)(2,1)S(1)}, u32[]{:S(2)}, u32[]{:S(2)}) %all-to-all-start) | async-done | bytes 1474592 | tf_op jit(solution)/shard_map/all_to_all | solution.py:41
  80.1 5.7 all-to-all-start.1
  85.8 0.2 reduce-scatter.2.cloned.1.call-start
  86.1 5.2 reshape.70
  91.2 9.2 copy.34
  100.5 7.5 reshape.63
  108.0 13.7 all-to-all-done.1
  121.7 5.1 reshape.72
  126.8 9.2 copy.36
  136.1 7.5 reshape.64
  143.6 4.6 convolution_multiply_fusion
  148.3 10.9 reshape.65
  159.1 12.1 copy.37
  171.2 0.0 reduce-scatter.2.cloned.1.call-update
  171.3 1275.4 %reduce-scatter.2.cloned.1.call-done = f32[40,160]{1,0:T(8,128)} async-done(((f32[10240,160]{1,0:T(8,128)}), f32[40,160]{1,0:T(8,128)}) %reduce-scatter.2.cloned.1.call-update) | async-done | bytes 25616 | tf_op jit(solution)/shard_map/reduce_scatter | solution.py:56
  (6 shorter events, 0.1 us)
Async XLA Ops:
  14.7 4.4 copy-start
  23.5 19.6 %copy-start.2 = (s32[6,6]{1,0:T(8,128)S(1)}, s32[6,6]{1,0:T(8,128)}, u32[]{:S(2)}) copy-start(s32[6,6]{1,0:T(8,128)} %param.7) | copy-start | bytes 436
  23.5 19.8 %copy-start.1 = (bf16[384,384]{1,0:T(8,128)(2,1)S(1)}, bf16[384,384]{1,0:T(8,128)(2,1)}, u32[]{:S(2)}) copy-start(bf16[384,384]{1,0:T(8,128)(2,1)} %param.9) | copy-start | bytes 884740
  31.6 48.5 %all-to-all-start = ((bf16[32,2,11520]{2,1,0:T(2,128)(2,1)}), bf16[32,2,11520]{2,1,0:T(2,128)(2,1)S(1)}, u32[]{:S(2)}, u32[]{:S(2)}) async-start(bf16[32,2,11520]{2,1,0:T(2,128)(2,1)} %reshape.69), calls=%async_computation | async-start | bytes 2949120 | tf_op jit(solution)/shard_map/all_to_all | solution.py:41
  80.1 41.6 %all-to-all-start.1 = ((bf16[32,2,11520]{2,1,0:T(2,128)(2,1)}), bf16[32,2,11520]{2,1,0:T(2,128)(2,1)S(1)}, u32[]{:S(2)}, u32[]{:S(2)}) async-start(bf16[32,2,11520]{2,1,0:T(2,128)(2,1)} %reshape.71), calls=%async_computation.1 | async-start | bytes 2949120 | tf_op jit(solution)/shard_map/all_to_all | solution.py:42
  85.8 1360.8 %reduce-scatter.2.cloned.1.call-start = ((), (), s32[]{:S(2)}) async-start(), calls=%async_computation.3 | async-start | bytes 10526720 | tf_op jit(solution)/shard_map/reduce_scatter | solution.py:56
Sparse Core Ops, SparseCore 0:
  171.4 1275.2 reduce-scatter.1
where the time goes:
time: 1460 us; the launch traced here: 1450 us
  waiting for transfers between devices  1310 us (90%)
  local copies, waits for them, and re-layouts  97.1 us (7%)
  starting transfers between devices  17.4 us (1%)
    reduce_scatter x1, waiting for transfers between devices, local(): lax.psum_scatter(tiles, ('aux', 'rep'), scatter_dimension=0, tiled=True)  1280 us
    unnamed x10, local copies, waits for them, and re-layouts  30.8 us
  transfers between devices with their start and end apart: 3, of which 3 were waited for; matrix products, arithmetic and copies ran while one was open for 3% of the time, Pallas kernels for 0%

commit v1 on v0

v1 whole, which is shorter than its diff:
```python
import functools

import jax
import jax.numpy as jnp
from jax import lax
from jax.experimental import pallas as pl
from jax.experimental.pallas import tpu as pltpu
from jax.sharding import Mesh, PartitionSpec as P

BLOCK = 64
ABLOCK = 64
NZ, NY, NX, NC = 8, 4, 4, 2
NR = NX * NC
LA = 40
NAO = 384
ROWS = NAO // NR
SUB = ROWS // NZ
HALF = SUB * NAO // 2
NB = NAO // BLOCK
F32 = jnp.float32
BF16 = jnp.bfloat16
LIMIT = 56 * 1024 * 1024


def row_mask(read, width=NAO):
    lane = lax.broadcasted_iota(jnp.int32, (1, width), 1) // BLOCK
    out = jnp.zeros((1, width), F32)
    for n in range(NB):
        out = jnp.where(lane == n, read(n).astype(F32), out)
    return out


def emit_chunks(sc_ref, held, own_ref, plus_ref, minus_ref):
    z = sc_ref[1]
    for d in range(NZ):
        dest = lax.rem(z + d, NZ)
        for j in range(SUB):
            h = j // 3
            if d == 0:
                out_ref, place = own_ref, h
            elif d < 4:
                out_ref, place = plus_ref, 2 * (d - 1) + h
            elif d > 4:
                out_ref, place = minus_ref, 2 * (7 - d) + h
            else:
                out_ref, place = (plus_ref, minus_ref)[h], 6
            for t in range(NAO // 128):
                rows = held[t, pl.ds(dest * SUB + j, LA, stride=ROWS), :]
                out_ref[place, :, pl.ds((j % 3) * NAO + 128 * t, 128)] = rows.astype(BF16)


def prep_kernel(sc_ref, pat_ref, basis_ref, own_ref, plus_ref, minus_ref, held):
    r, place = sc_ref[0], sc_ref[2]
    for o in range(LA // 8):
        b = (place * LA + 8 * o) // ABLOCK
        for jo in range(ROWS // 8):
            mb = (r * ROWS + 8 * jo) // BLOCK
            mask = row_mask(lambda n: pat_ref[(b * NB + mb) * NB + n])
            for p in range(8 * o, 8 * o + 8):
                rows = basis_ref[p, pl.ds(8 * jo, 8), :].astype(F32) * mask
                for t in range(NAO // 128):
                    held[t, pl.ds(p * ROWS + 8 * jo, 8), :] = rows[:, 128 * t : 128 * t + 128]
    emit_chunks(sc_ref, held, own_ref, plus_ref, minus_ref)


CHUNKS = (
    jax.ShapeDtypeStruct((2, LA, HALF), BF16),
    jax.ShapeDtypeStruct((7, LA, HALF), BF16),
    jax.ShapeDtypeStruct((7, LA, HALF), BF16),
)
CHUNK_SPECS = tuple(pl.BlockSpec(s.shape, lambda *_: (0, 0, 0)) for s in CHUNKS)


def prep(sc, pat, basis):
    return pl.pallas_call(
        prep_kernel,
        out_shape=CHUNKS,
        grid_spec=pltpu.PrefetchScalarGridSpec(
            num_scalar_prefetch=2,
            grid=(1,),
            in_specs=[pl.BlockSpec((LA, ROWS, NAO), lambda i, sc, pat: (0, sc[0], 0))],
            out_specs=CHUNK_SPECS,
            scratch_shapes=[pltpu.VMEM((NAO // 128, LA * ROWS, 128), F32)],
        ),
        compiler_params=pltpu.CompilerParams(vmem_limit_bytes=LIMIT),
        cost_estimate=pl.CostEstimate(flops=10**6, bytes_accessed=3 * 10**6, transcendentals=0),
        name="prep",
    )(sc, pat, basis)


STEPQ = 8


def product_kernel(
    sc_ref, pat_ref, gpat_ref, basis_ref, occ_ref, vir_ref, own_ref, plus_ref, minus_ref,
    first, held, occ, vir, masks,
):
    i = pl.program_id(0)
    r, place = sc_ref[0], sc_ref[2]
    b0 = (place * LA) // ABLOCK
    nblocks = pat_ref.shape[0] // (NB * NB)

    @pl.when(i == 0)
    def _():
        for mb in range(NB):
            rows = pl.ds(mb * BLOCK, BLOCK)
            g = row_mask(lambda n: gpat_ref[mb * NB + n]).astype(BF16)
            vir[rows, :] = vir_ref[rows, :] * g
            for k in range(2):
                b = jnp.minimum(b0 + k, nblocks - 1)
                m = row_mask(lambda n: pat_ref[(b * NB + mb) * NB + n])
                masks[k, rows, :] = jnp.broadcast_to(m, (BLOCK, NAO)).astype(BF16)
        for jo in range(ROWS // 16):
            gb = (r * ROWS + 16 * jo) // BLOCK
            g = row_mask(lambda n: gpat_ref[gb * NB + n]).astype(BF16)
            rows = pl.ds(16 * jo, 16)
            occ[rows, :] = occ_ref[rows, :] * g

    which = (place * LA + STEPQ * i) // ABLOCK - b0
    mask = masks[which]
    rows_r = occ[...]
    for q in range(STEPQ):
        masked = basis_ref[q] * mask
        f = jnp.dot(rows_r, masked, preferred_element_type=F32).astype(BF16)
        first[pl.ds(pl.multiple_of((STEPQ * i + q) * ROWS, 16), ROWS), :] = f

    @pl.when(i == LA // STEPQ - 1)
    def _():
        v = vir[...]
        n = LA * ROWS // 4
        for t in range(4):
            part = jnp.dot(first[pl.ds(t * n, n), :], v, preferred_element_type=F32)
            for u in range(NAO // 128):
                held[u, pl.ds(t * n, n), :] = part[:, 128 * u : 128 * u + 128]
        emit_chunks(sc_ref, held, own_ref, plus_ref, minus_ref)


def products(sc, pat, gpat, basis, occ, vir):
    return pl.pallas_call(
        product_kernel,
        out_shape=CHUNKS,
        grid_spec=pltpu.PrefetchScalarGridSpec(
            num_scalar_prefetch=3,
            grid=(LA // STEPQ,),
            in_specs=[
                pl.BlockSpec((STEPQ, NAO, NAO), lambda i, *_: (i, 0, 0)),
                pl.BlockSpec((ROWS, NAO), lambda i, sc, pat, gpat: (sc[0], 0)),
                pl.BlockSpec((NAO, NAO), lambda i, *_: (0, 0)),
            ],
            out_specs=CHUNK_SPECS,
            scratch_shapes=[
                pltpu.VMEM((LA * ROWS, NAO), BF16),
                pltpu.VMEM((NAO // 128, LA * ROWS, 128), F32),
                pltpu.VMEM((ROWS, NAO), BF16),
                pltpu.VMEM((NAO, NAO), BF16),
                pltpu.VMEM((2, NAO, NAO), BF16),
            ],
        ),
        compiler_params=pltpu.CompilerParams(vmem_limit_bytes=LIMIT),
        cost_estimate=pl.CostEstimate(
            flops=4 * LA * ROWS * NAO * NAO, bytes_accessed=14 * 10**6, transcendentals=0
        ),
        name="products",
    )(sc, pat, gpat, basis, occ, vir)


def shift(value, by, axis, n):
    return lax.ppermute(value, axis, [(i, (i + by) % n) for i in range(n)])


def along_z(own, plus, minus):
    got = {(0, 0): (own, 0), (0, 1): (own, 1)}
    for t in range(1, 5):
        plus, minus = shift(plus, 1, "z", NZ), shift(minus, -1, "z", NZ)
        if t < 4:
            for h in range(2):
                got[t, h] = (plus, h)
                got[8 - t, h] = (minus, h)
            plus, minus = plus[2:], minus[2:]
        else:
            got[4, 0] = (plus, 0)
            got[4, 1] = (minus, 0)
    return got


GROUPS = (
    ((0, 0), (0, 1), (1, 0), (1, 1), (7, 0), (7, 1)),
    ((2, 0), (2, 1), (6, 0), (6, 1), (3, 0), (3, 1), (5, 0), (5, 1), (4, 0), (4, 1)),
)


def along_y(got):
    out = {}
    for keys in GROUPS:
        group = jnp.concatenate([got[k][0][got[k][1]][None] for k in keys], axis=0)
        n = len(keys) // 2
        below, above = shift(group, 1, "y", NY), shift(group, -1, "y", NY)
        far = shift(below[:n], 1, "y", NY), shift(above[n:], -1, "y", NY)
        for i, (d, h) in enumerate(keys):
            out[d, 0, h] = (group, i)
            out[d, 1, h] = (below, i)
            out[d, 3, h] = (above, i)
            out[d, 2, h] = (far[i // n], i % n)
    return out


TILE = 256


def contract_kernel(m_places, p_places, n_arrays, sc_ref, *refs):
    arrays, (keep_ref, send_ref, left, right) = refs[:n_arrays], refs[n_arrays:]
    z, c = sc_ref[1], sc_ref[3]
    first_even = lax.rem(z + c, 2) == 0
    for (d, h), (a, i) in p_places.items():
        left[h, pl.ds(d * LA, LA), :] = arrays[a][i]
    for (d, e, h), (a, i) in m_places.items():
        right[h, pl.ds((d * NY + e) * LA, LA), :] = arrays[a][i]

    @pl.loop(0, NZ * NY * LA // TILE)
    def _(t):
        cols = pl.ds(pl.multiple_of(t * TILE, TILE), TILE)
        acc = jnp.zeros((NZ * LA, TILE), F32)
        for h in range(2):
            acc += lax.dot_general(
                left[h], right[h, cols, :], (((1,), (1,)), ((), ())), preferred_element_type=F32
            )
        acc = acc.reshape(NZ // 2, 2, LA, TILE)
        keep_ref[:, :, cols] = jnp.where(first_even, acc[:, 0], acc[:, 1])
        send_ref[:, :, cols] = jnp.where(first_even, acc[:, 1], acc[:, 0])


def contract(sc, m, p):
    arrays, index = [], {}

    def places(table):
        out = {}
        for key, (array, i) in table.items():
            if id(array) not in index:
                index[id(array)] = len(arrays)
                arrays.append(array)
            out[key] = (index[id(array)], i)
        return out

    m_places, p_places = places(m), places(p)
    shape = jax.ShapeDtypeStruct((NZ // 2, LA, NZ * NY * LA), F32)
    return pl.pallas_call(
        functools.partial(contract_kernel, m_places, p_places, len(arrays)),
        out_shape=(shape, shape),
        in_specs=[pl.BlockSpec(memory_space=pltpu.SMEM)]
        + [pl.BlockSpec(memory_space=pltpu.VMEM)] * len(arrays),
        out_specs=(pl.BlockSpec(memory_space=pltpu.VMEM),) * 2,
        scratch_shapes=[
            pltpu.VMEM((2, NZ * LA, HALF), BF16),
            pltpu.VMEM((2, NZ * NY * LA, HALF), BF16),
        ],
        compiler_params=pltpu.CompilerParams(vmem_limit_bytes=LIMIT),
        cost_estimate=pl.CostEstimate(
            flops=4 * 320 * 1280 * 1152, bytes_accessed=10**7, transcendentals=0
        ),
        name="contract",
    )(sc, *arrays)


def pair_kernel(sc_ref, a_ref, b_ref, out_ref):
    out_ref[...] = a_ref[...] + b_ref[...]


def pair_sum(sc, keep, recv):
    block = (1,) + keep.shape[1:]

    def source(i, sc):
        first = lax.rem(sc[1] + sc[3], 2)
        return (lax.rem((sc[1] - first - sc[3]) // 2 - i + 8, NX), 0, 0)

    return pl.pallas_call(
        pair_kernel,
        out_shape=jax.ShapeDtypeStruct(keep.shape, F32),
        grid_spec=pltpu.PrefetchScalarGridSpec(
            num_scalar_prefetch=1,
            grid=(NX,),
            in_specs=[pl.BlockSpec(block, source)] * 2,
            out_specs=pl.BlockSpec(block, lambda i, sc: (i, 0, 0)),
        ),
        name="pair_sum",
    )(sc, keep, recv)


def pack_kernel(sc_ref, in_ref, out_ref):
    z, y = sc_ref[1], sc_ref[4]
    total = (in_ref[0] + in_ref[1]) + (in_ref[2] + in_ref[3])
    for d in range(NZ):
        for e in range(NY):
            k = d * NY + e
            part = total[:, k * LA : (k + 1) * LA]
            oct8 = [part[8 * o : 8 * o + 8] for o in range(5)]
            fill = jnp.zeros((8, 8), F32)
            upper = jnp.concatenate([oct8[0], oct8[1], oct8[2], fill], axis=1)
            lower = jnp.concatenate([oct8[3], oct8[4], jnp.zeros((8, 48), F32)], axis=1)
            dest = lax.rem(z - d + NZ, NZ) * NY + lax.rem(y - e + NY, NY)
            out_ref[dest, 0:8, :] = upper
            out_ref[dest, 8:16, :] = lower


def pack(sc, value):
    return pl.pallas_call(
        pack_kernel,
        out_shape=jax.ShapeDtypeStruct((NZ * NY, 16, 128), F32),
        in_specs=[
            pl.BlockSpec(memory_space=pltpu.SMEM),
            pl.BlockSpec(memory_space=pltpu.VMEM),
        ],
        out_specs=pl.BlockSpec(memory_space=pltpu.VMEM),
        name="pack",
    )(sc, value)


def finish_kernel(in_ref, out_ref):
    parts = []
    for y in range(NY):
        total = in_ref[y]
        for z in range(1, NZ):
            total = total + in_ref[z * NY + y]
        for o in range(5):
            lo = (o % 3) * LA
            parts.append(total[8 * (o // 3) : 8 * (o // 3) + 8, lo : lo + LA])
    rows = jnp.concatenate(parts, axis=0)
    rows = jnp.concatenate([rows, jnp.zeros((NY * LA, 128 - LA), F32)], axis=1)
    rows = jnp.concatenate([rows, jnp.zeros((256 - NY * LA, 128), F32)], axis=0)
    out_ref[...] = rows.T[:LA, : NY * LA] * (1.0 / NAO)


def finish(value):
    return pl.pallas_call(
        finish_kernel,
        out_shape=jax.ShapeDtypeStruct((LA, NY * LA), F32),
        in_specs=[pl.BlockSpec(memory_space=pltpu.VMEM)],
        out_specs=pl.BlockSpec(memory_space=pltpu.VMEM),
        name="finish",
    )(value)


def local(basis, aux_pattern, green_pattern, green_occ, green_vir):
    z, y, x, c = (lax.axis_index(a) for a in ("z", "y", "x", "core"))
    sc = jnp.stack([x * NC + c, z, z * NY + y, c, y, x]).astype(jnp.int32)
    pat, gpat = aux_pattern.reshape(-1), green_pattern.reshape(-1)
    m = along_y(along_z(*prep(sc, pat, basis)))
    p = along_z(*products(sc, pat, gpat, basis, green_occ, green_vir))
    keep, send = contract(sc, m, p)
    recv = shift(send, 1, "core", NC)
    by_x = lax.all_to_all(pair_sum(sc, keep, recv), "x", split_axis=0, concat_axis=0, tiled=True)
    by_zy = lax.all_to_all(pack(sc, by_x), ("z", "y"), split_axis=0, concat_axis=0, tiled=True)
    return finish(by_zy)


def solution(mesh):
    fine = Mesh(mesh.devices.reshape(NZ, NY, NX, NC), ("z", "y", "x", "core"))
    return jax.shard_map(
        local,
        mesh=fine,
        in_specs=(P(("z", "y"), None, None), P(), P(), P(), P()),
        out_specs=P(("z", "y"), ("x", "core")),
        check_vma=False,
    )
```

time: 1460 us -> 181 us (0.12)
  waiting for transfers between devices: 1310 us -> 57.7 us
  local copies, waits for them, and re-layouts: 97.1 us -> 9.58 us
  blocking collectives: 0 us -> 37.8 us
  Pallas kernels: 0 us -> 31.6 us
  starting transfers between devices: 17.4 us -> 43.4 us
    reduce_scatter x1 -> x0, waiting for transfers between devices: 1280 us -> none  [local(): lax.psum_scatter(tiles, ('aux', 'rep'), scatter_dimension=0, tiled=True)]
    ppermute x0 -> x25, waiting for transfers between devices: none -> 57.7 us  [shift(): return lax.ppermute(value, axis, [(i, (i + by) % n) for i in range(n)])]
    ppermute x0 -> x25, starting transfers between devices: none -> 43.4 us  [shift(): return lax.ppermute(value, axis, [(i, (i + by) % n) for i in range(n)])]
    all_to_all x0 -> x2, blocking collectives: none -> 37.8 us  [the longest x1 21.2 us: local(): lax.all_to_all(pack(sc, by_x), ('z', 'y'), split_axis=0, concat_axis=0, t...]
    pallas_call x0 -> x6, Pallas kernels: none -> 31.6 us  [the longest x1 11 us: products(): pl.pallas_call(product_kernel, out_shape=CHUNKS, grid_spec=pltpu.Prefetch...]
    all_to_all x2 -> x0, waiting for transfers between devices: 30.6 us -> none  [the longest x1 16.9 us: local(): lax.all_to_all(basis_rows, 'aux', split_axis=2, concat_axis=0, tiled=True)]
    unnamed x10 -> x48, local copies, waits for them, and re-layouts: 30.8 us -> 5.27 us
    reshape x3 -> x2, local copies, waits for them, and re-layouts: 25.9 us -> 1.39 us  [local(): pat, gpat = (aux_pattern.reshape(-1), green_pattern.reshape(-1))]
  transfers between devices with their start and end apart: 3 -> 25, of which waited for: 3 -> 11; matrix products, arithmetic and copies ran while one was open for 3% -> 3% of each run, Pallas kernels for 0% -> 6%
where the time goes in v1:
time: 181 us
  waiting for transfers between devices  57.7 us (32%)
  starting transfers between devices  43.4 us (24%)
  blocking collectives  37.8 us (21%)
  Pallas kernels  31.6 us (17%)
  local copies, waits for them, and re-layouts  9.58 us (5%)
    ppermute x25, waiting for transfers between devices, shift(): return lax.ppermute(value, axis, [(i, (i + by) % n) for i in range(n)])  57.7 us
    ppermute x25, starting transfers between devices, shift(): return lax.ppermute(value, axis, [(i, (i + by) % n) for i in range(n)])  43.4 us
    all_to_all x1, blocking collectives, local(): lax.all_to_all(pack(sc, by_x), ('z', 'y'), split_axis=0, concat_axis=0, t...  21.2 us
    all_to_all x1, blocking collectives, local(): lax.all_to_all(pair_sum(sc, keep, recv), 'x', split_axis=0, concat_axis=0...  16.6 us
    pallas_call x1, Pallas kernels, products(): pl.pallas_call(product_kernel, out_shape=CHUNKS, grid_spec=pltpu.Prefetch...  11 us
    pallas_call x1, Pallas kernels, contract(): pl.pallas_call(functools.partial(contract_kernel, m_places, p_places, len...  8.27 us
    unnamed x48, local copies, waits for them, and re-layouts  5.27 us
    pallas_call x1, Pallas kernels, prep(): pl.pallas_call(prep_kernel, out_shape=CHUNKS, grid_spec=pltpu.PrefetchSca...  4.31 us
  transfers between devices with their start and end apart: 25, of which 11 were waited for; matrix products, arithmetic and copies ran while one was open for 3% of the time, Pallas kernels for 6%

profile of v1, /device:TPU:2, one launch (start us, length us, event | category | flops | bytes accessed | tf_op | source)
XLA Modules:
  0.0 180.6 jit_solution(6965327718650261973)
XLA Ops:
  0.0 0.9 copy.6
  0.9 0.7 reshape.6.pat_ref
  1.6 0.6 stack.27.sc_ref
  2.2 4.3 %prep.1 = (bf16[2,40,1152]{2,1,0:T(8,128)(2,1)}, bf16[7,40,1152]{2,1,0:T(8,128)(2,1)}, bf16[7,40,1152]{2,1,0:T(8,128)(2,1)}) custom-call(s32[6]{0:T(128)} %stack.27.sc_ref, s32[720]{0:T(1024)} %reshape.6.pat_ref, bf16[40,384,384]{2,1,0:T(8,128)(2,1)} %basis_ref.3), custom_call_target="tpu_custom_call" | custom-call | flops 1000000 | bytes 3000000 | tf_op jit(solution)/shard_map/prep/pallas_call | solution.py:75
  6.5 1.9 %collective-permute-start = (bf16[7,40,1152]{2,1,0:T(8,128)(2,1)}, bf16[7,40,1152]{2,1,0:T(8,128)(2,1)S(1)}, u32[]{:S(2)}, u32[]{:S(2)}) collective-permute-start(bf16[7,40,1152]{2,1,0:T(8,128)(2,1)} %get-tuple-element.14), channel_id=1, source_target_pairs={{0,32},{32,64},{64,96},{96,128},{128,160},{160,192},{192,224},{224... | collective-permute-start | bytes 1935368 | tf_op jit(solution)/shard_map/ppermute | solution.py:168
  8.4 3.9 %collective-permute-start.1 = (bf16[7,40,1152]{2,1,0:T(8,128)(2,1)}, bf16[7,40,1152]{2,1,0:T(8,128)(2,1)S(1)}, u32[]{:S(2)}, u32[]{:S(2)}) collective-permute-start(bf16[7,40,1152]{2,1,0:T(8,128)(2,1)} %get-tuple-element.15), channel_id=1, source_target_pairs={{0,224},{32,0},{64,32},{96,64},{128,96},{160,128},{192,160},{224,1... | collective-permute-start | bytes 1935368 | tf_op jit(solution)/shard_map/ppermute | solution.py:168
  12.4 14.7 %collective-permute-done = bf16[7,40,1152]{2,1,0:T(8,128)(2,1)S(1)} collective-permute-done((bf16[7,40,1152]{2,1,0:T(8,128)(2,1)}, bf16[7,40,1152]{2,1,0:T(8,128)(2,1)S(1)}, u32[]{:S(2)}, u32[]{:S(2)}) %collective-permute-start) | collective-permute-done | bytes 645152 | tf_op jit(solution)/shard_map/ppermute | solution.py:168
  27.1 0.1 collective-permute-start.6
  27.2 0.0 collective-permute-done.1
  27.3 3.3 %collective-permute-start.7 = (bf16[5,40,1152]{2,1,0:T(8,128)(2,1)S(1)}, bf16[5,40,1152]{2,1,0:T(8,128)(2,1)}, u32[]{:S(2)}, u32[]{:S(2)}) collective-permute-start(bf16[5,40,1152]{2,1,0:T(8,128)(2,1)S(1)} %slice.109), channel_id=1, source_target_pairs={{0,224},{32,0},{64,32},{96,64},{128,96},{160,128},{192,160},{224,1... | collective-permute-start | bytes 1382408 | tf_op jit(solution)/shard_map/ppermute | solution.py:168
  30.6 0.7 reshape.7.gpat_ref
  31.2 11.0 %products.1 = (bf16[2,40,1152]{2,1,0:T(8,128)(2,1)}, bf16[7,40,1152]{2,1,0:T(8,128)(2,1)}, bf16[7,40,1152]{2,1,0:T(8,128)(2,1)}) custom-call(s32[6]{0:T(128)} %stack.27.sc_ref, s32[720]{0:T(1024)} %reshape.6.pat_ref, s32[36]{0:T(128)} %reshape.7.gpat_ref, bf16[40,384,384]{2,1,0:T(8,128)(2,1)} %basis_ref.3, bf16[384,384]{1,0:T(8,128)(2,1)} %occ_ref.1, ...), custom_call_target="tpu_custom_call" | custom-call | flops 1132462080 | bytes 14000000 | tf_op jit(solution)/shard_map/products/pallas_call | solution.py:139
  42.2 0.0 collective-permute-start.16
  42.2 3.2 %collective-permute-start.17 = (bf16[7,40,1152]{2,1,0:T(8,128)(2,1)}, bf16[7,40,1152]{2,1,0:T(8,128)(2,1)S(1)}, u32[]{:S(2)}, u32[]{:S(2)}) collective-permute-start(bf16[7,40,1152]{2,1,0:T(8,128)(2,1)} %get-tuple-element.18), channel_id=1, source_target_pairs={{0,224},{32,0},{64,32},{96,64},{128,96},{160,128},{192,160},{224,1... | collective-permute-start | bytes 1935368 | tf_op jit(solution)/shard_map/ppermute | solution.py:168
  45.5 1.0 slice.111
  46.4 0.1 collective-permute-start.8
  46.5 0.0 collective-permute-done.7
  46.5 1.0 slice.113
  47.5 3.3 %collective-permute-start.9 = (bf16[3,40,1152]{2,1,0:T(8,128)(2,1)S(1)}, bf16[3,40,1152]{2,1,0:T(8,128)(2,1)S(1)}, u32[]{:S(2)}, u32[]{:S(2)}) collective-permute-start(bf16[3,40,1152]{2,1,0:T(8,128)(2,1)S(1)} %slice.113), channel_id=1, source_target_pairs={{0,224},{32,0},{64,32},{96,64},{128,96},{160,128},{192,160},{224,1... | collective-permute-start | bytes 829448 | tf_op jit(solution)/shard_map/ppermute | solution.py:168
  50.8 0.9 slice_dynamic-update-slice_fusion.3
  51.8 0.9 slice_dynamic-update-slice_fusion.2
  52.7 12.0 %collective-permute-done.8 = bf16[3,40,1152]{2,1,0:T(8,128)(2,1)S(1)} collective-permute-done((bf16[3,40,1152]{2,1,0:T(8,128)(2,1)S(1)}, bf16[3,40,1152]{2,1,0:T(8,128)(2,1)S(1)}, u32[]{:S(2)}, u32[]{:S(2)}) %collective-permute-start.8) | collective-permute-done | bytes 276512 | tf_op jit(solution)/shard_map/ppermute | solution.py:168
  64.7 0.1 collective-permute-start.10
  64.8 0.0 collective-permute-done.9
  64.8 3.5 %collective-permute-start.11 = (bf16[1,40,1152]{2,1,0:T(8,128)(2,1)S(1)}, bf16[1,40,1152]{2,1,0:T(8,128)(2,1)S(1)}, u32[]{:S(2)}, u32[]{:S(2)}) collective-permute-start(bf16[1,40,1152]{2,1,0:T(8,128)(2,1)S(1)} %slice.116), channel_id=1, source_target_pairs={{0,224},{32,0},{64,32},{96,64},{128,96},{160,128},{192,160},{224,1... | collective-permute-start | bytes 276488 | tf_op jit(solution)/shard_map/ppermute | solution.py:168
  68.3 2.2 %collective-permute-done.10 = bf16[1,40,1152]{2,1,0:T(8,128)(2,1)S(1)} collective-permute-done((bf16[1,40,1152]{2,1,0:T(8,128)(2,1)S(1)}, bf16[1,40,1152]{2,1,0:T(8,128)(2,1)S(1)}, u32[]{:S(2)}, u32[]{:S(2)}) %collective-permute-start.10) | collective-permute-done | bytes 92192 | tf_op jit(solution)/shard_map/ppermute | solution.py:168
  70.6 3.1 %collective-permute-start.13 = (bf16[10,40,1152]{2,1,0:T(8,128)(2,1)S(1)}, bf16[10,40,1152]{2,1,0:T(8,128)(2,1)S(1)}, u32[]{:S(2)}, u32[]{:S(2)}) collective-permute-start(bf16[10,40,1152]{2,1,0:T(8,128)(2,1)S(1)} %constant_dynamic-update-slice_fusion.refs_5_), channel_id=1, source_target_pairs={{0,24},{8,0},{16,8},{24,16},{1,25},{9,1},{17,9},{25,17},{2,26},{10... | collective-permute-start | bytes 2764808 | tf_op jit(solution)/shard_map/ppermute | solution.py:168
  73.8 0.1 collective-permute-start.18
  73.9 0.0 collective-permute-done.17.refs_12_
  73.9 3.6 %collective-permute-start.19 = (bf16[5,40,1152]{2,1,0:T(8,128)(2,1)S(1)}, bf16[5,40,1152]{2,1,0:T(8,128)(2,1)S(1)}, u32[]{:S(2)}, u32[]{:S(2)}) collective-permute-start(bf16[5,40,1152]{2,1,0:T(8,128)(2,1)S(1)} %slice.120), channel_id=1, source_target_pairs={{0,224},{32,0},{64,32},{96,64},{128,96},{160,128},{192,160},{224,1... | collective-permute-start | bytes 1382408 | tf_op jit(solution)/shard_map/ppermute | solution.py:168
  77.5 0.1 pad_maximum_fusion.refs_0_
  77.6 3.3 %collective-permute-start.3 = (bf16[6,40,1152]{2,1,0:T(8,128)(2,1)S(1)}, bf16[6,40,1152]{2,1,0:T(8,128)(2,1)S(1)}, u32[]{:S(2)}, u32[]{:S(2)}) collective-permute-start(bf16[6,40,1152]{2,1,0:T(8,128)(2,1)S(1)} %pad_maximum_fusion.refs_0_), channel_id=1, source_target_pairs={{0,24},{8,0},{16,8},{24,16},{1,25},{9,1},{17,9},{25,17},{2,26},{10... | collective-permute-start | bytes 1658888 | tf_op jit(solution)/shard_map/ppermute | solution.py:168
  80.9 3.8 %collective-permute-done.18.refs_13_ = bf16[5,40,1152]{2,1,0:T(8,128)(2,1)S(1)} collective-permute-done((bf16[5,40,1152]{2,1,0:T(8,128)(2,1)S(1)}, bf16[5,40,1152]{2,1,0:T(8,128)(2,1)S(1)}, u32[]{:S(2)}, u32[]{:S(2)}) %collective-permute-start.18) | collective-permute-done | bytes 460832 | tf_op jit(solution)/shard_map/ppermute | solution.py:168
  84.7 0.0 collective-permute-start.2
  84.7 0.0 collective-permute-done.19.refs_14_
  84.7 1.6 collective-permute-start.20
  86.4 8.2 %collective-permute-done.13.refs_7_ = bf16[10,40,1152]{2,1,0:T(8,128)(2,1)S(1)} collective-permute-done((bf16[10,40,1152]{2,1,0:T(8,128)(2,1)S(1)}, bf16[10,40,1152]{2,1,0:T(8,128)(2,1)S(1)}, u32[]{:S(2)}, u32[]{:S(2)}) %collective-permute-start.13) | collective-permute-done | bytes 921632 | tf_op jit(solution)/shard_map/ppermute | solution.py:168
  94.6 3.5 %collective-permute-start.21 = (bf16[3,40,1152]{2,1,0:T(8,128)(2,1)S(1)}, bf16[3,40,1152]{2,1,0:T(8,128)(2,1)S(1)}, u32[]{:S(2)}, u32[]{:S(2)}) collective-permute-start(bf16[3,40,1152]{2,1,0:T(8,128)(2,1)S(1)} %slice.122), channel_id=1, source_target_pairs={{0,224},{32,0},{64,32},{96,64},{128,96},{160,128},{192,160},{224,1... | collective-permute-start | bytes 829448 | tf_op jit(solution)/shard_map/ppermute | solution.py:168
  98.1 0.2 collective-permute-done.12.refs_6_
  98.3 3.6 %collective-permute-start.15 = (bf16[5,40,1152]{2,1,0:T(8,128)(2,1)S(1)}, bf16[5,40,1152]{2,1,0:T(8,128)(2,1)S(1)}, u32[]{:S(2)}, u32[]{:S(2)}) collective-permute-start(bf16[5,40,1152]{2,1,0:T(8,128)(2,1)S(1)} %slice.118), channel_id=1, source_target_pairs={{0,24},{8,0},{16,8},{24,16},{1,25},{9,1},{17,9},{25,17},{2,26},{10... | collective-permute-start | bytes 1382408 | tf_op jit(solution)/shard_map/ppermute | solution.py:168
  101.9 4.5 %collective-permute-done.3.refs_2_ = bf16[6,40,1152]{2,1,0:T(8,128)(2,1)S(1)} collective-permute-done((bf16[6,40,1152]{2,1,0:T(8,128)(2,1)S(1)}, bf16[6,40,1152]{2,1,0:T(8,128)(2,1)S(1)}, u32[]{:S(2)}, u32[]{:S(2)}) %collective-permute-start.3) | collective-permute-done | bytes 552992 | tf_op jit(solution)/shard_map/ppermute | solution.py:168
  106.5 1.0 collective-permute-start.14
  107.5 1.0 collective-permute-done.2.refs_1_
  108.6 1.7 collective-permute-start.5
  110.3 0.0 collective-permute-done.20.refs_15_
  110.3 0.4 collective-permute-start.4
  110.7 0.1 collective-permute-start.22
  110.8 6.0 %collective-permute-done.22.refs_17_ = bf16[1,40,1152]{2,1,0:T(8,128)(2,1)S(1)} collective-permute-done((bf16[1,40,1152]{2,1,0:T(8,128)(2,1)S(1)}, bf16[1,40,1152]{2,1,0:T(8,128)(2,1)S(1)}, u32[]{:S(2)}, u32[]{:S(2)}) %collective-permute-start.22) | collective-permute-done | bytes 92192 | tf_op jit(solution)/shard_map/ppermute | solution.py:168
  116.8 2.0 %collective-permute-start.23 = (bf16[1,40,1152]{2,1,0:T(8,128)(2,1)S(1)}, bf16[1,40,1152]{2,1,0:T(8,128)(2,1)S(1)}, u32[]{:S(2)}, u32[]{:S(2)}) collective-permute-start(bf16[1,40,1152]{2,1,0:T(8,128)(2,1)S(1)} %slice.124), channel_id=1, source_target_pairs={{0,224},{32,0},{64,32},{96,64},{128,96},{160,128},{192,160},{224,1... | collective-permute-start | bytes 276488 | tf_op jit(solution)/shard_map/ppermute | solution.py:168
  118.8 2.5 %collective-permute-done.23.refs_18_ = bf16[1,40,1152]{2,1,0:T(8,128)(2,1)S(1)} collective-permute-done((bf16[1,40,1152]{2,1,0:T(8,128)(2,1)S(1)}, bf16[1,40,1152]{2,1,0:T(8,128)(2,1)S(1)}, u32[]{:S(2)}, u32[]{:S(2)}) %collective-permute-start.23) | collective-permute-done | bytes 92192 | tf_op jit(solution)/shard_map/ppermute | solution.py:168
  121.4 0.0 collective-permute-done.14.refs_8_
  121.4 0.7 copy-done.15
  122.1 0.1 copy-done.16
  122.3 0.1 copy-done.13
  122.4 0.6 copy-done.14
  123.0 8.3 %contract.1 = (f32[4,40,1280]{2,1,0:T(8,128)}, f32[4,40,1280]{2,1,0:T(8,128)}) custom-call(s32[6]{0:T(128)} %stack.27.sc_ref, bf16[6,40,1152]{2,1,0:T(8,128)(2,1)} %copy-done, bf16[6,40,1152]{2,1,0:T(8,128)(2,1)} %copy-done.7, bf16[6,40,1152]{2,1,0:T(8,128)(2,1)} %copy-done.6, bf16[3,40,1152]{2,1,0:T(8,128)(2,1)} %copy-done.16, ...), custom_call_target="tpu_custom_call" | custom-call | flops 1887436800 | bytes 10000000 | tf_op jit(solution)/shard_map/contract/pallas_call | solution.py:246
  131.3 0.0 collective-permute-start.24
  131.3 2.5 %collective-permute-done.24.b_ref = f32[4,40,1280]{2,1,0:T(8,128)S(1)} collective-permute-done((f32[4,40,1280]{2,1,0:T(8,128)}, f32[4,40,1280]{2,1,0:T(8,128)S(1)}, u32[]{:S(2)}, u32[]{:S(2)}) %collective-permute-start.24) | collective-permute-done | bytes 819232 | tf_op jit(solution)/shard_map/ppermute | solution.py:168
  133.8 0.9 copy-done.10
  134.7 4.2 %pair_sum.1 = f32[4,40,1280]{2,1,0:T(8,128)} custom-call(s32[6]{0:T(128)} %stack.27.sc_ref, f32[4,40,1280]{2,1,0:T(8,128)} %get-tuple-element.19.a_ref, f32[4,40,1280]{2,1,0:T(8,128)} %copy-done.10), custom_call_target="tpu_custom_call" | custom-call | tf_op jit(solution)/shard_map/pair_sum/pallas_call | solution.py:275
  138.9 16.6 %all_to_all.10.in_ref = f32[4,40,1280]{2,1,0:T(8,128)} all-to-all(f32[4,40,1280]{2,1,0:T(8,128)} %pair_sum.1), channel_id=1, replica_groups=mesh['z'=8,'y'=4,'x'=4,'core'=2] {'x'}, dimensions={0} | all-to-all | bytes 1638400 | tf_op jit(solution)/shard_map/all_to_all | solution.py:350
  155.5 2.1 %pack.1 = f32[32,16,128]{2,1,0:T(8,128)} custom-call(s32[6]{0:T(128)} %stack.27.sc_ref, f32[4,40,1280]{2,1,0:T(8,128)} %all_to_all.10.in_ref), custom_call_target="tpu_custom_call" | custom-call | tf_op jit(solution)/shard_map/pack/pallas_call | solution.py:305
  157.6 21.2 %all_to_all.11.in_ref = f32[32,16,128]{2,1,0:T(8,128)} all-to-all(f32[32,16,128]{2,1,0:T(8,128)} %pack.1), channel_id=1, replica_groups=mesh['z'=8,'y'=4,'x'=4,'core'=2] {'z','y'}, dimensions={0} | all-to-all | bytes 524288 | tf_op jit(solution)/shard_map/all_to_all | solution.py:351
  178.9 1.7 finish.1
  (65 shorter events, 0.5 us)
Async XLA Ops:
  0.0 30.6 %copy-start.20 = (s32[6,6]{1,0:T(8,128)S(1)}, s32[6,6]{1,0:T(8,128)}, u32[]{:S(2)}) copy-start(s32[6,6]{1,0:T(8,128)} %param.7) | copy-start | bytes 436
  6.5 20.6 %collective-permute-start = (bf16[7,40,1152]{2,1,0:T(8,128)(2,1)}, bf16[7,40,1152]{2,1,0:T(8,128)(2,1)S(1)}, u32[]{:S(2)}, u32[]{:S(2)}) collective-permute-start(bf16[7,40,1152]{2,1,0:T(8,128)(2,1)} %get-tuple-element.14), channel_id=1, source_target_pairs={{0,32},{32,64},{64,96},{96,128},{128,160},{160,192},{192,224},{224... | collective-permute-start | bytes 1935368 | tf_op jit(solution)/shard_map/ppermute | solution.py:168
  8.4 18.8 %collective-permute-start.1 = (bf16[7,40,1152]{2,1,0:T(8,128)(2,1)}, bf16[7,40,1152]{2,1,0:T(8,128)(2,1)S(1)}, u32[]{:S(2)}, u32[]{:S(2)}) collective-permute-start(bf16[7,40,1152]{2,1,0:T(8,128)(2,1)} %get-tuple-element.15), channel_id=1, source_target_pairs={{0,224},{32,0},{64,32},{96,64},{128,96},{160,128},{192,160},{224,1... | collective-permute-start | bytes 1935368 | tf_op jit(solution)/shard_map/ppermute | solution.py:168
  27.1 18.3 %collective-permute-start.6 = (bf16[5,40,1152]{2,1,0:T(8,128)(2,1)S(1)}, bf16[5,40,1152]{2,1,0:T(8,128)(2,1)}, u32[]{:S(2)}, u32[]{:S(2)}) collective-permute-start(bf16[5,40,1152]{2,1,0:T(8,128)(2,1)S(1)} %slice.107), channel_id=1, source_target_pairs={{0,32},{32,64},{64,96},{96,128},{128,160},{160,192},{192,224},{224... | collective-permute-start | bytes 1382408 | tf_op jit(solution)/shard_map/ppermute | solution.py:168
  27.3 19.3 %collective-permute-start.7 = (bf16[5,40,1152]{2,1,0:T(8,128)(2,1)S(1)}, bf16[5,40,1152]{2,1,0:T(8,128)(2,1)}, u32[]{:S(2)}, u32[]{:S(2)}) collective-permute-start(bf16[5,40,1152]{2,1,0:T(8,128)(2,1)S(1)} %slice.109), channel_id=1, source_target_pairs={{0,224},{32,0},{64,32},{96,64},{128,96},{160,128},{192,160},{224,1... | collective-permute-start | bytes 1382408 | tf_op jit(solution)/shard_map/ppermute | solution.py:168
  31.2 46.3 %copy-start.17 = (bf16[2,40,1152]{2,1,0:T(8,128)(2,1)S(1)}, bf16[2,40,1152]{2,1,0:T(8,128)(2,1)}, u32[]{:S(2)}) copy-start(bf16[2,40,1152]{2,1,0:T(8,128)(2,1)} %get-tuple-element.13) | copy-start | bytes 552964
  42.2 31.5 %collective-permute-start.16 = (bf16[7,40,1152]{2,1,0:T(8,128)(2,1)}, bf16[7,40,1152]{2,1,0:T(8,128)(2,1)S(1)}, u32[]{:S(2)}, u32[]{:S(2)}) collective-permute-start(bf16[7,40,1152]{2,1,0:T(8,128)(2,1)} %get-tuple-element.17), channel_id=1, source_target_pairs={{0,32},{32,64},{64,96},{96,128},{128,160},{160,192},{192,224},{224... | collective-permute-start | bytes 1935368 | tf_op jit(solution)/shard_map/ppermute | solution.py:168
  42.2 31.6 %collective-permute-start.17 = (bf16[7,40,1152]{2,1,0:T(8,128)(2,1)}, bf16[7,40,1152]{2,1,0:T(8,128)(2,1)S(1)}, u32[]{:S(2)}, u32[]{:S(2)}) collective-permute-start(bf16[7,40,1152]{2,1,0:T(8,128)(2,1)} %get-tuple-element.18), channel_id=1, source_target_pairs={{0,224},{32,0},{64,32},{96,64},{128,96},{160,128},{192,160},{224,1... | collective-permute-start | bytes 1935368 | tf_op jit(solution)/shard_map/ppermute | solution.py:168
  46.4 18.3 %collective-permute-start.8 = (bf16[3,40,1152]{2,1,0:T(8,128)(2,1)S(1)}, bf16[3,40,1152]{2,1,0:T(8,128)(2,1)S(1)}, u32[]{:S(2)}, u32[]{:S(2)}) collective-permute-start(bf16[3,40,1152]{2,1,0:T(8,128)(2,1)S(1)} %slice.111), channel_id=1, source_target_pairs={{0,32},{32,64},{64,96},{96,128},{128,160},{160,192},{192,224},{224... | collective-permute-start | bytes 829448 | tf_op jit(solution)/shard_map/ppermute | solution.py:168
  47.5 17.3 %collective-permute-start.9 = (bf16[3,40,1152]{2,1,0:T(8,128)(2,1)S(1)}, bf16[3,40,1152]{2,1,0:T(8,128)(2,1)S(1)}, u32[]{:S(2)}, u32[]{:S(2)}) collective-permute-start(bf16[3,40,1152]{2,1,0:T(8,128)(2,1)S(1)} %slice.113), channel_id=1, source_target_pairs={{0,224},{32,0},{64,32},{96,64},{128,96},{160,128},{192,160},{224,1... | collective-permute-start | bytes 829448 | tf_op jit(solution)/shard_map/ppermute | solution.py:168
  64.7 5.8 %collective-permute-start.10 = (bf16[1,40,1152]{2,1,0:T(8,128)(2,1)S(1)}, bf16[1,40,1152]{2,1,0:T(8,128)(2,1)S(1)}, u32[]{:S(2)}, u32[]{:S(2)}) collective-permute-start(bf16[1,40,1152]{2,1,0:T(8,128)(2,1)S(1)} %slice.115), channel_id=1, source_target_pairs={{0,32},{32,64},{64,96},{96,128},{128,160},{160,192},{192,224},{224... | collective-permute-start | bytes 276488 | tf_op jit(solution)/shard_map/ppermute | solution.py:168
  64.8 5.7 %collective-permute-start.11 = (bf16[1,40,1152]{2,1,0:T(8,128)(2,1)S(1)}, bf16[1,40,1152]{2,1,0:T(8,128)(2,1)S(1)}, u32[]{:S(2)}, u32[]{:S(2)}) collective-permute-start(bf16[1,40,1152]{2,1,0:T(8,128)(2,1)S(1)} %slice.116), channel_id=1, source_target_pairs={{0,224},{32,0},{64,32},{96,64},{128,96},{160,128},{192,160},{224,1... | collective-permute-start | bytes 276488 | tf_op jit(solution)/shard_map/ppermute | solution.py:168
  70.6 51.6 %copy-start.5 = (bf16[10,40,1152]{2,1,0:T(8,128)(2,1)}, bf16[10,40,1152]{2,1,0:T(8,128)(2,1)S(1)}, u32[]{:S(2)}) copy-start(bf16[10,40,1152]{2,1,0:T(8,128)(2,1)S(1)} %constant_dynamic-update-slice_fusion.refs_5_) | copy-start | bytes 2764804
  70.6 24.0 %collective-permute-start.13 = (bf16[10,40,1152]{2,1,0:T(8,128)(2,1)S(1)}, bf16[10,40,1152]{2,1,0:T(8,128)(2,1)S(1)}, u32[]{:S(2)}, u32[]{:S(2)}) collective-permute-start(bf16[10,40,1152]{2,1,0:T(8,128)(2,1)S(1)} %constant_dynamic-update-slice_fusion.refs_5_), channel_id=1, source_target_pairs={{0,24},{8,0},{16,8},{24,16},{1,25},{9,1},{17,9},{25,17},{2,26},{10... | collective-permute-start | bytes 2764808 | tf_op jit(solution)/shard_map/ppermute | solution.py:168
  73.7 24.6 %collective-permute-start.12 = (bf16[10,40,1152]{2,1,0:T(8,128)(2,1)S(1)}, bf16[10,40,1152]{2,1,0:T(8,128)(2,1)S(1)}, u32[]{:S(2)}, u32[]{:S(2)}) collective-permute-start(bf16[10,40,1152]{2,1,0:T(8,128)(2,1)S(1)} %constant_dynamic-update-slice_fusion.refs_5_), channel_id=1, source_target_pairs={{0,8},{8,16},{16,24},{24,0},{1,9},{9,17},{17,25},{25,1},{2,10},{10... | collective-permute-start | bytes 2764808 | tf_op jit(solution)/shard_map/ppermute | solution.py:168
  73.7 48.5 %copy-start.3 = (bf16[7,40,1152]{2,1,0:T(8,128)(2,1)}, bf16[7,40,1152]{2,1,0:T(8,128)(2,1)S(1)}, u32[]{:S(2)}) copy-start(bf16[7,40,1152]{2,1,0:T(8,128)(2,1)S(1)} %collective-permute-done.16.refs_11_) | copy-start | bytes 1935364
  73.8 10.9 %collective-permute-start.18 = (bf16[5,40,1152]{2,1,0:T(8,128)(2,1)S(1)}, bf16[5,40,1152]{2,1,0:T(8,128)(2,1)S(1)}, u32[]{:S(2)}, u32[]{:S(2)}) collective-permute-start(bf16[5,40,1152]{2,1,0:T(8,128)(2,1)S(1)} %slice.119), channel_id=1, source_target_pairs={{0,32},{32,64},{64,96},{96,128},{128,160},{160,192},{192,224},{224... | collective-permute-start | bytes 1382408 | tf_op jit(solution)/shard_map/ppermute | solution.py:168
  73.9 48.3 %copy-start.4 = (bf16[7,40,1152]{2,1,0:T(8,128)(2,1)}, bf16[7,40,1152]{2,1,0:T(8,128)(2,1)S(1)}, u32[]{:S(2)}) copy-start(bf16[7,40,1152]{2,1,0:T(8,128)(2,1)S(1)} %collective-permute-done.17.refs_12_) | copy-start | bytes 1935364
  73.9 10.8 %collective-permute-start.19 = (bf16[5,40,1152]{2,1,0:T(8,128)(2,1)S(1)}, bf16[5,40,1152]{2,1,0:T(8,128)(2,1)S(1)}, u32[]{:S(2)}, u32[]{:S(2)}) collective-permute-start(bf16[5,40,1152]{2,1,0:T(8,128)(2,1)S(1)} %slice.120), channel_id=1, source_target_pairs={{0,224},{32,0},{64,32},{96,64},{128,96},{160,128},{192,160},{224,1... | collective-permute-start | bytes 1382408 | tf_op jit(solution)/shard_map/ppermute | solution.py:168
  77.6 44.6 %copy-start = (bf16[6,40,1152]{2,1,0:T(8,128)(2,1)}, bf16[6,40,1152]{2,1,0:T(8,128)(2,1)S(1)}, u32[]{:S(2)}) copy-start(bf16[6,40,1152]{2,1,0:T(8,128)(2,1)S(1)} %pad_maximum_fusion.refs_0_) | copy-start | bytes 1658884
  77.6 28.8 %collective-permute-start.3 = (bf16[6,40,1152]{2,1,0:T(8,128)(2,1)S(1)}, bf16[6,40,1152]{2,1,0:T(8,128)(2,1)S(1)}, u32[]{:S(2)}, u32[]{:S(2)}) collective-permute-start(bf16[6,40,1152]{2,1,0:T(8,128)(2,1)S(1)} %pad_maximum_fusion.refs_0_), channel_id=1, source_target_pairs={{0,24},{8,0},{16,8},{24,16},{1,25},{9,1},{17,9},{25,17},{2,26},{10... | collective-permute-start | bytes 1658888 | tf_op jit(solution)/shard_map/ppermute | solution.py:168
  84.7 37.5 %copy-start.8 = (bf16[5,40,1152]{2,1,0:T(8,128)(2,1)}, bf16[5,40,1152]{2,1,0:T(8,128)(2,1)S(1)}, u32[]{:S(2)}) copy-start(bf16[5,40,1152]{2,1,0:T(8,128)(2,1)S(1)} %collective-permute-done.18.refs_13_) | copy-start | bytes 1382404
  84.7 23.9 %collective-permute-start.2 = (bf16[6,40,1152]{2,1,0:T(8,128)(2,1)S(1)}, bf16[6,40,1152]{2,1,0:T(8,128)(2,1)S(1)}, u32[]{:S(2)}, u32[]{:S(2)}) collective-permute-start(bf16[6,40,1152]{2,1,0:T(8,128)(2,1)S(1)} %pad_maximum_fusion.refs_0_), channel_id=1, source_target_pairs={{0,8},{8,16},{16,24},{24,0},{1,9},{9,17},{17,25},{25,1},{2,10},{10... | collective-permute-start | bytes 1658888 | tf_op jit(solution)/shard_map/ppermute | solution.py:168
  84.7 37.5 %copy-start.9 = (bf16[5,40,1152]{2,1,0:T(8,128)(2,1)}, bf16[5,40,1152]{2,1,0:T(8,128)(2,1)S(1)}, u32[]{:S(2)}) copy-start(bf16[5,40,1152]{2,1,0:T(8,128)(2,1)S(1)} %collective-permute-done.19.refs_14_) | copy-start | bytes 1382404
  84.7 25.6 %collective-permute-start.20 = (bf16[3,40,1152]{2,1,0:T(8,128)(2,1)S(1)}, bf16[3,40,1152]{2,1,0:T(8,128)(2,1)S(1)}, u32[]{:S(2)}, u32[]{:S(2)}) collective-permute-start(bf16[3,40,1152]{2,1,0:T(8,128)(2,1)S(1)} %slice.121), channel_id=1, source_target_pairs={{0,32},{32,64},{64,96},{96,128},{128,160},{160,192},{192,224},{224... | collective-permute-start | bytes 829448 | tf_op jit(solution)/shard_map/ppermute | solution.py:168
  94.6 27.6 %copy-start.1 = (bf16[10,40,1152]{2,1,0:T(8,128)(2,1)}, bf16[10,40,1152]{2,1,0:T(8,128)(2,1)S(1)}, u32[]{:S(2)}) copy-start(bf16[10,40,1152]{2,1,0:T(8,128)(2,1)S(1)} %collective-permute-done.13.refs_7_) | copy-start | bytes 2764804
  94.6 16.1 %collective-permute-start.21 = (bf16[3,40,1152]{2,1,0:T(8,128)(2,1)S(1)}, bf16[3,40,1152]{2,1,0:T(8,128)(2,1)S(1)}, u32[]{:S(2)}, u32[]{:S(2)}) collective-permute-start(bf16[3,40,1152]{2,1,0:T(8,128)(2,1)S(1)} %slice.122), channel_id=1, source_target_pairs={{0,224},{32,0},{64,32},{96,64},{128,96},{160,128},{192,160},{224,1... | collective-permute-start | bytes 829448 | tf_op jit(solution)/shard_map/ppermute | solution.py:168
  98.3 24.0 %copy-start.2 = (bf16[10,40,1152]{2,1,0:T(8,128)(2,1)}, bf16[10,40,1152]{2,1,0:T(8,128)(2,1)S(1)}, u32[]{:S(2)}) copy-start(bf16[10,40,1152]{2,1,0:T(8,128)(2,1)S(1)} %collective-permute-done.12.refs_6_) | copy-start | bytes 2764804
  98.3 23.1 %collective-permute-start.15 = (bf16[5,40,1152]{2,1,0:T(8,128)(2,1)S(1)}, bf16[5,40,1152]{2,1,0:T(8,128)(2,1)S(1)}, u32[]{:S(2)}, u32[]{:S(2)}) collective-permute-start(bf16[5,40,1152]{2,1,0:T(8,128)(2,1)S(1)} %slice.118), channel_id=1, source_target_pairs={{0,24},{8,0},{16,8},{24,16},{1,25},{9,1},{17,9},{25,17},{2,26},{10... | collective-permute-start | bytes 1382408 | tf_op jit(solution)/shard_map/ppermute | solution.py:168
  106.4 15.8 %copy-start.6 = (bf16[6,40,1152]{2,1,0:T(8,128)(2,1)}, bf16[6,40,1152]{2,1,0:T(8,128)(2,1)S(1)}, u32[]{:S(2)}) copy-start(bf16[6,40,1152]{2,1,0:T(8,128)(2,1)S(1)} %collective-permute-done.3.refs_2_) | copy-start | bytes 1658884
  106.5 15.0 %collective-permute-start.14 = (bf16[5,40,1152]{2,1,0:T(8,128)(2,1)S(1)}, bf16[5,40,1152]{2,1,0:T(8,128)(2,1)S(1)}, u32[]{:S(2)}, u32[]{:S(2)}) collective-permute-start(bf16[5,40,1152]{2,1,0:T(8,128)(2,1)S(1)} %slice.117), channel_id=1, source_target_pairs={{0,8},{8,16},{16,24},{24,0},{1,9},{9,17},{17,25},{25,1},{2,10},{10... | collective-permute-start | bytes 1382408 | tf_op jit(solution)/shard_map/ppermute | solution.py:168
  108.6 13.7 %copy-start.7 = (bf16[6,40,1152]{2,1,0:T(8,128)(2,1)}, bf16[6,40,1152]{2,1,0:T(8,128)(2,1)S(1)}, u32[]{:S(2)}) copy-start(bf16[6,40,1152]{2,1,0:T(8,128)(2,1)S(1)} %collective-permute-done.2.refs_1_) | copy-start | bytes 1658884
  108.6 12.8 %collective-permute-start.5 = (bf16[3,40,1152]{2,1,0:T(8,128)(2,1)S(1)}, bf16[3,40,1152]{2,1,0:T(8,128)(2,1)S(1)}, u32[]{:S(2)}, u32[]{:S(2)}) collective-permute-start(bf16[3,40,1152]{2,1,0:T(8,128)(2,1)S(1)} %slice.106), channel_id=1, source_target_pairs={{0,24},{8,0},{16,8},{24,16},{1,25},{9,1},{17,9},{25,17},{2,26},{10... | collective-permute-start | bytes 829448 | tf_op jit(solution)/shard_map/ppermute | solution.py:168
  110.3 12.0 %copy-start.11 = (bf16[3,40,1152]{2,1,0:T(8,128)(2,1)}, bf16[3,40,1152]{2,1,0:T(8,128)(2,1)S(1)}, u32[]{:S(2)}) copy-start(bf16[3,40,1152]{2,1,0:T(8,128)(2,1)S(1)} %collective-permute-done.20.refs_15_) | copy-start | bytes 829444
  110.3 11.1 %collective-permute-start.4 = (bf16[3,40,1152]{2,1,0:T(8,128)(2,1)S(1)}, bf16[3,40,1152]{2,1,0:T(8,128)(2,1)S(1)}, u32[]{:S(2)}, u32[]{:S(2)}) collective-permute-start(bf16[3,40,1152]{2,1,0:T(8,128)(2,1)S(1)} %slice.105), channel_id=1, source_target_pairs={{0,8},{8,16},{16,24},{24,0},{1,9},{9,17},{17,25},{25,1},{2,10},{10... | collective-permute-start | bytes 829448 | tf_op jit(solution)/shard_map/ppermute | solution.py:168
  110.7 11.6 %copy-start.12 = (bf16[3,40,1152]{2,1,0:T(8,128)(2,1)}, bf16[3,40,1152]{2,1,0:T(8,128)(2,1)S(1)}, u32[]{:S(2)}) copy-start(bf16[3,40,1152]{2,1,0:T(8,128)(2,1)S(1)} %collective-permute-done.21.refs_16_) | copy-start | bytes 829444
  110.7 6.1 %collective-permute-start.22 = (bf16[1,40,1152]{2,1,0:T(8,128)(2,1)S(1)}, bf16[1,40,1152]{2,1,0:T(8,128)(2,1)S(1)}, u32[]{:S(2)}, u32[]{:S(2)}) collective-permute-start(bf16[1,40,1152]{2,1,0:T(8,128)(2,1)S(1)} %slice.123), channel_id=1, source_target_pairs={{0,32},{32,64},{64,96},{96,128},{128,160},{160,192},{192,224},{224... | collective-permute-start | bytes 276488 | tf_op jit(solution)/shard_map/ppermute | solution.py:168
  116.8 5.5 %copy-start.18 = (bf16[1,40,1152]{2,1,0:T(8,128)(2,1)}, bf16[1,40,1152]{2,1,0:T(8,128)(2,1)S(1)}, u32[]{:S(2)}) copy-start(bf16[1,40,1152]{2,1,0:T(8,128)(2,1)S(1)} %collective-permute-done.22.refs_17_) | copy-start | bytes 276484
  116.8 4.6 %collective-permute-start.23 = (bf16[1,40,1152]{2,1,0:T(8,128)(2,1)S(1)}, bf16[1,40,1152]{2,1,0:T(8,128)(2,1)S(1)}, u32[]{:S(2)}, u32[]{:S(2)}) collective-permute-start(bf16[1,40,1152]{2,1,0:T(8,128)(2,1)S(1)} %slice.124), channel_id=1, source_target_pairs={{0,224},{32,0},{64,32},{96,64},{128,96},{160,128},{192,160},{224,1... | collective-permute-start | bytes 276488 | tf_op jit(solution)/shard_map/ppermute | solution.py:168
  121.4 0.9 copy-start.19
  121.4 0.8 copy-start.15
  121.4 0.8 copy-start.16
  121.4 1.0 copy-start.13
  122.2 0.8 copy-start.14
  131.3 2.5 %collective-permute-start.24 = (f32[4,40,1280]{2,1,0:T(8,128)}, f32[4,40,1280]{2,1,0:T(8,128)S(1)}, u32[]{:S(2)}, u32[]{:S(2)}) collective-permute-start(f32[4,40,1280]{2,1,0:T(8,128)} %get-tuple-element.20), channel_id=1, source_target_pairs={{0,1},{1,0},{2,3},{3,2},{4,5},{5,4},{6,7},{7,6},{8,9},{9,8},{10,11... | collective-permute-start | bytes 2457608 | tf_op jit(solution)/shard_map/ppermute | solution.py:168
  133.8 0.9 copy-start.10

commit v2 on v0

v2 whole, which is shorter than its diff:
```python
import functools

import jax
import jax.numpy as jnp
from jax import lax
from jax.experimental import pallas as pl
from jax.experimental.pallas import tpu as pltpu
from jax.sharding import Mesh, PartitionSpec as P

BLOCK = 64
ABLOCK = 64
NZ, NY, NX, NC = 8, 4, 4, 2
NR = NX * NC
LA = 40
NAO = 384
LANES = 128
ROWS = NAO // NR
SUB = ROWS // NZ
FULL = SUB * NAO
HALF = FULL // 2
NB = NAO // BLOCK
F32 = jnp.float32
BF16 = jnp.bfloat16
MIB = 1024 * 1024


def places():
    z, y, x, c = (lax.axis_index(a) for a in ("z", "y", "x", "core"))
    return z, y, x * NC + c


def row_mask(read):
    lane = lax.broadcasted_iota(jnp.int32, (1, NAO), 1) // BLOCK
    out = jnp.zeros((1, NAO), F32)
    for n in range(NB):
        out = jnp.where(lane == n, read(n).astype(F32), out)
    return out


def emit(z, held, own_ref, plus_ref, minus_ref):
    for d in range(NZ):
        dest = lax.rem(z + d, NZ)
        for j in range(SUB):
            h = j // 3
            if d == 0:
                out_ref, place = own_ref, h
            elif d < 4:
                out_ref, place = plus_ref, 2 * (d - 1) + h
            elif d > 4:
                out_ref, place = minus_ref, 2 * (7 - d) + h
            else:
                out_ref, place = (plus_ref, minus_ref)[h], 6
            for t in range(NAO // LANES):
                rows = held[t, pl.ds(dest * SUB + j, LA, stride=ROWS), :]
                out_ref[place, :, pl.ds((j % 3) * NAO + LANES * t, LANES)] = rows.astype(BF16)


CHUNKS = tuple(jax.ShapeDtypeStruct((n, LA, HALF), BF16) for n in (2, 7, 7))


def prep_kernel(pat_ref, basis_ref, own_ref, plus_ref, minus_ref, slab, held, sems):
    z, y, r = places()
    place = z * NY + y
    steps = LA // 8
    start = pl.multiple_of(r * ROWS, 16)
    copies = [
        pltpu.make_async_copy(
            basis_ref.at[pl.ds(8 * o, 8), pl.ds(start, ROWS), :], slab.at[pl.ds(8 * o, 8)], sems.at[o]
        )
        for o in range(steps)
    ]
    for copy in copies:
        copy.start()
    for o in range(steps):
        b = (place * LA + 8 * o) // ABLOCK
        masks = [
            row_mask(lambda n: pat_ref[(r * ROWS + 8 * jo) // BLOCK, n, b]) for jo in range(ROWS // 8)
        ]
        copies[o].wait()
        for jo in range(ROWS // 8):
            for p in range(8 * o, 8 * o + 8):
                rows = slab[p, pl.ds(8 * jo, 8), :].astype(F32) * masks[jo]
                for t in range(NAO // LANES):
                    held[t, pl.ds(p * ROWS + 8 * jo, 8), :] = rows[:, LANES * t : LANES * (t + 1)]
    emit(z, held, own_ref, plus_ref, minus_ref)


SMEM = pl.BlockSpec(memory_space=pltpu.SMEM)
VMEM = pl.BlockSpec(memory_space=pltpu.VMEM)
HBM = pl.BlockSpec(memory_space=pltpu.HBM)
ANY = pl.BlockSpec(memory_space=pl.ANY)


def prep(pat, basis):
    return pl.pallas_call(
        prep_kernel,
        out_shape=CHUNKS,
        in_specs=[SMEM, HBM],
        out_specs=(VMEM, VMEM, VMEM),
        scratch_shapes=[
            pltpu.VMEM((LA, ROWS, NAO), BF16),
            pltpu.VMEM((NAO // LANES, LA * ROWS, LANES), F32),
            pltpu.SemaphoreType.DMA((LA // 8,)),
        ],
        compiler_params=pltpu.CompilerParams(vmem_limit_bytes=56 * MIB),
        cost_estimate=pl.CostEstimate(flops=10**6, bytes_accessed=3 * 10**6, transcendentals=0),
        name="prep",
    )(pat, basis)


STEPQ = 8


def product_kernel(
    pat_ref, gpat_ref, basis_ref, occ_ref, vir_ref, own_ref, plus_ref, minus_ref, first, held, occ, vir, masks
):
    i = pl.program_id(0)
    z, y, r = places()
    place = z * NY + y
    b0 = (place * LA) // ABLOCK
    nblocks = pat_ref.shape[2]

    @pl.when(i == 0)
    def _():
        for mb in range(NB):
            rows = pl.ds(mb * BLOCK, BLOCK)
            g = row_mask(lambda n: gpat_ref[mb, n]).astype(BF16)
            vir[rows, :] = vir_ref[rows, :] * g
            for k in range(2):
                b = jnp.minimum(b0 + k, nblocks - 1)
                m = row_mask(lambda n: pat_ref[mb, n, b])
                masks[k, rows, :] = jnp.broadcast_to(m, (BLOCK, NAO)).astype(BF16)
        for jo in range(ROWS // 16):
            start = pl.multiple_of(r * ROWS + 16 * jo, 16)
            g = row_mask(lambda n: gpat_ref[start // BLOCK, n]).astype(BF16)
            occ[pl.ds(16 * jo, 16), :] = occ_ref[pl.ds(start, 16), :] * g

    which = (place * LA + STEPQ * i) // ABLOCK - b0
    mask = masks[which]
    rows_r = occ[...]
    for q in range(STEPQ):
        masked = basis_ref[q] * mask
        f = jnp.dot(rows_r, masked, preferred_element_type=F32).astype(BF16)
        first[pl.ds(pl.multiple_of((STEPQ * i + q) * ROWS, 16), ROWS), :] = f

    @pl.when(i == LA // STEPQ - 1)
    def _():
        v = vir[...]
        n = LA * ROWS // 4
        for t in range(4):
            part = jnp.dot(first[pl.ds(t * n, n), :], v, preferred_element_type=F32)
            for u in range(NAO // LANES):
                held[u, pl.ds(t * n, n), :] = part[:, LANES * u : LANES * (u + 1)]
        emit(z, held, own_ref, plus_ref, minus_ref)


def products(pat, gpat, basis, occ, vir):
    return pl.pallas_call(
        product_kernel,
        out_shape=CHUNKS,
        grid=(LA // STEPQ,),
        in_specs=[
            SMEM,
            SMEM,
            pl.BlockSpec((STEPQ, NAO, NAO), lambda i: (i, 0, 0)),
            pl.BlockSpec((NAO, NAO), lambda i: (0, 0)),
            pl.BlockSpec((NAO, NAO), lambda i: (0, 0)),
        ],
        out_specs=tuple(pl.BlockSpec(c.shape, lambda i: (0, 0, 0)) for c in CHUNKS),
        scratch_shapes=[
            pltpu.VMEM((LA * ROWS, NAO), BF16),
            pltpu.VMEM((NAO // LANES, LA * ROWS, LANES), F32),
            pltpu.VMEM((ROWS, NAO), BF16),
            pltpu.VMEM((NAO, NAO), BF16),
            pltpu.VMEM((2, NAO, NAO), BF16),
        ],
        compiler_params=pltpu.CompilerParams(vmem_limit_bytes=56 * MIB),
        cost_estimate=pl.CostEstimate(
            flops=4 * LA * ROWS * NAO * NAO, bytes_accessed=14 * 10**6, transcendentals=0
        ),
        name="products",
    )(pat, gpat, basis, occ, vir)


def shift(value, by, axis, n):
    return lax.ppermute(value, axis, [(i, (i + by) % n) for i in range(n)])


def after(value, *others):
    return lax.optimization_barrier((value,) + others)[0]


GROUPS = ((0, 1, 7), (2, 6), (3, 5, 4))
EORDER = (0, 1, 3, 2)


def both(plus, minus, hops=1):
    return shift(plus, hops, "z", NZ), shift(minus, -hops, "z", NZ)


def round_y(group):
    return shift(group, 1, "y", NY), shift(group, -1, "y", NY)


def far_y(below, above):
    n = below.shape[0] // 2
    return shift(below[:n], 1, "y", NY), shift(above[n:], -1, "y", NY)


tie = lax.optimization_barrier


def spread(chunks, products_of):
    own, plus, minus = chunks
    p1, m1 = both(plus, minus)
    pown, pplus, pminus = products_of()
    n1 = jnp.concatenate([own, p1[:2], m1[:2]], axis=0)
    p1r, m1r, n1, pplus, pminus = tie((p1[2:], m1[2:], n1, pplus, pminus))
    p2, m2 = both(p1r, m1r)
    b1, a1 = round_y(n1)
    b1, a1, pplus, pminus = tie((b1, a1, pplus, pminus))
    p3, m3 = both(p2[2:4], m2[2:4])
    p4, m4 = both(p2[4:], m2[4:], 2)
    n2 = jnp.concatenate([p2[:2], m2[:2]], axis=0)
    b2, a2 = round_y(n2)
    f1 = far_y(b1, a1)
    q1, r1 = both(pplus, pminus)
    n3 = jnp.concatenate([p3, m3, p4, m4], axis=0)
    b3, a3 = round_y(n3)
    f2 = far_y(b2, a2)
    q2, r2 = both(q1[2:], r1[2:])
    b3, a3, q2, r2 = tie((b3, a3, q2, r2))
    f3 = far_y(b3, a3)
    q3, r3 = both(q2[2:4], r2[2:4])
    q4, r4 = both(q2[4:], r2[4:], 2)
    m = [n1, b1, a1, *f1, n2, b2, a2, *f2, n3, b3, a3, *f3]
    return m, [pown, q1, q2, q3, q4, r4, r3, r2, r1]


ORDER = [(d, e) for group in GROUPS for e in EORDER for d in group]


TILE = 256


def contract_kernel(np_, *refs):
    products_, arrays, (out_ref, left, right) = refs[:np_], refs[np_:-3], refs[-3:]
    z = lax.axis_index("z")
    at = 0
    for a in products_:
        for i in range(min(a.shape[0], 2)):
            left[at % 2, pl.ds(at // 2 * LA, LA), :] = a[i]
            at += 1
    at = 0
    for a in arrays:
        for i in range(a.shape[0]):
            right[at % 2, pl.ds(at // 2 * LA, LA), :] = a[i]
            at += 1
    for t in range(NZ * NY * LA // TILE):
        cols = pl.ds(t * TILE, TILE)
        acc = jnp.zeros((NZ * LA, TILE), F32)
        for h in range(2):
            acc += lax.dot_general(
                left[h], right[h, cols, :], (((1,), (1,)), ((), ())), preferred_element_type=F32
            )
        part = acc.reshape(NZ, LA, TILE).astype(BF16)
        for d in range(NZ):
            out_ref[lax.rem(z - d + NZ, NZ), :, cols] = part[d]


def contract(m, p):
    return pl.pallas_call(
        functools.partial(contract_kernel, len(p)),
        out_shape=jax.ShapeDtypeStruct((NZ, LA, NZ * NY * LA), BF16),
        in_specs=[VMEM] * (len(p) + len(m)),
        out_specs=VMEM,
        scratch_shapes=[
            pltpu.VMEM((2, NZ * LA, HALF), BF16),
            pltpu.VMEM((2, NZ * NY * LA, HALF), BF16),
        ],
        compiler_params=pltpu.CompilerParams(vmem_limit_bytes=24 * MIB),
        cost_estimate=pl.CostEstimate(
            flops=4 * 320 * 1280 * 1152, bytes_accessed=10**7, transcendentals=0
        ),
        name="contract",
    )(*p, *m)


def pack_kernel(in_ref, out_ref):
    z, y, _ = places()
    total = in_ref[0].astype(F32)
    for k in range(1, NR):
        total += in_ref[k].astype(F32)
    for k, (d, e) in enumerate(ORDER):
        part = total[:, k * LA : (k + 1) * LA]
        oct8 = [part[8 * o : 8 * o + 8] for o in range(5)]
        upper = jnp.concatenate([oct8[0], oct8[1], oct8[2], jnp.zeros((8, 8), F32)], axis=1)
        lower = jnp.concatenate([oct8[3], oct8[4], jnp.zeros((8, 48), F32)], axis=1)
        dest = lax.rem(z - d + NZ, NZ) * NY + lax.rem(y - e + NY, NY)
        out_ref[dest, 0:8, :] = upper
        out_ref[dest, 8:16, :] = lower


def pack(value):
    return pl.pallas_call(
        pack_kernel,
        out_shape=jax.ShapeDtypeStruct((NZ * NY, 16, LANES), F32),
        in_specs=[VMEM],
        out_specs=VMEM,
        name="pack",
    )(value)


def finish_kernel(in_ref, out_ref):
    parts = []
    for y in range(NY):
        total = in_ref[y]
        for z in range(1, NZ):
            total = total + in_ref[z * NY + y]
        for o in range(5):
            lo = (o % 3) * LA
            parts.append(total[8 * (o // 3) : 8 * (o // 3) + 8, lo : lo + LA])
    rows = jnp.concatenate(parts, axis=0)
    rows = jnp.concatenate([rows, jnp.zeros((NY * LA, LANES - LA), F32)], axis=1)
    rows = jnp.concatenate([rows, jnp.zeros((256 - NY * LA, LANES), F32)], axis=0)
    out_ref[...] = rows.T[:LA, : NY * LA] * (1.0 / NAO)


def finish(value):
    return pl.pallas_call(
        finish_kernel,
        out_shape=jax.ShapeDtypeStruct((LA, NY * LA), F32),
        in_specs=[VMEM],
        out_specs=VMEM,
        name="finish",
    )(value)


def local(basis, aux_pattern, green_pattern, green_occ, green_vir):
    pat = jnp.transpose(aux_pattern, (1, 2, 0))
    m, p = spread(
        prep(pat, basis), lambda: products(pat, green_pattern, basis, green_occ, green_vir)
    )
    parts = contract(m, p)
    by_rep = lax.all_to_all(parts, ("x", "core"), split_axis=0, concat_axis=0, tiled=True)
    by_zy = lax.all_to_all(pack(by_rep), ("z", "y"), split_axis=0, concat_axis=0, tiled=True)
    return finish(by_zy)


def solution(mesh):
    fine = Mesh(mesh.devices.reshape(NZ, NY, NX, NC), ("z", "y", "x", "core"))
    return jax.shard_map(
        local,
        mesh=fine,
        in_specs=(P(("z", "y"), None, None), P(), P(), P(), P()),
        out_specs=P(("z", "y"), ("x", "core")),
        check_vma=False,
    )
```

time: 1460 us -> 143 us (0.10)
  waiting for transfers between devices: 1310 us -> 42 us
  local copies, waits for them, and re-layouts: 97.1 us -> 0.49 us
  blocking collectives: 0 us -> 35 us
  starting transfers between devices: 17.4 us -> 43.7 us
  Pallas kernels: 0 us -> 20.8 us
    reduce_scatter x1 -> x0, waiting for transfers between devices: 1280 us -> none  [local(): lax.psum_scatter(tiles, ('aux', 'rep'), scatter_dimension=0, tiled=True)]
    ppermute x0 -> x28, starting transfers between devices: none -> 43.7 us  [shift(): return lax.ppermute(value, axis, [(i, (i + by) % n) for i in range(n)])]
    ppermute x0 -> x28, waiting for transfers between devices: none -> 42 us  [shift(): return lax.ppermute(value, axis, [(i, (i + by) % n) for i in range(n)])]
    all_to_all x0 -> x2, blocking collectives: none -> 35 us  [the longest x1 18.1 us: local(): lax.all_to_all(pack(by_rep), ('z', 'y'), split_axis=0, concat_axis=0, til...]
    unnamed x10 -> x7, local copies, waits for them, and re-layouts: 30.8 us -> 0.06 us
    all_to_all x2 -> x0, waiting for transfers between devices: 30.6 us -> none  [the longest x1 16.9 us: local(): lax.all_to_all(basis_rows, 'aux', split_axis=2, concat_axis=0, tiled=True)]
    reshape x3 -> x0, local copies, waits for them, and re-layouts: 25.9 us -> none  [the longest x1 10.9 us: local(): tiles = partial_value.reshape(aux_count, local_aux, rep_count, column_count)]
    pallas_call x0 -> x5, Pallas kernels: none -> 20.8 us  [the longest x1 10.1 us: products(): pl.pallas_call(product_kernel, out_shape=CHUNKS, grid=(LA // STEPQ,), in_...]
  transfers between devices with their start and end apart: 3 -> 28, of which waited for: 3 -> 10; matrix products, arithmetic and copies ran while one was open for 3% -> 0% of each run, Pallas kernels for 0% -> 7%
where the time goes in v2:
time: 143 us; the launch traced here: 142 us
  starting transfers between devices  43.7 us (31%)
  waiting for transfers between devices  42 us (29%)
  blocking collectives  35 us (24%)
  Pallas kernels  20.8 us (15%)
    ppermute x28, starting transfers between devices, shift(): return lax.ppermute(value, axis, [(i, (i + by) % n) for i in range(n)])  43.7 us
    ppermute x28, waiting for transfers between devices, shift(): return lax.ppermute(value, axis, [(i, (i + by) % n) for i in range(n)])  42 us
    all_to_all x1, blocking collectives, local(): lax.all_to_all(pack(by_rep), ('z', 'y'), split_axis=0, concat_axis=0, til...  18.1 us
    all_to_all x1, blocking collectives, local(): lax.all_to_all(parts, ('x', 'core'), split_axis=0, concat_axis=0, tiled=T...  16.9 us
    pallas_call x1, Pallas kernels, products(): pl.pallas_call(product_kernel, out_shape=CHUNKS, grid=(LA // STEPQ,), in_...  10.1 us
    pallas_call x1, Pallas kernels, prep(): pl.pallas_call(prep_kernel, out_shape=CHUNKS, in_specs=[SMEM, HBM], out_s...  4.41 us
  transfers between devices with their start and end apart: 28, of which 10 were waited for; matrix products, arithmetic and copies ran while one was open for 0% of the time, Pallas kernels for 7%

profile of v2, /device:TPU:2, one launch (start us, length us, event | category | flops | bytes accessed | tf_op | source)
XLA Modules:
  0.0 142.4 jit_solution(8535865410983528507)
XLA Ops:
  0.0 4.4 %prep.1 = (bf16[2,40,1152]{2,1,0:T(8,128)(2,1)}, bf16[7,40,1152]{2,1,0:T(8,128)(2,1)}, bf16[7,40,1152]{2,1,0:T(8,128)(2,1)}) custom-call(s32[6,6,20]{2,1,0:T(8,128)} %bitcast.1, bf16[40,384,384]{2,1,0:T(8,128)(2,1)} %basis_ref.3), custom_call_target="tpu_custom_call" | custom-call | flops 1000000 | bytes 3000000 | tf_op jit(solution)/shard_map/prep/pallas_call | solution.py:95
  4.4 2.0 %collective-permute-start = (bf16[7,40,1152]{2,1,0:T(8,128)(2,1)}, bf16[7,40,1152]{2,1,0:T(8,128)(2,1)S(1)}, u32[]{:S(2)}, u32[]{:S(2)}) collective-permute-start(bf16[7,40,1152]{2,1,0:T(8,128)(2,1)} %get-tuple-element.25), channel_id=1, source_target_pairs={{0,32},{32,64},{64,96},{96,128},{128,160},{160,192},{192,224},{224... | collective-permute-start | bytes 1935368 | tf_op jit(solution)/shard_map/ppermute | solution.py:186
  6.4 4.0 %collective-permute-start.1 = (bf16[7,40,1152]{2,1,0:T(8,128)(2,1)}, bf16[7,40,1152]{2,1,0:T(8,128)(2,1)S(1)}, u32[]{:S(2)}, u32[]{:S(2)}) collective-permute-start(bf16[7,40,1152]{2,1,0:T(8,128)(2,1)} %get-tuple-element.26), channel_id=1, source_target_pairs={{0,224},{32,0},{64,32},{96,64},{128,96},{160,128},{192,160},{224,1... | collective-permute-start | bytes 1935368 | tf_op jit(solution)/shard_map/ppermute | solution.py:186
  10.5 10.1 %products.1 = (bf16[2,40,1152]{2,1,0:T(8,128)(2,1)}, bf16[7,40,1152]{2,1,0:T(8,128)(2,1)}, bf16[7,40,1152]{2,1,0:T(8,128)(2,1)}) custom-call(s32[6,6,20]{2,1,0:T(8,128)} %bitcast.2, s32[6,6]{1,0:T(8,128)} %gpat_ref.1, bf16[40,384,384]{2,1,0:T(8,128)(2,1)} %basis_ref.3, bf16[384,384]{1,0:T(8,128)(2,1)} %occ_ref.1, bf16[384,384]{1,0:T(8,128)(2,1)} %vir_ref.1), custom_call_target="tpu_custom_call" | custom-call | flops 1132462080 | bytes 14000000 | tf_op jit(solution)/shard_map/products/pallas_call | solution.py:158
  20.6 4.5 %collective-permute-done = bf16[7,40,1152]{2,1,0:T(8,128)(2,1)S(1)} collective-permute-done((bf16[7,40,1152]{2,1,0:T(8,128)(2,1)}, bf16[7,40,1152]{2,1,0:T(8,128)(2,1)S(1)}, u32[]{:S(2)}, u32[]{:S(2)}) %collective-permute-start) | collective-permute-done | bytes 645152 | tf_op jit(solution)/shard_map/ppermute | solution.py:186
  25.1 0.0 collective-permute-done.1
  25.1 0.1 pad_maximum_fusion.refs_9_
  25.3 0.1 collective-permute-start.5
  25.4 3.1 %collective-permute-start.3 = (bf16[6,40,1152]{2,1,0:T(8,128)(2,1)S(1)}, bf16[6,40,1152]{2,1,0:T(8,128)(2,1)S(1)}, u32[]{:S(2)}, u32[]{:S(2)}) collective-permute-start(bf16[6,40,1152]{2,1,0:T(8,128)(2,1)S(1)} %pad_maximum_fusion.refs_9_), channel_id=1, source_target_pairs={{0,24},{8,0},{16,8},{24,16},{1,25},{9,1},{17,9},{25,17},{2,26},{10... | collective-permute-start | bytes 1658888 | tf_op jit(solution)/shard_map/ppermute | solution.py:186
  28.5 0.0 collective-permute-start.2
  28.5 3.1 %collective-permute-start.7 = (bf16[5,40,1152]{2,1,0:T(8,128)(2,1)S(1)}, bf16[5,40,1152]{2,1,0:T(8,128)(2,1)S(1)}, u32[]{:S(2)}, u32[]{:S(2)}) collective-permute-start(bf16[5,40,1152]{2,1,0:T(8,128)(2,1)S(1)} %slice.89), channel_id=1, source_target_pairs={{0,224},{32,0},{64,32},{96,64},{128,96},{160,128},{192,160},{224,1... | collective-permute-start | bytes 1382408 | tf_op jit(solution)/shard_map/ppermute | solution.py:186
  31.7 6.7 %collective-permute-done.5 = bf16[5,40,1152]{2,1,0:T(8,128)(2,1)S(1)} collective-permute-done((bf16[5,40,1152]{2,1,0:T(8,128)(2,1)S(1)}, bf16[5,40,1152]{2,1,0:T(8,128)(2,1)S(1)}, u32[]{:S(2)}, u32[]{:S(2)}) %collective-permute-start.5) | collective-permute-done | bytes 460832 | tf_op jit(solution)/shard_map/ppermute | solution.py:186
  38.4 0.8 collective-permute-start.9
  39.2 2.6 %collective-permute-start.6 = (bf16[2,40,1152]{2,1,0:T(8,128)(2,1)S(1)}, bf16[2,40,1152]{2,1,0:T(8,128)(2,1)S(1)}, u32[]{:S(2)}, u32[]{:S(2)}) collective-permute-start(bf16[2,40,1152]{2,1,0:T(8,128)(2,1)S(1)} %get-tuple-element.44), channel_id=1, source_target_pairs={{0,32},{32,64},{64,96},{96,128},{128,160},{160,192},{192,224},{224... | collective-permute-start | bytes 552968 | tf_op jit(solution)/shard_map/ppermute | solution.py:186
  41.8 0.0 collective-permute-done.7
  41.8 2.0 %collective-permute-start.10 = (bf16[1,40,1152]{2,1,0:T(8,128)(2,1)S(1)}, bf16[1,40,1152]{2,1,0:T(8,128)(2,1)S(1)}, u32[]{:S(2)}, u32[]{:S(2)}) collective-permute-start(bf16[1,40,1152]{2,1,0:T(8,128)(2,1)S(1)} %slice.95), channel_id=1, source_target_pairs={{0,192},{32,224},{64,0},{96,32},{128,64},{160,96},{192,128},{224,1... | collective-permute-start | bytes 276488 | tf_op jit(solution)/shard_map/ppermute | solution.py:186
  43.9 0.0 collective-permute-done.3.refs_11_
  43.9 1.0 collective-permute-start.8
  45.0 0.0 collective-permute-done.2.refs_10_
  45.0 3.0 %collective-permute-start.23 = (bf16[4,40,1152]{2,1,0:T(8,128)(2,1)S(1)}, bf16[4,40,1152]{2,1,0:T(8,128)(2,1)S(1)}, u32[]{:S(2)}, u32[]{:S(2)}) collective-permute-start(bf16[4,40,1152]{2,1,0:T(8,128)(2,1)S(1)} %pad_maximum_fusion.1.refs_14_), channel_id=1, source_target_pairs={{0,24},{8,0},{16,8},{24,16},{1,25},{9,1},{17,9},{25,17},{2,26},{10... | collective-permute-start | bytes 1105928 | tf_op jit(solution)/shard_map/ppermute | solution.py:186
  48.0 0.0 collective-permute-done.6
  48.0 1.0 collective-permute-start.4
  49.0 1.9 %collective-permute-done.8 = bf16[2,40,1152]{2,1,0:T(8,128)(2,1)S(1)} collective-permute-done((bf16[2,40,1152]{2,1,0:T(8,128)(2,1)S(1)}, bf16[2,40,1152]{2,1,0:T(8,128)(2,1)S(1)}, u32[]{:S(2)}, u32[]{:S(2)}) %collective-permute-start.8) | collective-permute-done | bytes 184352 | tf_op jit(solution)/shard_map/ppermute | solution.py:186
  50.9 2.3 %collective-permute-start.14 = (bf16[7,40,1152]{2,1,0:T(8,128)(2,1)}, bf16[7,40,1152]{2,1,0:T(8,128)(2,1)S(1)}, u32[]{:S(2)}, u32[]{:S(2)}) collective-permute-start(bf16[7,40,1152]{2,1,0:T(8,128)(2,1)} %get-tuple-element.36), channel_id=1, source_target_pairs={{0,224},{32,0},{64,32},{96,64},{128,96},{160,128},{192,160},{224,1... | collective-permute-start | bytes 1935368 | tf_op jit(solution)/shard_map/ppermute | solution.py:186
  53.2 0.0 collective-permute-done.9
  53.3 0.0 collective-permute-done.10
  53.3 3.1 %collective-permute-start.12 = (bf16[6,40,1152]{2,1,0:T(8,128)(2,1)S(1)}, bf16[6,40,1152]{2,1,0:T(8,128)(2,1)S(1)}, u32[]{:S(2)}, u32[]{:S(2)}) collective-permute-start(bf16[6,40,1152]{2,1,0:T(8,128)(2,1)S(1)} %constant_dynamic-update-slice_fusion.refs_19_), channel_id=1, source_target_pairs={{0,24},{8,0},{16,8},{24,16},{1,25},{9,1},{17,9},{25,17},{2,26},{10... | collective-permute-start | bytes 1658888 | tf_op jit(solution)/shard_map/ppermute | solution.py:186
  56.4 0.0 collective-permute-start.11
  56.4 6.7 %collective-permute-done.4.refs_1_ = bf16[7,40,1152]{2,1,0:T(8,128)(2,1)S(1)} collective-permute-done((bf16[7,40,1152]{2,1,0:T(8,128)(2,1)}, bf16[7,40,1152]{2,1,0:T(8,128)(2,1)S(1)}, u32[]{:S(2)}, u32[]{:S(2)}) %collective-permute-start.4) | collective-permute-done | bytes 645152 | tf_op jit(solution)/shard_map/ppermute | solution.py:186
  63.1 1.6 %collective-permute-start.22 = (bf16[4,40,1152]{2,1,0:T(8,128)(2,1)S(1)}, bf16[4,40,1152]{2,1,0:T(8,128)(2,1)S(1)}, u32[]{:S(2)}, u32[]{:S(2)}) collective-permute-start(bf16[4,40,1152]{2,1,0:T(8,128)(2,1)S(1)} %pad_maximum_fusion.1.refs_14_), channel_id=1, source_target_pairs={{0,8},{8,16},{16,24},{24,0},{1,9},{9,17},{17,25},{25,1},{2,10},{10... | collective-permute-start | bytes 1105928 | tf_op jit(solution)/shard_map/ppermute | solution.py:186
  64.7 0.0 collective-permute-done.14.refs_8_
  64.8 1.8 %collective-permute-start.13 = (bf16[5,40,1152]{2,1,0:T(8,128)(2,1)S(1)}, bf16[5,40,1152]{2,1,0:T(8,128)(2,1)S(1)}, u32[]{:S(2)}, u32[]{:S(2)}) collective-permute-start(bf16[5,40,1152]{2,1,0:T(8,128)(2,1)S(1)} %slice.96), channel_id=1, source_target_pairs={{0,32},{32,64},{64,96},{96,128},{128,160},{160,192},{192,224},{224... | collective-permute-start | bytes 1382408 | tf_op jit(solution)/shard_map/ppermute | solution.py:186
  66.6 0.0 collective-permute-done.23.refs_16_
  66.6 1.6 %collective-permute-start.15 = (bf16[5,40,1152]{2,1,0:T(8,128)(2,1)S(1)}, bf16[5,40,1152]{2,1,0:T(8,128)(2,1)S(1)}, u32[]{:S(2)}, u32[]{:S(2)}) collective-permute-start(bf16[5,40,1152]{2,1,0:T(8,128)(2,1)S(1)} %slice.97), channel_id=1, source_target_pairs={{0,224},{32,0},{64,32},{96,64},{128,96},{160,128},{192,160},{224,1... | collective-permute-start | bytes 1382408 | tf_op jit(solution)/shard_map/ppermute | solution.py:186
  68.2 8.1 %collective-permute-done.22.refs_15_ = bf16[4,40,1152]{2,1,0:T(8,128)(2,1)S(1)} collective-permute-done((bf16[4,40,1152]{2,1,0:T(8,128)(2,1)S(1)}, bf16[4,40,1152]{2,1,0:T(8,128)(2,1)S(1)}, u32[]{:S(2)}, u32[]{:S(2)}) %collective-permute-start.22) | collective-permute-done | bytes 368672 | tf_op jit(solution)/shard_map/ppermute | solution.py:186
  76.3 0.9 collective-permute-start.21
  77.3 0.0 collective-permute-done.12.refs_21_
  77.3 1.2 collective-permute-start.20
  78.5 0.0 collective-permute-done.11.refs_20_
  78.5 2.2 %collective-permute-start.25 = (bf16[2,40,1152]{2,1,0:T(8,128)(2,1)S(1)}, bf16[2,40,1152]{2,1,0:T(8,128)(2,1)S(1)}, u32[]{:S(2)}, u32[]{:S(2)}) collective-permute-start(bf16[2,40,1152]{2,1,0:T(8,128)(2,1)S(1)} %slice.101), channel_id=1, source_target_pairs={{0,24},{8,0},{16,8},{24,16},{1,25},{9,1},{17,9},{25,17},{2,26},{10... | collective-permute-start | bytes 552968 | tf_op jit(solution)/shard_map/ppermute | solution.py:186
  80.7 0.0 collective-permute-done.13.refs_2_
  80.7 0.0 collective-permute-start.24
  80.7 0.0 collective-permute-done.15.refs_7_
  80.8 3.3 %collective-permute-start.27 = (bf16[3,40,1152]{2,1,0:T(8,128)(2,1)S(1)}, bf16[3,40,1152]{2,1,0:T(8,128)(2,1)S(1)}, u32[]{:S(2)}, u32[]{:S(2)}) collective-permute-start(bf16[3,40,1152]{2,1,0:T(8,128)(2,1)S(1)} %slice.87), channel_id=1, source_target_pairs={{0,24},{8,0},{16,8},{24,16},{1,25},{9,1},{17,9},{25,17},{2,26},{10... | collective-permute-start | bytes 829448 | tf_op jit(solution)/shard_map/ppermute | solution.py:186
  84.1 1.5 %collective-permute-done.21.refs_13_ = bf16[3,40,1152]{2,1,0:T(8,128)(2,1)S(1)} collective-permute-done((bf16[3,40,1152]{2,1,0:T(8,128)(2,1)S(1)}, bf16[3,40,1152]{2,1,0:T(8,128)(2,1)S(1)}, u32[]{:S(2)}, u32[]{:S(2)}) %collective-permute-start.21) | collective-permute-done | bytes 276512 | tf_op jit(solution)/shard_map/ppermute | solution.py:186
  85.6 0.0 collective-permute-start.26
  85.7 2.4 %collective-permute-done.20.refs_12_ = bf16[3,40,1152]{2,1,0:T(8,128)(2,1)S(1)} collective-permute-done((bf16[3,40,1152]{2,1,0:T(8,128)(2,1)S(1)}, bf16[3,40,1152]{2,1,0:T(8,128)(2,1)S(1)}, u32[]{:S(2)}, u32[]{:S(2)}) %collective-permute-start.20) | collective-permute-done | bytes 276512 | tf_op jit(solution)/shard_map/ppermute | solution.py:186
  88.1 1.0 collective-permute-start.18
  89.1 0.0 collective-permute-done.25.refs_18_
  89.1 0.0 collective-permute-start.19
  89.1 1.7 %collective-permute-done.24.refs_17_ = bf16[2,40,1152]{2,1,0:T(8,128)(2,1)S(1)} collective-permute-done((bf16[2,40,1152]{2,1,0:T(8,128)(2,1)S(1)}, bf16[2,40,1152]{2,1,0:T(8,128)(2,1)S(1)}, u32[]{:S(2)}, u32[]{:S(2)}) %collective-permute-start.24) | collective-permute-done | bytes 184352 | tf_op jit(solution)/shard_map/ppermute | solution.py:186
  90.8 0.4 collective-permute-start.16
  91.2 2.5 %collective-permute-done.18.refs_5_ = bf16[1,40,1152]{2,1,0:T(8,128)(2,1)S(1)} collective-permute-done((bf16[1,40,1152]{2,1,0:T(8,128)(2,1)S(1)}, bf16[1,40,1152]{2,1,0:T(8,128)(2,1)S(1)}, u32[]{:S(2)}, u32[]{:S(2)}) %collective-permute-start.18) | collective-permute-done | bytes 92192 | tf_op jit(solution)/shard_map/ppermute | solution.py:186
  93.7 1.5 %collective-permute-start.17 = (bf16[1,40,1152]{2,1,0:T(8,128)(2,1)S(1)}, bf16[1,40,1152]{2,1,0:T(8,128)(2,1)S(1)}, u32[]{:S(2)}, u32[]{:S(2)}) collective-permute-start(bf16[1,40,1152]{2,1,0:T(8,128)(2,1)S(1)} %slice.77), channel_id=1, source_target_pairs={{0,64},{32,96},{64,128},{96,160},{128,192},{160,224},{192,0},{224,... | collective-permute-start | bytes 276488 | tf_op jit(solution)/shard_map/ppermute | solution.py:186
  95.2 5.8 %collective-permute-done.17.refs_4_ = bf16[1,40,1152]{2,1,0:T(8,128)(2,1)S(1)} collective-permute-done((bf16[1,40,1152]{2,1,0:T(8,128)(2,1)S(1)}, bf16[1,40,1152]{2,1,0:T(8,128)(2,1)S(1)}, u32[]{:S(2)}, u32[]{:S(2)}) %collective-permute-start.17) | collective-permute-done | bytes 92192 | tf_op jit(solution)/shard_map/ppermute | solution.py:186
  101.0 0.0 collective-permute-done.19.refs_6_
  101.0 0.0 collective-permute-done.16.refs_3_
  101.0 0.0 collective-permute-done.27.refs_23_
  101.0 0.0 collective-permute-done.26.refs_22_
  101.1 2.4 %contract.1 = bf16[8,40,1280]{2,1,0:T(8,128)(2,1)S(1)} custom-call(bf16[2,40,1152]{2,1,0:T(8,128)(2,1)S(1)} %copy-done, bf16[7,40,1152]{2,1,0:T(8,128)(2,1)S(1)} %collective-permute-done.4.refs_1_, bf16[5,40,1152]{2,1,0:T(8,128)(2,1)S(1)} %collective-permute-done.13.refs_2_, bf16[2,40,1152]{2,1,0:T(8,128)(2,1)S(1)} %collective-permute-done.16.refs_3_, ...), custom_call_target="tpu_custom_call" | custom-call | flops 1887436800 | bytes 10000000 | tf_op jit(solution)/shard_map/contract/pallas_call | solution.py:272
  103.5 16.9 %all_to_all.10.in_ref = bf16[8,40,1280]{2,1,0:T(8,128)(2,1)} all-to-all(bf16[8,40,1280]{2,1,0:T(8,128)(2,1)S(1)} %contract.1), channel_id=1, replica_groups=mesh['z'=8,'y'=4,'x'=4,'core'=2] {'x','core'}, dimensions={0} | all-to-all | bytes 1638400 | tf_op jit(solution)/shard_map/all_to_all | solution.py:345
  120.4 2.1 %pack.1 = f32[32,16,128]{2,1,0:T(8,128)} custom-call(bf16[8,40,1280]{2,1,0:T(8,128)(2,1)} %all_to_all.10.in_ref), custom_call_target="tpu_custom_call" | custom-call | tf_op jit(solution)/shard_map/pack/pallas_call | solution.py:305
  122.5 18.1 %all_to_all.11.in_ref = f32[32,16,128]{2,1,0:T(8,128)} all-to-all(f32[32,16,128]{2,1,0:T(8,128)} %pack.1), channel_id=1, replica_groups=mesh['z'=8,'y'=4,'x'=4,'core'=2] {'z','y'}, dimensions={0} | all-to-all | bytes 524288 | tf_op jit(solution)/shard_map/all_to_all | solution.py:346
  140.6 1.7 %finish.1 = f32[40,160]{1,0:T(8,128)} custom-call(f32[32,16,128]{2,1,0:T(8,128)} %all_to_all.11.in_ref), custom_call_target="tpu_custom_call" | custom-call | tf_op jit(solution)/shard_map/finish/pallas_call | solution.py:330
  (29 shorter events, 0.5 us)
Async XLA Ops:
  4.4 20.7 %copy-start.1 = (bf16[2,40,1152]{2,1,0:T(8,128)(2,1)S(1)}, bf16[2,40,1152]{2,1,0:T(8,128)(2,1)}, u32[]{:S(2)}) copy-start(bf16[2,40,1152]{2,1,0:T(8,128)(2,1)} %get-tuple-element.27) | copy-start | bytes 552964
  4.4 20.7 %collective-permute-start = (bf16[7,40,1152]{2,1,0:T(8,128)(2,1)}, bf16[7,40,1152]{2,1,0:T(8,128)(2,1)S(1)}, u32[]{:S(2)}, u32[]{:S(2)}) collective-permute-start(bf16[7,40,1152]{2,1,0:T(8,128)(2,1)} %get-tuple-element.25), channel_id=1, source_target_pairs={{0,32},{32,64},{64,96},{96,128},{128,160},{160,192},{192,224},{224... | collective-permute-start | bytes 1935368 | tf_op jit(solution)/shard_map/ppermute | solution.py:186
  6.4 18.7 %collective-permute-start.1 = (bf16[7,40,1152]{2,1,0:T(8,128)(2,1)}, bf16[7,40,1152]{2,1,0:T(8,128)(2,1)S(1)}, u32[]{:S(2)}, u32[]{:S(2)}) collective-permute-start(bf16[7,40,1152]{2,1,0:T(8,128)(2,1)} %get-tuple-element.26), channel_id=1, source_target_pairs={{0,224},{32,0},{64,32},{96,64},{128,96},{160,128},{192,160},{224,1... | collective-permute-start | bytes 1935368 | tf_op jit(solution)/shard_map/ppermute | solution.py:186
  20.6 80.5 %copy-start = (bf16[2,40,1152]{2,1,0:T(8,128)(2,1)S(1)}, bf16[2,40,1152]{2,1,0:T(8,128)(2,1)}, u32[]{:S(2)}) copy-start(bf16[2,40,1152]{2,1,0:T(8,128)(2,1)} %get-tuple-element.24.refs_0_) | copy-start | bytes 552964
  25.3 13.0 %collective-permute-start.5 = (bf16[5,40,1152]{2,1,0:T(8,128)(2,1)S(1)}, bf16[5,40,1152]{2,1,0:T(8,128)(2,1)S(1)}, u32[]{:S(2)}, u32[]{:S(2)}) collective-permute-start(bf16[5,40,1152]{2,1,0:T(8,128)(2,1)S(1)} %slice.88), channel_id=1, source_target_pairs={{0,32},{32,64},{64,96},{96,128},{128,160},{160,192},{192,224},{224... | collective-permute-start | bytes 1382408 | tf_op jit(solution)/shard_map/ppermute | solution.py:186
  25.4 18.5 %collective-permute-start.3 = (bf16[6,40,1152]{2,1,0:T(8,128)(2,1)S(1)}, bf16[6,40,1152]{2,1,0:T(8,128)(2,1)S(1)}, u32[]{:S(2)}, u32[]{:S(2)}) collective-permute-start(bf16[6,40,1152]{2,1,0:T(8,128)(2,1)S(1)} %pad_maximum_fusion.refs_9_), channel_id=1, source_target_pairs={{0,24},{8,0},{16,8},{24,16},{1,25},{9,1},{17,9},{25,17},{2,26},{10... | collective-permute-start | bytes 1658888 | tf_op jit(solution)/shard_map/ppermute | solution.py:186
  28.5 16.5 %collective-permute-start.2 = (bf16[6,40,1152]{2,1,0:T(8,128)(2,1)S(1)}, bf16[6,40,1152]{2,1,0:T(8,128)(2,1)S(1)}, u32[]{:S(2)}, u32[]{:S(2)}) collective-permute-start(bf16[6,40,1152]{2,1,0:T(8,128)(2,1)S(1)} %pad_maximum_fusion.refs_9_), channel_id=1, source_target_pairs={{0,8},{8,16},{16,24},{24,0},{1,9},{9,17},{17,25},{25,1},{2,10},{10... | collective-permute-start | bytes 1658888 | tf_op jit(solution)/shard_map/ppermute | solution.py:186
  28.5 13.3 %collective-permute-start.7 = (bf16[5,40,1152]{2,1,0:T(8,128)(2,1)S(1)}, bf16[5,40,1152]{2,1,0:T(8,128)(2,1)S(1)}, u32[]{:S(2)}, u32[]{:S(2)}) collective-permute-start(bf16[5,40,1152]{2,1,0:T(8,128)(2,1)S(1)} %slice.89), channel_id=1, source_target_pairs={{0,224},{32,0},{64,32},{96,64},{128,96},{160,128},{192,160},{224,1... | collective-permute-start | bytes 1382408 | tf_op jit(solution)/shard_map/ppermute | solution.py:186
  38.4 14.9 %collective-permute-start.9 = (bf16[1,40,1152]{2,1,0:T(8,128)(2,1)S(1)}, bf16[1,40,1152]{2,1,0:T(8,128)(2,1)S(1)}, u32[]{:S(2)}, u32[]{:S(2)}) collective-permute-start(bf16[1,40,1152]{2,1,0:T(8,128)(2,1)S(1)} %slice.94), channel_id=1, source_target_pairs={{0,64},{32,96},{64,128},{96,160},{128,192},{160,224},{192,0},{224,... | collective-permute-start | bytes 276488 | tf_op jit(solution)/shard_map/ppermute | solution.py:186
  39.2 8.8 %collective-permute-start.6 = (bf16[2,40,1152]{2,1,0:T(8,128)(2,1)S(1)}, bf16[2,40,1152]{2,1,0:T(8,128)(2,1)S(1)}, u32[]{:S(2)}, u32[]{:S(2)}) collective-permute-start(bf16[2,40,1152]{2,1,0:T(8,128)(2,1)S(1)} %get-tuple-element.44), channel_id=1, source_target_pairs={{0,32},{32,64},{64,96},{96,128},{128,160},{160,192},{192,224},{224... | collective-permute-start | bytes 552968 | tf_op jit(solution)/shard_map/ppermute | solution.py:186
  41.8 11.4 %collective-permute-start.10 = (bf16[1,40,1152]{2,1,0:T(8,128)(2,1)S(1)}, bf16[1,40,1152]{2,1,0:T(8,128)(2,1)S(1)}, u32[]{:S(2)}, u32[]{:S(2)}) collective-permute-start(bf16[1,40,1152]{2,1,0:T(8,128)(2,1)S(1)} %slice.95), channel_id=1, source_target_pairs={{0,192},{32,224},{64,0},{96,32},{128,64},{160,96},{192,128},{224,1... | collective-permute-start | bytes 276488 | tf_op jit(solution)/shard_map/ppermute | solution.py:186
  43.9 7.0 %collective-permute-start.8 = (bf16[2,40,1152]{2,1,0:T(8,128)(2,1)S(1)}, bf16[2,40,1152]{2,1,0:T(8,128)(2,1)S(1)}, u32[]{:S(2)}, u32[]{:S(2)}) collective-permute-start(bf16[2,40,1152]{2,1,0:T(8,128)(2,1)S(1)} %get-tuple-element.46), channel_id=1, source_target_pairs={{0,224},{32,0},{64,32},{96,64},{128,96},{160,128},{192,160},{224,1... | collective-permute-start | bytes 552968 | tf_op jit(solution)/shard_map/ppermute | solution.py:186
  45.0 21.6 %collective-permute-start.23 = (bf16[4,40,1152]{2,1,0:T(8,128)(2,1)S(1)}, bf16[4,40,1152]{2,1,0:T(8,128)(2,1)S(1)}, u32[]{:S(2)}, u32[]{:S(2)}) collective-permute-start(bf16[4,40,1152]{2,1,0:T(8,128)(2,1)S(1)} %pad_maximum_fusion.1.refs_14_), channel_id=1, source_target_pairs={{0,24},{8,0},{16,8},{24,16},{1,25},{9,1},{17,9},{25,17},{2,26},{10... | collective-permute-start | bytes 1105928 | tf_op jit(solution)/shard_map/ppermute | solution.py:186
  48.0 15.1 %collective-permute-start.4 = (bf16[7,40,1152]{2,1,0:T(8,128)(2,1)}, bf16[7,40,1152]{2,1,0:T(8,128)(2,1)S(1)}, u32[]{:S(2)}, u32[]{:S(2)}) collective-permute-start(bf16[7,40,1152]{2,1,0:T(8,128)(2,1)} %get-tuple-element.33), channel_id=1, source_target_pairs={{0,32},{32,64},{64,96},{96,128},{128,160},{160,192},{192,224},{224... | collective-permute-start | bytes 1935368 | tf_op jit(solution)/shard_map/ppermute | solution.py:186
  50.9 13.9 %collective-permute-start.14 = (bf16[7,40,1152]{2,1,0:T(8,128)(2,1)}, bf16[7,40,1152]{2,1,0:T(8,128)(2,1)S(1)}, u32[]{:S(2)}, u32[]{:S(2)}) collective-permute-start(bf16[7,40,1152]{2,1,0:T(8,128)(2,1)} %get-tuple-element.36), channel_id=1, source_target_pairs={{0,224},{32,0},{64,32},{96,64},{128,96},{160,128},{192,160},{224,1... | collective-permute-start | bytes 1935368 | tf_op jit(solution)/shard_map/ppermute | solution.py:186
  53.3 24.0 %collective-permute-start.12 = (bf16[6,40,1152]{2,1,0:T(8,128)(2,1)S(1)}, bf16[6,40,1152]{2,1,0:T(8,128)(2,1)S(1)}, u32[]{:S(2)}, u32[]{:S(2)}) collective-permute-start(bf16[6,40,1152]{2,1,0:T(8,128)(2,1)S(1)} %constant_dynamic-update-slice_fusion.refs_19_), channel_id=1, source_target_pairs={{0,24},{8,0},{16,8},{24,16},{1,25},{9,1},{17,9},{25,17},{2,26},{10... | collective-permute-start | bytes 1658888 | tf_op jit(solution)/shard_map/ppermute | solution.py:186
  56.4 22.1 %collective-permute-start.11 = (bf16[6,40,1152]{2,1,0:T(8,128)(2,1)S(1)}, bf16[6,40,1152]{2,1,0:T(8,128)(2,1)S(1)}, u32[]{:S(2)}, u32[]{:S(2)}) collective-permute-start(bf16[6,40,1152]{2,1,0:T(8,128)(2,1)S(1)} %constant_dynamic-update-slice_fusion.refs_19_), channel_id=1, source_target_pairs={{0,8},{8,16},{16,24},{24,0},{1,9},{9,17},{17,25},{25,1},{2,10},{10... | collective-permute-start | bytes 1658888 | tf_op jit(solution)/shard_map/ppermute | solution.py:186
  63.1 13.2 %collective-permute-start.22 = (bf16[4,40,1152]{2,1,0:T(8,128)(2,1)S(1)}, bf16[4,40,1152]{2,1,0:T(8,128)(2,1)S(1)}, u32[]{:S(2)}, u32[]{:S(2)}) collective-permute-start(bf16[4,40,1152]{2,1,0:T(8,128)(2,1)S(1)} %pad_maximum_fusion.1.refs_14_), channel_id=1, source_target_pairs={{0,8},{8,16},{16,24},{24,0},{1,9},{9,17},{17,25},{25,1},{2,10},{10... | collective-permute-start | bytes 1105928 | tf_op jit(solution)/shard_map/ppermute | solution.py:186
  64.8 15.9 %collective-permute-start.13 = (bf16[5,40,1152]{2,1,0:T(8,128)(2,1)S(1)}, bf16[5,40,1152]{2,1,0:T(8,128)(2,1)S(1)}, u32[]{:S(2)}, u32[]{:S(2)}) collective-permute-start(bf16[5,40,1152]{2,1,0:T(8,128)(2,1)S(1)} %slice.96), channel_id=1, source_target_pairs={{0,32},{32,64},{64,96},{96,128},{128,160},{160,192},{192,224},{224... | collective-permute-start | bytes 1382408 | tf_op jit(solution)/shard_map/ppermute | solution.py:186
  66.6 14.1 %collective-permute-start.15 = (bf16[5,40,1152]{2,1,0:T(8,128)(2,1)S(1)}, bf16[5,40,1152]{2,1,0:T(8,128)(2,1)S(1)}, u32[]{:S(2)}, u32[]{:S(2)}) collective-permute-start(bf16[5,40,1152]{2,1,0:T(8,128)(2,1)S(1)} %slice.97), channel_id=1, source_target_pairs={{0,224},{32,0},{64,32},{96,64},{128,96},{160,128},{192,160},{224,1... | collective-permute-start | bytes 1382408 | tf_op jit(solution)/shard_map/ppermute | solution.py:186
  76.3 9.3 %collective-permute-start.21 = (bf16[3,40,1152]{2,1,0:T(8,128)(2,1)S(1)}, bf16[3,40,1152]{2,1,0:T(8,128)(2,1)S(1)}, u32[]{:S(2)}, u32[]{:S(2)}) collective-permute-start(bf16[3,40,1152]{2,1,0:T(8,128)(2,1)S(1)} %slice.81), channel_id=1, source_target_pairs={{0,24},{8,0},{16,8},{24,16},{1,25},{9,1},{17,9},{25,17},{2,26},{10... | collective-permute-start | bytes 829448 | tf_op jit(solution)/shard_map/ppermute | solution.py:186
  77.3 10.8 %collective-permute-start.20 = (bf16[3,40,1152]{2,1,0:T(8,128)(2,1)S(1)}, bf16[3,40,1152]{2,1,0:T(8,128)(2,1)S(1)}, u32[]{:S(2)}, u32[]{:S(2)}) collective-permute-start(bf16[3,40,1152]{2,1,0:T(8,128)(2,1)S(1)} %slice.80), channel_id=1, source_target_pairs={{0,8},{8,16},{16,24},{24,0},{1,9},{9,17},{17,25},{25,1},{2,10},{10... | collective-permute-start | bytes 829448 | tf_op jit(solution)/shard_map/ppermute | solution.py:186
  78.5 10.6 %collective-permute-start.25 = (bf16[2,40,1152]{2,1,0:T(8,128)(2,1)S(1)}, bf16[2,40,1152]{2,1,0:T(8,128)(2,1)S(1)}, u32[]{:S(2)}, u32[]{:S(2)}) collective-permute-start(bf16[2,40,1152]{2,1,0:T(8,128)(2,1)S(1)} %slice.101), channel_id=1, source_target_pairs={{0,24},{8,0},{16,8},{24,16},{1,25},{9,1},{17,9},{25,17},{2,26},{10... | collective-permute-start | bytes 552968 | tf_op jit(solution)/shard_map/ppermute | solution.py:186
  80.7 10.1 %collective-permute-start.24 = (bf16[2,40,1152]{2,1,0:T(8,128)(2,1)S(1)}, bf16[2,40,1152]{2,1,0:T(8,128)(2,1)S(1)}, u32[]{:S(2)}, u32[]{:S(2)}) collective-permute-start(bf16[2,40,1152]{2,1,0:T(8,128)(2,1)S(1)} %slice.100), channel_id=1, source_target_pairs={{0,8},{8,16},{16,24},{24,0},{1,9},{9,17},{17,25},{25,1},{2,10},{10... | collective-permute-start | bytes 552968 | tf_op jit(solution)/shard_map/ppermute | solution.py:186
  80.8 20.2 %collective-permute-start.27 = (bf16[3,40,1152]{2,1,0:T(8,128)(2,1)S(1)}, bf16[3,40,1152]{2,1,0:T(8,128)(2,1)S(1)}, u32[]{:S(2)}, u32[]{:S(2)}) collective-permute-start(bf16[3,40,1152]{2,1,0:T(8,128)(2,1)S(1)} %slice.87), channel_id=1, source_target_pairs={{0,24},{8,0},{16,8},{24,16},{1,25},{9,1},{17,9},{25,17},{2,26},{10... | collective-permute-start | bytes 829448 | tf_op jit(solution)/shard_map/ppermute | solution.py:186
  85.6 15.4 %collective-permute-start.26 = (bf16[3,40,1152]{2,1,0:T(8,128)(2,1)S(1)}, bf16[3,40,1152]{2,1,0:T(8,128)(2,1)S(1)}, u32[]{:S(2)}, u32[]{:S(2)}) collective-permute-start(bf16[3,40,1152]{2,1,0:T(8,128)(2,1)S(1)} %slice.86), channel_id=1, source_target_pairs={{0,8},{8,16},{16,24},{24,0},{1,9},{9,17},{17,25},{25,1},{2,10},{10... | collective-permute-start | bytes 829448 | tf_op jit(solution)/shard_map/ppermute | solution.py:186
  88.1 5.5 %collective-permute-start.18 = (bf16[1,40,1152]{2,1,0:T(8,128)(2,1)S(1)}, bf16[1,40,1152]{2,1,0:T(8,128)(2,1)S(1)}, u32[]{:S(2)}, u32[]{:S(2)}) collective-permute-start(bf16[1,40,1152]{2,1,0:T(8,128)(2,1)S(1)} %slice.78), channel_id=1, source_target_pairs={{0,192},{32,224},{64,0},{96,32},{128,64},{160,96},{192,128},{224,1... | collective-permute-start | bytes 276488 | tf_op jit(solution)/shard_map/ppermute | solution.py:186
  89.1 11.9 %collective-permute-start.19 = (bf16[2,40,1152]{2,1,0:T(8,128)(2,1)S(1)}, bf16[2,40,1152]{2,1,0:T(8,128)(2,1)S(1)}, u32[]{:S(2)}, u32[]{:S(2)}) collective-permute-start(bf16[2,40,1152]{2,1,0:T(8,128)(2,1)S(1)} %slice.79), channel_id=1, source_target_pairs={{0,224},{32,0},{64,32},{96,64},{128,96},{160,128},{192,160},{224,1... | collective-permute-start | bytes 552968 | tf_op jit(solution)/shard_map/ppermute | solution.py:186
  90.8 10.2 %collective-permute-start.16 = (bf16[2,40,1152]{2,1,0:T(8,128)(2,1)S(1)}, bf16[2,40,1152]{2,1,0:T(8,128)(2,1)S(1)}, u32[]{:S(2)}, u32[]{:S(2)}) collective-permute-start(bf16[2,40,1152]{2,1,0:T(8,128)(2,1)S(1)} %slice.76), channel_id=1, source_target_pairs={{0,32},{32,64},{64,96},{96,128},{128,160},{160,192},{192,224},{224... | collective-permute-start | bytes 552968 | tf_op jit(solution)/shard_map/ppermute | solution.py:186
  93.7 7.4 %collective-permute-start.17 = (bf16[1,40,1152]{2,1,0:T(8,128)(2,1)S(1)}, bf16[1,40,1152]{2,1,0:T(8,128)(2,1)S(1)}, u32[]{:S(2)}, u32[]{:S(2)}) collective-permute-start(bf16[1,40,1152]{2,1,0:T(8,128)(2,1)S(1)} %slice.77), channel_id=1, source_target_pairs={{0,64},{32,96},{64,128},{96,160},{128,192},{160,224},{192,0},{224,... | collective-permute-start | bytes 276488 | tf_op jit(solution)/shard_map/ppermute | solution.py:186

commit v3 on v2

--- a/solution.py
+++ b/solution.py
@@ -37,7 +37,7 @@
     return out
 
 
-def emit(z, held, own_ref, plus_ref, minus_ref):
+def emit(z, held, own_ref, plus_ref, minus_ref, *far_refs):
     for d in range(NZ):
         dest = lax.rem(z + d, NZ)
         for j in range(SUB):
@@ -49,16 +49,18 @@
             elif d > 4:
                 out_ref, place = minus_ref, 2 * (7 - d) + h
             else:
-                out_ref, place = (plus_ref, minus_ref)[h], 6
+                out_ref, place = (far_refs[h], 0) if far_refs else ((plus_ref, minus_ref)[h], 6)
             for t in range(NAO // LANES):
                 rows = held[t, pl.ds(dest * SUB + j, LA, stride=ROWS), :]
                 out_ref[place, :, pl.ds((j % 3) * NAO + LANES * t, LANES)] = rows.astype(BF16)
 
 
-CHUNKS = tuple(jax.ShapeDtypeStruct((n, LA, HALF), BF16) for n in (2, 7, 7))
-
-
-def prep_kernel(pat_ref, basis_ref, own_ref, plus_ref, minus_ref, slab, held, sems):
+CHUNKS = tuple(jax.ShapeDtypeStruct((n, LA, HALF), BF16) for n in (2, 6, 6, 1, 1))
+WHOLE = tuple(jax.ShapeDtypeStruct((n, LA, HALF), BF16) for n in (2, 7, 7))
+
+
+def prep_kernel(pat_ref, basis_ref, *refs):
+    out_refs, (slab, held, sems) = refs[:-3], refs[-3:]
     z, y, r = places()
     place = z * NY + y
     steps = LA // 8
@@ -82,7 +84,7 @@
                 rows = slab[p, pl.ds(8 * jo, 8), :].astype(F32) * masks[jo]
                 for t in range(NAO // LANES):
                     held[t, pl.ds(p * ROWS + 8 * jo, 8), :] = rows[:, LANES * t : LANES * (t + 1)]
-    emit(z, held, own_ref, plus_ref, minus_ref)
+    emit(z, held, *out_refs)
 
 
 SMEM = pl.BlockSpec(memory_space=pltpu.SMEM)
@@ -96,13 +98,13 @@
         prep_kernel,
         out_shape=CHUNKS,
         in_specs=[SMEM, HBM],
-        out_specs=(VMEM, VMEM, VMEM),
+        out_specs=(VMEM,) * len(CHUNKS),
         scratch_shapes=[
             pltpu.VMEM((LA, ROWS, NAO), BF16),
             pltpu.VMEM((NAO // LANES, LA * ROWS, LANES), F32),
             pltpu.SemaphoreType.DMA((LA // 8,)),
         ],
-        compiler_params=pltpu.CompilerParams(vmem_limit_bytes=56 * MIB),
+        compiler_params=pltpu.CompilerParams(vmem_limit_bytes=54 * MIB),
         cost_estimate=pl.CostEstimate(flops=10**6, bytes_accessed=3 * 10**6, transcendentals=0),
         name="prep",
     )(pat, basis)
@@ -111,9 +113,8 @@
 STEPQ = 8
 
 
-def product_kernel(
-    pat_ref, gpat_ref, basis_ref, occ_ref, vir_ref, own_ref, plus_ref, minus_ref, first, held, occ, vir, masks
-):
+def product_kernel(pat_ref, gpat_ref, basis_ref, occ_ref, vir_ref, *refs):
+    out_refs, (first, held, occ, vir, masks) = refs[:-5], refs[-5:]
     i = pl.program_id(0)
     z, y, r = places()
     place = z * NY + y
@@ -151,13 +152,13 @@
             part = jnp.dot(first[pl.ds(t * n, n), :], v, preferred_element_type=F32)
             for u in range(NAO // LANES):
                 held[u, pl.ds(t * n, n), :] = part[:, LANES * u : LANES * (u + 1)]
-        emit(z, held, own_ref, plus_ref, minus_ref)
+        emit(z, held, *out_refs)
 
 
 def products(pat, gpat, basis, occ, vir):
     return pl.pallas_call(
         product_kernel,
-        out_shape=CHUNKS,
+        out_shape=WHOLE,
         grid=(LA // STEPQ,),
         in_specs=[
             SMEM,
@@ -166,7 +167,7 @@
             pl.BlockSpec((NAO, NAO), lambda i: (0, 0)),
             pl.BlockSpec((NAO, NAO), lambda i: (0, 0)),
         ],
-        out_specs=tuple(pl.BlockSpec(c.shape, lambda i: (0, 0, 0)) for c in CHUNKS),
+        out_specs=tuple(pl.BlockSpec(c.shape, lambda i: (0, 0, 0)) for c in WHOLE),
         scratch_shapes=[
             pltpu.VMEM((LA * ROWS, NAO), BF16),
             pltpu.VMEM((NAO // LANES, LA * ROWS, LANES), F32),
@@ -190,7 +191,7 @@
     return lax.optimization_barrier((value,) + others)[0]
 
 
-GROUPS = ((0, 1, 7), (2, 6), (3, 5, 4))
+GROUPS = ((0, 1, 7), (2, 6, 3, 5, 4))
 EORDER = (0, 1, 3, 2)
 
 
@@ -203,38 +204,38 @@
 
 
 def far_y(below, above):
-    n = below.shape[0] // 2
-    return shift(below[:n], 1, "y", NY), shift(above[n:], -1, "y", NY)
+    pairs = [(NC * y + c, NC * ((y + 1 - 2 * c) % NY) + c) for y in range(NY) for c in range(NC)]
+    value = jnp.where(lax.axis_index("core") == 0, below, above)
+    return lax.ppermute(value, ("y", "core"), pairs)
 
 
 tie = lax.optimization_barrier
 
 
 def spread(chunks, products_of):
-    own, plus, minus = chunks
+    own, plus, minus, up, down = chunks
     p1, m1 = both(plus, minus)
+    up, down = both(up, down, 2)
     pown, pplus, pminus = products_of()
     n1 = jnp.concatenate([own, p1[:2], m1[:2]], axis=0)
-    p1r, m1r, n1, pplus, pminus = tie((p1[2:], m1[2:], n1, pplus, pminus))
-    p2, m2 = both(p1r, m1r)
+    p1 = jnp.concatenate([p1[2:], up], axis=0)
+    m1 = jnp.concatenate([m1[2:], down], axis=0)
+    p1, m1, n1, pplus, pminus = tie((p1, m1, n1, pplus, pminus))
+    p2, m2 = both(p1, m1)
     b1, a1 = round_y(n1)
-    b1, a1, pplus, pminus = tie((b1, a1, pplus, pminus))
-    p3, m3 = both(p2[2:4], m2[2:4])
-    p4, m4 = both(p2[4:], m2[4:], 2)
-    n2 = jnp.concatenate([p2[:2], m2[:2]], axis=0)
-    b2, a2 = round_y(n2)
+    p2, m2, b1, a1, pplus, pminus = tie((p2, m2, b1, a1, pplus, pminus))
+    p3, m3 = both(p2[2:], m2[2:])
     f1 = far_y(b1, a1)
     q1, r1 = both(pplus, pminus)
-    n3 = jnp.concatenate([p3, m3, p4, m4], axis=0)
-    b3, a3 = round_y(n3)
+    n2 = jnp.concatenate([p2[:2], m2[:2], p3[:2], m3[:2], p3[2:], m3[2:]], axis=0)
+    n2, f1 = tie((n2, f1))
+    b2, a2 = round_y(n2)
+    q2, r2 = both(q1[2:], r1[2:])
+    b2, a2, q2, r2 = tie((b2, a2, q2, r2))
     f2 = far_y(b2, a2)
-    q2, r2 = both(q1[2:], r1[2:])
-    b3, a3, q2, r2 = tie((b3, a3, q2, r2))
-    f3 = far_y(b3, a3)
     q3, r3 = both(q2[2:4], r2[2:4])
     q4, r4 = both(q2[4:], r2[4:], 2)
-    m = [n1, b1, a1, *f1, n2, b2, a2, *f2, n3, b3, a3, *f3]
-    return m, [pown, q1, q2, q3, q4, r4, r3, r2, r1]
+    return [n1, b1, a1, f1, n2, b2, a2, f2], [pown, q1, q2, q3, q4, r4, r3, r2, r1]
 
 
 ORDER = [(d, e) for group in GROUPS for e in EORDER for d in group]
@@ -244,8 +245,9 @@
 
 
 def contract_kernel(np_, *refs):
-    products_, arrays, (out_ref, left, right) = refs[:np_], refs[np_:-3], refs[-3:]
-    z = lax.axis_index("z")
+    products_, arrays, (keep_ref, send_ref, left, right) = refs[:np_], refs[np_:-4], refs[-4:]
+    z, c = lax.axis_index("z"), lax.axis_index("core")
+    first = lax.rem(z + c, 2) == 0
     at = 0
     for a in products_:
         for i in range(min(a.shape[0], 2)):
@@ -263,22 +265,24 @@
             acc += lax.dot_general(
                 left[h], right[h, cols, :], (((1,), (1,)), ((), ())), preferred_element_type=F32
             )
-        part = acc.reshape(NZ, LA, TILE).astype(BF16)
-        for d in range(NZ):
-            out_ref[lax.rem(z - d + NZ, NZ), :, cols] = part[d]
+        part = acc.reshape(NZ, LA, TILE)
+        for d in range(0, NZ, 2):
+            at_a, at_b = (lax.rem(z - d - i + NZ, NZ) // 2 for i in range(2))
+            keep_ref[jnp.where(first, at_a, at_b), :, cols] = jnp.where(first, part[d], part[d + 1])
+            send_ref[jnp.where(first, at_b, at_a), :, cols] = jnp.where(first, part[d + 1], part[d])
 
 
 def contract(m, p):
     return pl.pallas_call(
         functools.partial(contract_kernel, len(p)),
-        out_shape=jax.ShapeDtypeStruct((NZ, LA, NZ * NY * LA), BF16),
+        out_shape=(jax.ShapeDtypeStruct((NX, LA, NZ * NY * LA), F32),) * 2,
         in_specs=[VMEM] * (len(p) + len(m)),
-        out_specs=VMEM,
+        out_specs=(VMEM, VMEM),
         scratch_shapes=[
             pltpu.VMEM((2, NZ * LA, HALF), BF16),
             pltpu.VMEM((2, NZ * NY * LA, HALF), BF16),
         ],
-        compiler_params=pltpu.CompilerParams(vmem_limit_bytes=24 * MIB),
+        compiler_params=pltpu.CompilerParams(vmem_limit_bytes=16 * MIB),
         cost_estimate=pl.CostEstimate(
             flops=4 * 320 * 1280 * 1152, bytes_accessed=10**7, transcendentals=0
         ),
@@ -289,7 +293,7 @@
 def pack_kernel(in_ref, out_ref):
     z, y, _ = places()
     total = in_ref[0].astype(F32)
-    for k in range(1, NR):
+    for k in range(1, NX):
         total += in_ref[k].astype(F32)
     for k, (d, e) in enumerate(ORDER):
         part = total[:, k * LA : (k + 1) * LA]
@@ -341,9 +345,10 @@
     m, p = spread(
         prep(pat, basis), lambda: products(pat, green_pattern, basis, green_occ, green_vir)
     )
-    parts = contract(m, p)
-    by_rep = lax.all_to_all(parts, ("x", "core"), split_axis=0, concat_axis=0, tiled=True)
-    by_zy = lax.all_to_all(pack(by_rep), ("z", "y"), split_axis=0, concat_axis=0, tiled=True)
+    keep, send = contract(m, p)
+    parts = (keep + shift(send, 1, "core", NC)).astype(BF16)
+    by_x = lax.all_to_all(parts, "x", split_axis=0, concat_axis=0, tiled=True)
+    by_zy = lax.all_to_all(pack(by_x), ("z", "y"), split_axis=0, concat_axis=0, tiled=True)
     return finish(by_zy)
 
 

time: 143 us -> 135 us (0.944)
  starting transfers between devices: 43.7 us -> 34.6 us
  blocking collectives: 35 us -> 30.7 us
  waiting for transfers between devices: 42 us -> 45.9 us
  local copies, waits for them, and re-layouts: 0.49 us -> 2.25 us
    ppermute x28 -> x21, starting transfers between devices: 43.7 us -> 34.4 us  [shift(): return lax.ppermute(value, axis, [(i, (i + by) % n) for i in range(n)])]
    all_to_all x2, blocking collectives: 35 us -> 30.7 us  [the longest x1 18.8 us: local(): lax.all_to_all(pack(by_x), ('z', 'y'), split_axis=0, concat_axis=0, tiled...]
    ppermute x28 -> x21, waiting for transfers between devices: 42 us -> 43.9 us  [shift(): return lax.ppermute(value, axis, [(i, (i + by) % n) for i in range(n)])]
    ppermute x0 -> x2, waiting for transfers between devices: none -> 1.94 us  [far_y(): return lax.ppermute(value, ('y', 'core'), pairs)]
  transfers between devices with their start and end apart: 28 -> 23, of which waited for: 10 -> 13; matrix products, arithmetic and copies ran while one was open for 0% -> 0% of each run, Pallas kernels for 7% -> 8%
where the time goes in v3:
time: 135 us
  waiting for transfers between devices  45.9 us (34%)
  starting transfers between devices  34.6 us (26%)
  blocking collectives  30.7 us (23%)
  Pallas kernels  20.7 us (15%)
  local copies, waits for them, and re-layouts  2.25 us (2%)
    ppermute x21, waiting for transfers between devices, shift(): return lax.ppermute(value, axis, [(i, (i + by) % n) for i in range(n)])  43.9 us
    ppermute x21, starting transfers between devices, shift(): return lax.ppermute(value, axis, [(i, (i + by) % n) for i in range(n)])  34.4 us
    all_to_all x1, blocking collectives, local(): lax.all_to_all(pack(by_x), ('z', 'y'), split_axis=0, concat_axis=0, tiled...  18.8 us
    all_to_all x1, blocking collectives, local(): by_x = lax.all_to_all(parts, 'x', split_axis=0, concat_axis=0, tiled=True)  11.8 us
    pallas_call x1, Pallas kernels, products(): pl.pallas_call(product_kernel, out_shape=WHOLE, grid=(LA // STEPQ,), in_s...  10.1 us
    pallas_call x1, Pallas kernels, prep(): pl.pallas_call(prep_kernel, out_shape=CHUNKS, in_specs=[SMEM, HBM], out_s...  4.42 us
  transfers between devices with their start and end apart: 23, of which 13 were waited for; matrix products, arithmetic and copies ran while one was open for 0% of the time, Pallas kernels for 8%

profile of v3, /device:TPU:2, one launch (start us, length us, event | category | flops | bytes accessed | tf_op | source)
XLA Modules:
  0.0 134.8 jit_solution(18436939016528824110)
XLA Ops:
  0.0 4.4 %prep.1 = (bf16[2,40,1152]{2,1,0:T(8,128)(2,1)}, bf16[6,40,1152]{2,1,0:T(8,128)(2,1)}, bf16[6,40,1152]{2,1,0:T(8,128)(2,1)}, bf16[1,40,1152]{2,1,0:T(8,128)(2,1)}, bf16[1,40,1152]{2,1,0:T(8,128)(2,1)}) custom-call(s32[6,6,20]{2,1,0:T(8,128)} %bitcast.1, bf16[40,384,384]{2,1,0:T(8,128)(2,1)} %basis_ref.3), custom_call_target="tpu_custom_call" | custom-call | flops 1000000 | bytes 3000000 | tf_op jit(solution)/shard_map/prep/pallas_call | solution.py:97
  4.4 0.0 copy-start.1
  4.4 2.0 %collective-permute-start = (bf16[6,40,1152]{2,1,0:T(8,128)(2,1)}, bf16[6,40,1152]{2,1,0:T(8,128)(2,1)S(1)}, u32[]{:S(2)}, u32[]{:S(2)}) collective-permute-start(bf16[6,40,1152]{2,1,0:T(8,128)(2,1)} %get-tuple-element.33), channel_id=1, source_target_pairs={{0,32},{32,64},{64,96},{96,128},{128,160},{160,192},{192,224},{224... | collective-permute-start | bytes 1658888 | tf_op jit(solution)/shard_map/ppermute | solution.py:187
  6.4 4.0 %collective-permute-start.2 = (bf16[6,40,1152]{2,1,0:T(8,128)(2,1)}, bf16[6,40,1152]{2,1,0:T(8,128)(2,1)S(1)}, u32[]{:S(2)}, u32[]{:S(2)}) collective-permute-start(bf16[6,40,1152]{2,1,0:T(8,128)(2,1)} %get-tuple-element.35), channel_id=1, source_target_pairs={{0,224},{32,0},{64,32},{96,64},{128,96},{160,128},{192,160},{224,1... | collective-permute-start | bytes 1658888 | tf_op jit(solution)/shard_map/ppermute | solution.py:187
  10.5 0.0 collective-permute-start.1
  10.5 4.1 %collective-permute-start.3 = (bf16[1,40,1152]{2,1,0:T(8,128)(2,1)}, bf16[1,40,1152]{2,1,0:T(8,128)(2,1)S(1)}, u32[]{:S(2)}, u32[]{:S(2)}) collective-permute-start(bf16[1,40,1152]{2,1,0:T(8,128)(2,1)} %get-tuple-element.36), channel_id=1, source_target_pairs={{0,192},{32,224},{64,0},{96,32},{128,64},{160,96},{192,128},{224,1... | collective-permute-start | bytes 276488 | tf_op jit(solution)/shard_map/ppermute | solution.py:187
  14.6 10.1 %products.1 = (bf16[2,40,1152]{2,1,0:T(8,128)(2,1)}, bf16[7,40,1152]{2,1,0:T(8,128)(2,1)}, bf16[7,40,1152]{2,1,0:T(8,128)(2,1)}) custom-call(s32[6,6,20]{2,1,0:T(8,128)} %bitcast.2, s32[6,6]{1,0:T(8,128)} %gpat_ref.1, bf16[40,384,384]{2,1,0:T(8,128)(2,1)} %basis_ref.3, bf16[384,384]{1,0:T(8,128)(2,1)} %occ_ref.1, bf16[384,384]{1,0:T(8,128)(2,1)} %vir_ref.1), custom_call_target="tpu_custom_call" | custom-call | flops 1132462080 | bytes 14000000 | tf_op jit(solution)/shard_map/products/pallas_call | solution.py:159
  24.7 0.0 collective-permute-done
  24.8 0.8 collective-permute-done.2
  25.6 0.0 copy-done.1
  25.6 0.1 pad_maximum_fusion.refs_9_
  25.7 1.4 %collective-permute-done.1 = bf16[1,40,1152]{2,1,0:T(8,128)(2,1)S(1)} collective-permute-done((bf16[1,40,1152]{2,1,0:T(8,128)(2,1)}, bf16[1,40,1152]{2,1,0:T(8,128)(2,1)S(1)}, u32[]{:S(2)}, u32[]{:S(2)}) %collective-permute-start.1) | collective-permute-done | bytes 92192 | tf_op jit(solution)/shard_map/ppermute | solution.py:187
  27.1 0.1 pad_maximum_fusion.1
  27.2 0.0 collective-permute-done.3
  27.2 0.1 pad_maximum_fusion.2
  27.3 3.1 %collective-permute-start.7 = (bf16[6,40,1152]{2,1,0:T(8,128)(2,1)S(1)}, bf16[6,40,1152]{2,1,0:T(8,128)(2,1)S(1)}, u32[]{:S(2)}, u32[]{:S(2)}) collective-permute-start(bf16[6,40,1152]{2,1,0:T(8,128)(2,1)S(1)} %pad_maximum_fusion.refs_9_), channel_id=1, source_target_pairs={{0,24},{8,0},{16,8},{24,16},{1,25},{9,1},{17,9},{25,17},{2,26},{10... | collective-permute-start | bytes 1658888 | tf_op jit(solution)/shard_map/ppermute | solution.py:187
  30.4 0.0 collective-permute-start.6
  30.4 0.4 collective-permute-start.4
  30.8 2.8 %collective-permute-start.5 = (bf16[5,40,1152]{2,1,0:T(8,128)(2,1)S(1)}, bf16[5,40,1152]{2,1,0:T(8,128)(2,1)S(1)}, u32[]{:S(2)}, u32[]{:S(2)}) collective-permute-start(bf16[5,40,1152]{2,1,0:T(8,128)(2,1)S(1)} %pad_maximum_fusion.2), channel_id=1, source_target_pairs={{0,224},{32,0},{64,32},{96,64},{128,96},{160,128},{192,160},{224,1... | collective-permute-start | bytes 1382408 | tf_op jit(solution)/shard_map/ppermute | solution.py:187
  33.6 8.7 %collective-permute-done.4 = bf16[5,40,1152]{2,1,0:T(8,128)(2,1)} collective-permute-done((bf16[5,40,1152]{2,1,0:T(8,128)(2,1)S(1)}, bf16[5,40,1152]{2,1,0:T(8,128)(2,1)}, u32[]{:S(2)}, u32[]{:S(2)}) %collective-permute-start.4) | collective-permute-done | bytes 460832 | tf_op jit(solution)/shard_map/ppermute | solution.py:187
  42.4 1.5 %collective-permute-done.5 = bf16[5,40,1152]{2,1,0:T(8,128)(2,1)S(1)} collective-permute-done((bf16[5,40,1152]{2,1,0:T(8,128)(2,1)S(1)}, bf16[5,40,1152]{2,1,0:T(8,128)(2,1)S(1)}, u32[]{:S(2)}, u32[]{:S(2)}) %collective-permute-start.5) | collective-permute-done | bytes 460832 | tf_op jit(solution)/shard_map/ppermute | solution.py:187
  43.9 0.0 collective-permute-done.7.refs_11_
  43.9 0.4 collective-permute-done.6.refs_10_
  44.2 1.0 slice.60
  45.2 0.9 slice_dynamic-update-slice_fusion.3
  46.2 2.7 %collective-permute-start.10 = (bf16[3,40,1152]{2,1,0:T(8,128)(2,1)S(1)}, bf16[3,40,1152]{2,1,0:T(8,128)(2,1)S(1)}, u32[]{:S(2)}, u32[]{:S(2)}) collective-permute-start(bf16[3,40,1152]{2,1,0:T(8,128)(2,1)S(1)} %slice.62), channel_id=1, source_target_pairs={{0,224},{32,0},{64,32},{96,64},{128,96},{160,128},{192,160},{224,1... | collective-permute-start | bytes 829448 | tf_op jit(solution)/shard_map/ppermute | solution.py:187
  48.9 0.0 collective-permute-start.9
  48.9 0.1 broadcast_select_fusion.1
  49.0 0.1 collective-permute-start.11
  49.1 2.6 %collective-permute-start.8 = (bf16[7,40,1152]{2,1,0:T(8,128)(2,1)}, bf16[7,40,1152]{2,1,0:T(8,128)(2,1)S(1)}, u32[]{:S(2)}, u32[]{:S(2)}) collective-permute-start(bf16[7,40,1152]{2,1,0:T(8,128)(2,1)} %get-tuple-element.45), channel_id=1, source_target_pairs={{0,32},{32,64},{64,96},{96,128},{128,160},{160,192},{192,224},{224... | collective-permute-start | bytes 1935368 | tf_op jit(solution)/shard_map/ppermute | solution.py:187
  51.6 0.8 collective-permute-start.15
  52.5 7.2 %collective-permute-done.9 = bf16[3,40,1152]{2,1,0:T(8,128)(2,1)S(1)} collective-permute-done((bf16[3,40,1152]{2,1,0:T(8,128)(2,1)S(1)}, bf16[3,40,1152]{2,1,0:T(8,128)(2,1)S(1)}, u32[]{:S(2)}, u32[]{:S(2)}) %collective-permute-start.9) | collective-permute-done | bytes 276512 | tf_op jit(solution)/shard_map/ppermute | solution.py:187
  59.7 0.0 collective-permute-done.10
  59.7 0.0 collective-permute-done.11.refs_12_
  59.7 1.4 %collective-permute-start.13 = (bf16[10,40,1152]{2,1,0:T(8,128)(2,1)S(1)}, bf16[10,40,1152]{2,1,0:T(8,128)(2,1)S(1)}, u32[]{:S(2)}, u32[]{:S(2)}) collective-permute-start(bf16[10,40,1152]{2,1,0:T(8,128)(2,1)S(1)} %slice_dynamic-update-slice_fusion.4.refs_13_), channel_id=1, source_target_pairs={{0,24},{8,0},{16,8},{24,16},{1,25},{9,1},{17,9},{25,17},{2,26},{10... | collective-permute-start | bytes 2764808 | tf_op jit(solution)/shard_map/ppermute | solution.py:187
  61.2 0.7 collective-permute-start.12
  61.9 8.0 %collective-permute-done.8.refs_1_ = bf16[7,40,1152]{2,1,0:T(8,128)(2,1)S(1)} collective-permute-done((bf16[7,40,1152]{2,1,0:T(8,128)(2,1)}, bf16[7,40,1152]{2,1,0:T(8,128)(2,1)S(1)}, u32[]{:S(2)}, u32[]{:S(2)}) %collective-permute-start.8) | collective-permute-done | bytes 645152 | tf_op jit(solution)/shard_map/ppermute | solution.py:187
  69.9 0.1 collective-permute-start.14
  70.0 0.0 collective-permute-done.15.refs_8_
  70.1 3.3 %collective-permute-start.16 = (bf16[5,40,1152]{2,1,0:T(8,128)(2,1)S(1)}, bf16[5,40,1152]{2,1,0:T(8,128)(2,1)S(1)}, u32[]{:S(2)}, u32[]{:S(2)}) collective-permute-start(bf16[5,40,1152]{2,1,0:T(8,128)(2,1)S(1)} %slice.81), channel_id=1, source_target_pairs={{0,224},{32,0},{64,32},{96,64},{128,96},{160,128},{192,160},{224,1... | collective-permute-start | bytes 1382408 | tf_op jit(solution)/shard_map/ppermute | solution.py:187
  73.3 6.8 %collective-permute-done.14.refs_2_ = bf16[5,40,1152]{2,1,0:T(8,128)(2,1)S(1)} collective-permute-done((bf16[5,40,1152]{2,1,0:T(8,128)(2,1)S(1)}, bf16[5,40,1152]{2,1,0:T(8,128)(2,1)S(1)}, u32[]{:S(2)}, u32[]{:S(2)}) %collective-permute-start.14) | collective-permute-done | bytes 460832 | tf_op jit(solution)/shard_map/ppermute | solution.py:187
  80.2 0.0 collective-permute-done.16.refs_7_
  80.2 0.0 collective-permute-done.13.refs_15_
  80.2 0.4 collective-permute-done.12.refs_14_
  80.6 0.1 broadcast_select_fusion
  80.7 0.1 collective-permute-start.21
  80.8 3.2 %collective-permute-start.20 = (bf16[2,40,1152]{2,1,0:T(8,128)(2,1)S(1)}, bf16[2,40,1152]{2,1,0:T(8,128)(2,1)S(1)}, u32[]{:S(2)}, u32[]{:S(2)}) collective-permute-start(bf16[2,40,1152]{2,1,0:T(8,128)(2,1)S(1)} %slice.71), channel_id=1, source_target_pairs={{0,224},{32,0},{64,32},{96,64},{128,96},{160,128},{192,160},{224,1... | collective-permute-start | bytes 552968 | tf_op jit(solution)/shard_map/ppermute | solution.py:187
  84.1 0.0 collective-permute-start.17
  84.1 1.6 %collective-permute-start.19 = (bf16[1,40,1152]{2,1,0:T(8,128)(2,1)S(1)}, bf16[1,40,1152]{2,1,0:T(8,128)(2,1)S(1)}, u32[]{:S(2)}, u32[]{:S(2)}) collective-permute-start(bf16[1,40,1152]{2,1,0:T(8,128)(2,1)S(1)} %slice.70), channel_id=1, source_target_pairs={{0,192},{32,224},{64,0},{96,32},{128,64},{160,96},{192,128},{224,1... | collective-permute-start | bytes 276488 | tf_op jit(solution)/shard_map/ppermute | solution.py:187
  85.7 1.4 %collective-permute-start.18 = (bf16[1,40,1152]{2,1,0:T(8,128)(2,1)S(1)}, bf16[1,40,1152]{2,1,0:T(8,128)(2,1)S(1)}, u32[]{:S(2)}, u32[]{:S(2)}) collective-permute-start(bf16[1,40,1152]{2,1,0:T(8,128)(2,1)S(1)} %slice.69), channel_id=1, source_target_pairs={{0,64},{32,96},{64,128},{96,160},{128,192},{160,224},{192,0},{224,... | collective-permute-start | bytes 276488 | tf_op jit(solution)/shard_map/ppermute | solution.py:187
  87.1 3.5 %collective-permute-done.19.refs_5_ = bf16[1,40,1152]{2,1,0:T(8,128)(2,1)S(1)} collective-permute-done((bf16[1,40,1152]{2,1,0:T(8,128)(2,1)S(1)}, bf16[1,40,1152]{2,1,0:T(8,128)(2,1)S(1)}, u32[]{:S(2)}, u32[]{:S(2)}) %collective-permute-start.19) | collective-permute-done | bytes 92192 | tf_op jit(solution)/shard_map/ppermute | solution.py:187
  90.6 2.8 %collective-permute-done.18.refs_4_ = bf16[1,40,1152]{2,1,0:T(8,128)(2,1)S(1)} collective-permute-done((bf16[1,40,1152]{2,1,0:T(8,128)(2,1)S(1)}, bf16[1,40,1152]{2,1,0:T(8,128)(2,1)S(1)}, u32[]{:S(2)}, u32[]{:S(2)}) %collective-permute-start.18) | collective-permute-done | bytes 92192 | tf_op jit(solution)/shard_map/ppermute | solution.py:187
  93.5 0.0 collective-permute-done.20.refs_6_
  93.5 0.0 collective-permute-done.17.refs_3_
  93.5 1.9 %collective-permute-done.21.refs_16_ = bf16[10,40,1152]{2,1,0:T(8,128)(2,1)S(1)} collective-permute-done((bf16[10,40,1152]{2,1,0:T(8,128)(2,1)S(1)}, bf16[10,40,1152]{2,1,0:T(8,128)(2,1)S(1)}, u32[]{:S(2)}, u32[]{:S(2)}) %collective-permute-start.21) | collective-permute-done | bytes 921632 | tf_op jit(solution)/shard_map/ppermute | solution.py:209
  95.4 0.0 copy-done
  95.4 2.4 %contract.1 = (f32[4,40,1280]{2,1,0:T(8,128)S(1)}, f32[4,40,1280]{2,1,0:T(8,128)S(1)}) custom-call(bf16[2,40,1152]{2,1,0:T(8,128)(2,1)S(1)} %copy-done, bf16[7,40,1152]{2,1,0:T(8,128)(2,1)S(1)} %collective-permute-done.8.refs_1_, bf16[5,40,1152]{2,1,0:T(8,128)(2,1)S(1)} %collective-permute-done.14.refs_2_, ...), custom_call_target="tpu_custom_call" | custom-call | flops 1887436800 | bytes 10000000 | tf_op jit(solution)/shard_map/contract/pallas_call | solution.py:276
  97.9 0.1 collective-permute-start.22
  98.0 2.3 %collective-permute-done.22 = f32[4,40,1280]{2,1,0:T(8,128)S(1)} collective-permute-done((f32[4,40,1280]{2,1,0:T(8,128)S(1)}, f32[4,40,1280]{2,1,0:T(8,128)S(1)}, u32[]{:S(2)}, u32[]{:S(2)}) %collective-permute-start.22) | collective-permute-done | bytes 819232 | tf_op jit(solution)/shard_map/ppermute | solution.py:187
  100.3 0.1 add_convert_fusion
  100.4 11.8 %all_to_all.10.in_ref = bf16[4,40,1280]{2,1,0:T(8,128)(2,1)} all-to-all(bf16[4,40,1280]{2,1,0:T(8,128)(2,1)S(1)} %add_convert_fusion), channel_id=1, replica_groups=mesh['z'=8,'y'=4,'x'=4,'core'=2] {'x'}, dimensions={0} | all-to-all | bytes 819200 | tf_op jit(solution)/shard_map/all_to_all | solution.py:350
  112.2 2.0 %pack.1 = f32[32,16,128]{2,1,0:T(8,128)} custom-call(bf16[4,40,1280]{2,1,0:T(8,128)(2,1)} %all_to_all.10.in_ref), custom_call_target="tpu_custom_call" | custom-call | tf_op jit(solution)/shard_map/pack/pallas_call | solution.py:309
  114.2 18.8 %all_to_all.11.in_ref = f32[32,16,128]{2,1,0:T(8,128)} all-to-all(f32[32,16,128]{2,1,0:T(8,128)} %pack.1), channel_id=1, replica_groups=mesh['z'=8,'y'=4,'x'=4,'core'=2] {'z','y'}, dimensions={0} | all-to-all | bytes 524288 | tf_op jit(solution)/shard_map/all_to_all | solution.py:351
  133.0 1.7 %finish.1 = f32[40,160]{1,0:T(8,128)} custom-call(f32[32,16,128]{2,1,0:T(8,128)} %all_to_all.11.in_ref), custom_call_target="tpu_custom_call" | custom-call | tf_op jit(solution)/shard_map/finish/pallas_call | solution.py:334
  (17 shorter events, 0.3 us)
Async XLA Ops:
  4.4 21.1 %copy-start.1 = (bf16[2,40,1152]{2,1,0:T(8,128)(2,1)S(1)}, bf16[2,40,1152]{2,1,0:T(8,128)(2,1)}, u32[]{:S(2)}) copy-start(bf16[2,40,1152]{2,1,0:T(8,128)(2,1)} %get-tuple-element.37) | copy-start | bytes 552964
  4.4 20.3 %collective-permute-start = (bf16[6,40,1152]{2,1,0:T(8,128)(2,1)}, bf16[6,40,1152]{2,1,0:T(8,128)(2,1)S(1)}, u32[]{:S(2)}, u32[]{:S(2)}) collective-permute-start(bf16[6,40,1152]{2,1,0:T(8,128)(2,1)} %get-tuple-element.33), channel_id=1, source_target_pairs={{0,32},{32,64},{64,96},{96,128},{128,160},{160,192},{192,224},{224... | collective-permute-start | bytes 1658888 | tf_op jit(solution)/shard_map/ppermute | solution.py:187
  6.4 19.1 %collective-permute-start.2 = (bf16[6,40,1152]{2,1,0:T(8,128)(2,1)}, bf16[6,40,1152]{2,1,0:T(8,128)(2,1)S(1)}, u32[]{:S(2)}, u32[]{:S(2)}) collective-permute-start(bf16[6,40,1152]{2,1,0:T(8,128)(2,1)} %get-tuple-element.35), channel_id=1, source_target_pairs={{0,224},{32,0},{64,32},{96,64},{128,96},{160,128},{192,160},{224,1... | collective-permute-start | bytes 1658888 | tf_op jit(solution)/shard_map/ppermute | solution.py:187
  10.5 16.7 %collective-permute-start.1 = (bf16[1,40,1152]{2,1,0:T(8,128)(2,1)}, bf16[1,40,1152]{2,1,0:T(8,128)(2,1)S(1)}, u32[]{:S(2)}, u32[]{:S(2)}) collective-permute-start(bf16[1,40,1152]{2,1,0:T(8,128)(2,1)} %get-tuple-element.34), channel_id=1, source_target_pairs={{0,64},{32,96},{64,128},{96,160},{128,192},{160,224},{192,0},{224,... | collective-permute-start | bytes 276488 | tf_op jit(solution)/shard_map/ppermute | solution.py:187
  10.5 16.8 %collective-permute-start.3 = (bf16[1,40,1152]{2,1,0:T(8,128)(2,1)}, bf16[1,40,1152]{2,1,0:T(8,128)(2,1)S(1)}, u32[]{:S(2)}, u32[]{:S(2)}) collective-permute-start(bf16[1,40,1152]{2,1,0:T(8,128)(2,1)} %get-tuple-element.36), channel_id=1, source_target_pairs={{0,192},{32,224},{64,0},{96,32},{128,64},{160,96},{192,128},{224,1... | collective-permute-start | bytes 276488 | tf_op jit(solution)/shard_map/ppermute | solution.py:187
  24.7 70.7 %copy-start = (bf16[2,40,1152]{2,1,0:T(8,128)(2,1)S(1)}, bf16[2,40,1152]{2,1,0:T(8,128)(2,1)}, u32[]{:S(2)}) copy-start(bf16[2,40,1152]{2,1,0:T(8,128)(2,1)} %get-tuple-element.32.refs_0_) | copy-start | bytes 552964
  27.3 16.6 %collective-permute-start.7 = (bf16[6,40,1152]{2,1,0:T(8,128)(2,1)S(1)}, bf16[6,40,1152]{2,1,0:T(8,128)(2,1)S(1)}, u32[]{:S(2)}, u32[]{:S(2)}) collective-permute-start(bf16[6,40,1152]{2,1,0:T(8,128)(2,1)S(1)} %pad_maximum_fusion.refs_9_), channel_id=1, source_target_pairs={{0,24},{8,0},{16,8},{24,16},{1,25},{9,1},{17,9},{25,17},{2,26},{10... | collective-permute-start | bytes 1658888 | tf_op jit(solution)/shard_map/ppermute | solution.py:187
  30.4 13.8 %collective-permute-start.6 = (bf16[6,40,1152]{2,1,0:T(8,128)(2,1)S(1)}, bf16[6,40,1152]{2,1,0:T(8,128)(2,1)S(1)}, u32[]{:S(2)}, u32[]{:S(2)}) collective-permute-start(bf16[6,40,1152]{2,1,0:T(8,128)(2,1)S(1)} %pad_maximum_fusion.refs_9_), channel_id=1, source_target_pairs={{0,8},{8,16},{16,24},{24,0},{1,9},{9,17},{17,25},{25,1},{2,10},{10... | collective-permute-start | bytes 1658888 | tf_op jit(solution)/shard_map/ppermute | solution.py:187
  30.4 12.0 %collective-permute-start.4 = (bf16[5,40,1152]{2,1,0:T(8,128)(2,1)S(1)}, bf16[5,40,1152]{2,1,0:T(8,128)(2,1)}, u32[]{:S(2)}, u32[]{:S(2)}) collective-permute-start(bf16[5,40,1152]{2,1,0:T(8,128)(2,1)S(1)} %pad_maximum_fusion.1), channel_id=1, source_target_pairs={{0,32},{32,64},{64,96},{96,128},{128,160},{160,192},{192,224},{224... | collective-permute-start | bytes 1382408 | tf_op jit(solution)/shard_map/ppermute | solution.py:187
  30.8 13.1 %collective-permute-start.5 = (bf16[5,40,1152]{2,1,0:T(8,128)(2,1)S(1)}, bf16[5,40,1152]{2,1,0:T(8,128)(2,1)S(1)}, u32[]{:S(2)}, u32[]{:S(2)}) collective-permute-start(bf16[5,40,1152]{2,1,0:T(8,128)(2,1)S(1)} %pad_maximum_fusion.2), channel_id=1, source_target_pairs={{0,224},{32,0},{64,32},{96,64},{128,96},{160,128},{192,160},{224,1... | collective-permute-start | bytes 1382408 | tf_op jit(solution)/shard_map/ppermute | solution.py:187
  46.2 13.5 %collective-permute-start.10 = (bf16[3,40,1152]{2,1,0:T(8,128)(2,1)S(1)}, bf16[3,40,1152]{2,1,0:T(8,128)(2,1)S(1)}, u32[]{:S(2)}, u32[]{:S(2)}) collective-permute-start(bf16[3,40,1152]{2,1,0:T(8,128)(2,1)S(1)} %slice.62), channel_id=1, source_target_pairs={{0,224},{32,0},{64,32},{96,64},{128,96},{160,128},{192,160},{224,1... | collective-permute-start | bytes 829448 | tf_op jit(solution)/shard_map/ppermute | solution.py:187
  48.9 10.8 %collective-permute-start.9 = (bf16[3,40,1152]{2,1,0:T(8,128)(2,1)S(1)}, bf16[3,40,1152]{2,1,0:T(8,128)(2,1)S(1)}, u32[]{:S(2)}, u32[]{:S(2)}) collective-permute-start(bf16[3,40,1152]{2,1,0:T(8,128)(2,1)S(1)} %slice.60), channel_id=1, source_target_pairs={{0,32},{32,64},{64,96},{96,128},{128,160},{160,192},{192,224},{224... | collective-permute-start | bytes 829448 | tf_op jit(solution)/shard_map/ppermute | solution.py:187
  49.0 10.8 %collective-permute-start.11 = (bf16[6,40,1152]{2,1,0:T(8,128)(2,1)S(1)}, bf16[6,40,1152]{2,1,0:T(8,128)(2,1)S(1)}, u32[]{:S(2)}, u32[]{:S(2)}) collective-permute-start(bf16[6,40,1152]{2,1,0:T(8,128)(2,1)S(1)} %broadcast_select_fusion.1), channel_id=1, source_target_pairs={{0,8},{1,25},{8,16},{9,1},{16,24},{17,9},{24,0},{25,17},{2,10},{3,... | collective-permute-start | bytes 1658888 | tf_op jit(solution)/shard_map/ppermute | solution.py:209
  49.1 20.8 %collective-permute-start.8 = (bf16[7,40,1152]{2,1,0:T(8,128)(2,1)}, bf16[7,40,1152]{2,1,0:T(8,128)(2,1)S(1)}, u32[]{:S(2)}, u32[]{:S(2)}) collective-permute-start(bf16[7,40,1152]{2,1,0:T(8,128)(2,1)} %get-tuple-element.45), channel_id=1, source_target_pairs={{0,32},{32,64},{64,96},{96,128},{128,160},{160,192},{192,224},{224... | collective-permute-start | bytes 1935368 | tf_op jit(solution)/shard_map/ppermute | solution.py:187
  51.6 18.4 %collective-permute-start.15 = (bf16[7,40,1152]{2,1,0:T(8,128)(2,1)}, bf16[7,40,1152]{2,1,0:T(8,128)(2,1)S(1)}, u32[]{:S(2)}, u32[]{:S(2)}) collective-permute-start(bf16[7,40,1152]{2,1,0:T(8,128)(2,1)} %get-tuple-element.51), channel_id=1, source_target_pairs={{0,224},{32,0},{64,32},{96,64},{128,96},{160,128},{192,160},{224,1... | collective-permute-start | bytes 1935368 | tf_op jit(solution)/shard_map/ppermute | solution.py:187
  59.7 20.4 %collective-permute-start.13 = (bf16[10,40,1152]{2,1,0:T(8,128)(2,1)S(1)}, bf16[10,40,1152]{2,1,0:T(8,128)(2,1)S(1)}, u32[]{:S(2)}, u32[]{:S(2)}) collective-permute-start(bf16[10,40,1152]{2,1,0:T(8,128)(2,1)S(1)} %slice_dynamic-update-slice_fusion.4.refs_13_), channel_id=1, source_target_pairs={{0,24},{8,0},{16,8},{24,16},{1,25},{9,1},{17,9},{25,17},{2,26},{10... | collective-permute-start | bytes 2764808 | tf_op jit(solution)/shard_map/ppermute | solution.py:187
  61.2 19.4 %collective-permute-start.12 = (bf16[10,40,1152]{2,1,0:T(8,128)(2,1)S(1)}, bf16[10,40,1152]{2,1,0:T(8,128)(2,1)S(1)}, u32[]{:S(2)}, u32[]{:S(2)}) collective-permute-start(bf16[10,40,1152]{2,1,0:T(8,128)(2,1)S(1)} %slice_dynamic-update-slice_fusion.4.refs_13_), channel_id=1, source_target_pairs={{0,8},{8,16},{16,24},{24,0},{1,9},{9,17},{17,25},{25,1},{2,10},{10... | collective-permute-start | bytes 2764808 | tf_op jit(solution)/shard_map/ppermute | solution.py:187
  69.9 10.3 %collective-permute-start.14 = (bf16[5,40,1152]{2,1,0:T(8,128)(2,1)S(1)}, bf16[5,40,1152]{2,1,0:T(8,128)(2,1)S(1)}, u32[]{:S(2)}, u32[]{:S(2)}) collective-permute-start(bf16[5,40,1152]{2,1,0:T(8,128)(2,1)S(1)} %slice.80), channel_id=1, source_target_pairs={{0,32},{32,64},{64,96},{96,128},{128,160},{160,192},{192,224},{224... | collective-permute-start | bytes 1382408 | tf_op jit(solution)/shard_map/ppermute | solution.py:187
  70.1 10.1 %collective-permute-start.16 = (bf16[5,40,1152]{2,1,0:T(8,128)(2,1)S(1)}, bf16[5,40,1152]{2,1,0:T(8,128)(2,1)S(1)}, u32[]{:S(2)}, u32[]{:S(2)}) collective-permute-start(bf16[5,40,1152]{2,1,0:T(8,128)(2,1)S(1)} %slice.81), channel_id=1, source_target_pairs={{0,224},{32,0},{64,32},{96,64},{128,96},{160,128},{192,160},{224,1... | collective-permute-start | bytes 1382408 | tf_op jit(solution)/shard_map/ppermute | solution.py:187
  80.7 14.7 %collective-permute-start.21 = (bf16[10,40,1152]{2,1,0:T(8,128)(2,1)S(1)}, bf16[10,40,1152]{2,1,0:T(8,128)(2,1)S(1)}, u32[]{:S(2)}, u32[]{:S(2)}) collective-permute-start(bf16[10,40,1152]{2,1,0:T(8,128)(2,1)S(1)} %broadcast_select_fusion), channel_id=1, source_target_pairs={{0,8},{1,25},{8,16},{9,1},{16,24},{17,9},{24,0},{25,17},{2,10},{3,... | collective-permute-start | bytes 2764808 | tf_op jit(solution)/shard_map/ppermute | solution.py:209
  80.8 12.7 %collective-permute-start.20 = (bf16[2,40,1152]{2,1,0:T(8,128)(2,1)S(1)}, bf16[2,40,1152]{2,1,0:T(8,128)(2,1)S(1)}, u32[]{:S(2)}, u32[]{:S(2)}) collective-permute-start(bf16[2,40,1152]{2,1,0:T(8,128)(2,1)S(1)} %slice.71), channel_id=1, source_target_pairs={{0,224},{32,0},{64,32},{96,64},{128,96},{160,128},{192,160},{224,1... | collective-permute-start | bytes 552968 | tf_op jit(solution)/shard_map/ppermute | solution.py:187
  84.1 9.4 %collective-permute-start.17 = (bf16[2,40,1152]{2,1,0:T(8,128)(2,1)S(1)}, bf16[2,40,1152]{2,1,0:T(8,128)(2,1)S(1)}, u32[]{:S(2)}, u32[]{:S(2)}) collective-permute-start(bf16[2,40,1152]{2,1,0:T(8,128)(2,1)S(1)} %slice.68), channel_id=1, source_target_pairs={{0,32},{32,64},{64,96},{96,128},{128,160},{160,192},{192,224},{224... | collective-permute-start | bytes 552968 | tf_op jit(solution)/shard_map/ppermute | solution.py:187
  84.1 6.5 %collective-permute-start.19 = (bf16[1,40,1152]{2,1,0:T(8,128)(2,1)S(1)}, bf16[1,40,1152]{2,1,0:T(8,128)(2,1)S(1)}, u32[]{:S(2)}, u32[]{:S(2)}) collective-permute-start(bf16[1,40,1152]{2,1,0:T(8,128)(2,1)S(1)} %slice.70), channel_id=1, source_target_pairs={{0,192},{32,224},{64,0},{96,32},{128,64},{160,96},{192,128},{224,1... | collective-permute-start | bytes 276488 | tf_op jit(solution)/shard_map/ppermute | solution.py:187
  85.7 7.8 %collective-permute-start.18 = (bf16[1,40,1152]{2,1,0:T(8,128)(2,1)S(1)}, bf16[1,40,1152]{2,1,0:T(8,128)(2,1)S(1)}, u32[]{:S(2)}, u32[]{:S(2)}) collective-permute-start(bf16[1,40,1152]{2,1,0:T(8,128)(2,1)S(1)} %slice.69), channel_id=1, source_target_pairs={{0,64},{32,96},{64,128},{96,160},{128,192},{160,224},{192,0},{224,... | collective-permute-start | bytes 276488 | tf_op jit(solution)/shard_map/ppermute | solution.py:187
  97.9 2.4 %collective-permute-start.22 = (f32[4,40,1280]{2,1,0:T(8,128)S(1)}, f32[4,40,1280]{2,1,0:T(8,128)S(1)}, u32[]{:S(2)}, u32[]{:S(2)}) collective-permute-start(f32[4,40,1280]{2,1,0:T(8,128)S(1)} %get-tuple-element.58), channel_id=1, source_target_pairs={{0,1},{1,0},{2,3},{3,2},{4,5},{5,4},{6,7},{7,6},{8,9},{9,8},{10,11... | collective-permute-start | bytes 2457608 | tf_op jit(solution)/shard_map/ppermute | solution.py:187

commit v4 on v3

--- a/solution.py
+++ b/solution.py
@@ -217,19 +217,20 @@
     p1, m1 = both(plus, minus)
     up, down = both(up, down, 2)
     pown, pplus, pminus = products_of()
-    n1 = jnp.concatenate([own, p1[:2], m1[:2]], axis=0)
+    n1, k1 = p1[:2], m1[:2]
     p1 = jnp.concatenate([p1[2:], up], axis=0)
     m1 = jnp.concatenate([m1[2:], down], axis=0)
-    p1, m1, n1, pplus, pminus = tie((p1, m1, n1, pplus, pminus))
+    p1, m1, own, n1, k1, pplus, pminus = tie((p1, m1, own, n1, k1, pplus, pminus))
+    n1 = jnp.concatenate([own, n1, k1], axis=0)
     p2, m2 = both(p1, m1)
     b1, a1 = round_y(n1)
-    p2, m2, b1, a1, pplus, pminus = tie((p2, m2, b1, a1, pplus, pminus))
+    p2, m2, pplus, pminus = tie((p2, m2, pplus, pminus))
     p3, m3 = both(p2[2:], m2[2:])
     f1 = far_y(b1, a1)
     q1, r1 = both(pplus, pminus)
     n2 = jnp.concatenate([p2[:2], m2[:2], p3[:2], m3[:2], p3[2:], m3[2:]], axis=0)
-    n2, f1 = tie((n2, f1))
     b2, a2 = round_y(n2)
+    q1, r1, f1 = tie((q1, r1, f1))
     q2, r2 = both(q1[2:], r1[2:])
     b2, a2, q2, r2 = tie((b2, a2, q2, r2))
     f2 = far_y(b2, a2)

time: 135 us -> 131 us (0.970)
  local copies, waits for them, and re-layouts: 2.25 us -> 0.44 us
  blocking collectives: 30.7 us -> 29.2 us
    ppermute x21, waiting for transfers between devices: 43.9 us -> 35.4 us  [shift(): return lax.ppermute(value, axis, [(i, (i + by) % n) for i in range(n)])]
    ppermute x2, waiting for transfers between devices: 1.94 us -> 9.83 us  [far_y(): return lax.ppermute(value, ('y', 'core'), pairs)]
    all_to_all x1, blocking collectives: 18.8 us -> 17.4 us  [local(): lax.all_to_all(pack(by_x), ('z', 'y'), split_axis=0, concat_axis=0, tiled...]
    ppermute x21, starting transfers between devices: 34.4 us -> 33 us  [shift(): return lax.ppermute(value, axis, [(i, (i + by) % n) for i in range(n)])]
  transfers between devices with their start and end apart: 23 -> 23, of which waited for: 13 -> 14; matrix products, arithmetic and copies ran while one was open for 0% -> 0% of each run, Pallas kernels for 8% -> 8%
where the time goes in v4:
time: 131 us; the launch traced here: 130 us
  waiting for transfers between devices  45.2 us (35%)
  starting transfers between devices  34.3 us (26%)
  blocking collectives  29.2 us (22%)
  Pallas kernels  20.6 us (16%)
    ppermute x21, waiting for transfers between devices, shift(): return lax.ppermute(value, axis, [(i, (i + by) % n) for i in range(n)])  35.4 us
    ppermute x21, starting transfers between devices, shift(): return lax.ppermute(value, axis, [(i, (i + by) % n) for i in range(n)])  33 us
    all_to_all x1, blocking collectives, local(): lax.all_to_all(pack(by_x), ('z', 'y'), split_axis=0, concat_axis=0, tiled...  17.4 us
    all_to_all x1, blocking collectives, local(): by_x = lax.all_to_all(parts, 'x', split_axis=0, concat_axis=0, tiled=True)  11.8 us
    pallas_call x1, Pallas kernels, products(): pl.pallas_call(product_kernel, out_shape=WHOLE, grid=(LA // STEPQ,), in_s...  10.1 us
    ppermute x2, waiting for transfers between devices, far_y(): return lax.ppermute(value, ('y', 'core'), pairs)  9.83 us
    pallas_call x1, Pallas kernels, prep(): pl.pallas_call(prep_kernel, out_shape=CHUNKS, in_specs=[SMEM, HBM], out_s...  4.42 us
  transfers between devices with their start and end apart: 23, of which 14 were waited for; matrix products, arithmetic and copies ran while one was open for 0% of the time, Pallas kernels for 8%

profile of v4, /device:TPU:2, one launch (start us, length us, event | category | flops | bytes accessed | tf_op | source)
XLA Modules:
  0.0 130.4 jit_solution(9218315531482997658)
XLA Ops:
  0.0 4.4 %prep.1 = (bf16[2,40,1152]{2,1,0:T(8,128)(2,1)}, bf16[6,40,1152]{2,1,0:T(8,128)(2,1)}, bf16[6,40,1152]{2,1,0:T(8,128)(2,1)}, bf16[1,40,1152]{2,1,0:T(8,128)(2,1)}, bf16[1,40,1152]{2,1,0:T(8,128)(2,1)}) custom-call(s32[6,6,20]{2,1,0:T(8,128)} %bitcast.1, bf16[40,384,384]{2,1,0:T(8,128)(2,1)} %basis_ref.3), custom_call_target="tpu_custom_call" | custom-call | flops 1000000 | bytes 3000000 | tf_op jit(solution)/shard_map/prep/pallas_call | solution.py:97
  4.4 0.0 copy-start.1
  4.4 2.0 %collective-permute-start = (bf16[6,40,1152]{2,1,0:T(8,128)(2,1)}, bf16[6,40,1152]{2,1,0:T(8,128)(2,1)S(1)}, u32[]{:S(2)}, u32[]{:S(2)}) collective-permute-start(bf16[6,40,1152]{2,1,0:T(8,128)(2,1)} %get-tuple-element.34), channel_id=1, source_target_pairs={{0,32},{32,64},{64,96},{96,128},{128,160},{160,192},{192,224},{224... | collective-permute-start | bytes 1658888 | tf_op jit(solution)/shard_map/ppermute | solution.py:187
  6.4 4.0 %collective-permute-start.2 = (bf16[6,40,1152]{2,1,0:T(8,128)(2,1)}, bf16[6,40,1152]{2,1,0:T(8,128)(2,1)S(1)}, u32[]{:S(2)}, u32[]{:S(2)}) collective-permute-start(bf16[6,40,1152]{2,1,0:T(8,128)(2,1)} %get-tuple-element.36), channel_id=1, source_target_pairs={{0,224},{32,0},{64,32},{96,64},{128,96},{160,128},{192,160},{224,1... | collective-permute-start | bytes 1658888 | tf_op jit(solution)/shard_map/ppermute | solution.py:187
  10.5 0.0 collective-permute-start.1
  10.5 4.1 %collective-permute-start.3 = (bf16[1,40,1152]{2,1,0:T(8,128)(2,1)}, bf16[1,40,1152]{2,1,0:T(8,128)(2,1)S(1)}, u32[]{:S(2)}, u32[]{:S(2)}) collective-permute-start(bf16[1,40,1152]{2,1,0:T(8,128)(2,1)} %get-tuple-element.37), channel_id=1, source_target_pairs={{0,192},{32,224},{64,0},{96,32},{128,64},{160,96},{192,128},{224,1... | collective-permute-start | bytes 276488 | tf_op jit(solution)/shard_map/ppermute | solution.py:187
  14.6 10.1 %products.1 = (bf16[2,40,1152]{2,1,0:T(8,128)(2,1)}, bf16[7,40,1152]{2,1,0:T(8,128)(2,1)}, bf16[7,40,1152]{2,1,0:T(8,128)(2,1)}) custom-call(s32[6,6,20]{2,1,0:T(8,128)} %bitcast.2, s32[6,6]{1,0:T(8,128)} %gpat_ref.1, bf16[40,384,384]{2,1,0:T(8,128)(2,1)} %basis_ref.3, bf16[384,384]{1,0:T(8,128)(2,1)} %occ_ref.1, bf16[384,384]{1,0:T(8,128)(2,1)} %vir_ref.1), custom_call_target="tpu_custom_call" | custom-call | flops 1132462080 | bytes 14000000 | tf_op jit(solution)/shard_map/products/pallas_call | solution.py:159
  24.7 0.0 copy-start
  24.7 0.0 collective-permute-done
  24.7 2.4 %collective-permute-done.1 = bf16[1,40,1152]{2,1,0:T(8,128)(2,1)S(1)} collective-permute-done((bf16[1,40,1152]{2,1,0:T(8,128)(2,1)}, bf16[1,40,1152]{2,1,0:T(8,128)(2,1)S(1)}, u32[]{:S(2)}, u32[]{:S(2)}) %collective-permute-start.1) | collective-permute-done | bytes 92192 | tf_op jit(solution)/shard_map/ppermute | solution.py:187
  27.1 0.1 pad_maximum_fusion
  27.2 0.0 collective-permute-done.2
  27.3 0.0 collective-permute-done.3
  27.3 0.1 pad_maximum_fusion.1
  27.4 0.5 collective-permute-start.4
  27.9 2.8 %collective-permute-start.5 = (bf16[5,40,1152]{2,1,0:T(8,128)(2,1)S(1)}, bf16[5,40,1152]{2,1,0:T(8,128)(2,1)S(1)}, u32[]{:S(2)}, u32[]{:S(2)}) collective-permute-start(bf16[5,40,1152]{2,1,0:T(8,128)(2,1)S(1)} %pad_maximum_fusion.1), channel_id=1, source_target_pairs={{0,224},{32,0},{64,32},{96,64},{128,96},{160,128},{192,160},{224,1... | collective-permute-start | bytes 1382408 | tf_op jit(solution)/shard_map/ppermute | solution.py:187
  30.7 0.0 copy-done.1
  30.8 3.1 %collective-permute-start.9 = (bf16[6,40,1152]{2,1,0:T(8,128)(2,1)S(1)}, bf16[6,40,1152]{2,1,0:T(8,128)(2,1)S(1)}, u32[]{:S(2)}, u32[]{:S(2)}) collective-permute-start(bf16[6,40,1152]{2,1,0:T(8,128)(2,1)S(1)} %constant_dynamic-update-slice_fusion.refs_9_), channel_id=1, source_target_pairs={{0,24},{8,0},{16,8},{24,16},{1,25},{9,1},{17,9},{25,17},{2,26},{10... | collective-permute-start | bytes 1658888 | tf_op jit(solution)/shard_map/ppermute | solution.py:187
  33.8 0.0 collective-permute-start.8
  33.8 5.7 %collective-permute-done.4 = bf16[5,40,1152]{2,1,0:T(8,128)(2,1)S(1)} collective-permute-done((bf16[5,40,1152]{2,1,0:T(8,128)(2,1)S(1)}, bf16[5,40,1152]{2,1,0:T(8,128)(2,1)S(1)}, u32[]{:S(2)}, u32[]{:S(2)}) %collective-permute-start.4) | collective-permute-done | bytes 460832 | tf_op jit(solution)/shard_map/ppermute | solution.py:187
  39.6 1.6 %collective-permute-done.5 = bf16[5,40,1152]{2,1,0:T(8,128)(2,1)S(1)} collective-permute-done((bf16[5,40,1152]{2,1,0:T(8,128)(2,1)S(1)}, bf16[5,40,1152]{2,1,0:T(8,128)(2,1)S(1)}, u32[]{:S(2)}, u32[]{:S(2)}) %collective-permute-start.5) | collective-permute-done | bytes 460832 | tf_op jit(solution)/shard_map/ppermute | solution.py:187
  41.2 1.5 %collective-permute-start.12 = (bf16[3,40,1152]{2,1,0:T(8,128)(2,1)S(1)}, bf16[3,40,1152]{2,1,0:T(8,128)(2,1)S(1)}, u32[]{:S(2)}, u32[]{:S(2)}) collective-permute-start(bf16[3,40,1152]{2,1,0:T(8,128)(2,1)S(1)} %slice.62), channel_id=1, source_target_pairs={{0,224},{32,0},{64,32},{96,64},{128,96},{160,128},{192,160},{224,1... | collective-permute-start | bytes 829448 | tf_op jit(solution)/shard_map/ppermute | solution.py:187
  42.7 0.6 collective-permute-start.11
  43.3 1.8 %collective-permute-start.6 = (bf16[7,40,1152]{2,1,0:T(8,128)(2,1)}, bf16[7,40,1152]{2,1,0:T(8,128)(2,1)S(1)}, u32[]{:S(2)}, u32[]{:S(2)}) collective-permute-start(bf16[7,40,1152]{2,1,0:T(8,128)(2,1)} %get-tuple-element.45), channel_id=1, source_target_pairs={{0,32},{32,64},{64,96},{96,128},{128,160},{160,192},{192,224},{224... | collective-permute-start | bytes 1935368 | tf_op jit(solution)/shard_map/ppermute | solution.py:187
  45.1 0.0 collective-permute-done.9.refs_11_
  45.1 1.6 %collective-permute-start.7 = (bf16[7,40,1152]{2,1,0:T(8,128)(2,1)}, bf16[7,40,1152]{2,1,0:T(8,128)(2,1)S(1)}, u32[]{:S(2)}, u32[]{:S(2)}) collective-permute-start(bf16[7,40,1152]{2,1,0:T(8,128)(2,1)} %get-tuple-element.46), channel_id=1, source_target_pairs={{0,224},{32,0},{64,32},{96,64},{128,96},{160,128},{192,160},{224,1... | collective-permute-start | bytes 1935368 | tf_op jit(solution)/shard_map/ppermute | solution.py:187
  46.7 0.4 collective-permute-done.8.refs_10_
  47.1 0.1 broadcast_select_fusion.1
  47.2 1.2 collective-permute-start.10
  48.4 5.0 %collective-permute-done.11 = bf16[3,40,1152]{2,1,0:T(8,128)(2,1)S(1)} collective-permute-done((bf16[3,40,1152]{2,1,0:T(8,128)(2,1)S(1)}, bf16[3,40,1152]{2,1,0:T(8,128)(2,1)S(1)}, u32[]{:S(2)}, u32[]{:S(2)}) %collective-permute-start.11) | collective-permute-done | bytes 276512 | tf_op jit(solution)/shard_map/ppermute | solution.py:187
  53.5 0.0 collective-permute-done.12
  53.5 3.1 %collective-permute-start.14 = (bf16[10,40,1152]{2,1,0:T(8,128)(2,1)S(1)}, bf16[10,40,1152]{2,1,0:T(8,128)(2,1)S(1)}, u32[]{:S(2)}, u32[]{:S(2)}) collective-permute-start(bf16[10,40,1152]{2,1,0:T(8,128)(2,1)S(1)} %slice_dynamic-update-slice_fusion.4.refs_13_), channel_id=1, source_target_pairs={{0,24},{8,0},{16,8},{24,16},{1,25},{9,1},{17,9},{25,17},{2,26},{10... | collective-permute-start | bytes 2764808 | tf_op jit(solution)/shard_map/ppermute | solution.py:187
  56.6 0.0 collective-permute-start.13
  56.6 6.3 %collective-permute-done.10.refs_12_ = bf16[6,40,1152]{2,1,0:T(8,128)(2,1)S(1)} collective-permute-done((bf16[6,40,1152]{2,1,0:T(8,128)(2,1)S(1)}, bf16[6,40,1152]{2,1,0:T(8,128)(2,1)S(1)}, u32[]{:S(2)}, u32[]{:S(2)}) %collective-permute-start.10) | collective-permute-done | bytes 552992 | tf_op jit(solution)/shard_map/ppermute | solution.py:209
  63.0 0.2 collective-permute-done.6.refs_1_
  63.2 0.0 collective-permute-done.7.refs_8_
  63.3 2.3 %collective-permute-start.16 = (bf16[5,40,1152]{2,1,0:T(8,128)(2,1)S(1)}, bf16[5,40,1152]{2,1,0:T(8,128)(2,1)S(1)}, u32[]{:S(2)}, u32[]{:S(2)}) collective-permute-start(bf16[5,40,1152]{2,1,0:T(8,128)(2,1)S(1)} %slice.67), channel_id=1, source_target_pairs={{0,224},{32,0},{64,32},{96,64},{128,96},{160,128},{192,160},{224,1... | collective-permute-start | bytes 1382408 | tf_op jit(solution)/shard_map/ppermute | solution.py:187
  65.6 0.4 collective-permute-start.15
  66.0 6.4 %collective-permute-done.16.refs_7_ = bf16[5,40,1152]{2,1,0:T(8,128)(2,1)S(1)} collective-permute-done((bf16[5,40,1152]{2,1,0:T(8,128)(2,1)S(1)}, bf16[5,40,1152]{2,1,0:T(8,128)(2,1)S(1)}, u32[]{:S(2)}, u32[]{:S(2)}) %collective-permute-start.16) | collective-permute-done | bytes 460832 | tf_op jit(solution)/shard_map/ppermute | solution.py:187
  72.4 2.9 %collective-permute-done.15.refs_2_ = bf16[5,40,1152]{2,1,0:T(8,128)(2,1)S(1)} collective-permute-done((bf16[5,40,1152]{2,1,0:T(8,128)(2,1)S(1)}, bf16[5,40,1152]{2,1,0:T(8,128)(2,1)S(1)}, u32[]{:S(2)}, u32[]{:S(2)}) %collective-permute-start.15) | collective-permute-done | bytes 460832 | tf_op jit(solution)/shard_map/ppermute | solution.py:187
  75.3 0.0 collective-permute-done.14.refs_15_
  75.3 2.4 %collective-permute-done.13.refs_14_ = bf16[10,40,1152]{2,1,0:T(8,128)(2,1)S(1)} collective-permute-done((bf16[10,40,1152]{2,1,0:T(8,128)(2,1)S(1)}, bf16[10,40,1152]{2,1,0:T(8,128)(2,1)S(1)}, u32[]{:S(2)}, u32[]{:S(2)}) %collective-permute-start.13) | collective-permute-done | bytes 921632 | tf_op jit(solution)/shard_map/ppermute | solution.py:187
  77.7 0.1 broadcast_select_fusion
  77.8 0.1 collective-permute-start.21
  78.0 1.2 collective-permute-start.20
  79.2 0.9 collective-permute-start.17
  80.1 1.8 %collective-permute-start.19 = (bf16[1,40,1152]{2,1,0:T(8,128)(2,1)S(1)}, bf16[1,40,1152]{2,1,0:T(8,128)(2,1)S(1)}, u32[]{:S(2)}, u32[]{:S(2)}) collective-permute-start(bf16[1,40,1152]{2,1,0:T(8,128)(2,1)S(1)} %slice.70), channel_id=1, source_target_pairs={{0,192},{32,224},{64,0},{96,32},{128,64},{160,96},{192,128},{224,1... | collective-permute-start | bytes 276488 | tf_op jit(solution)/shard_map/ppermute | solution.py:187
  81.9 1.2 collective-permute-start.18
  83.1 3.6 %collective-permute-done.19.refs_5_ = bf16[1,40,1152]{2,1,0:T(8,128)(2,1)S(1)} collective-permute-done((bf16[1,40,1152]{2,1,0:T(8,128)(2,1)S(1)}, bf16[1,40,1152]{2,1,0:T(8,128)(2,1)S(1)}, u32[]{:S(2)}, u32[]{:S(2)}) %collective-permute-start.19) | collective-permute-done | bytes 92192 | tf_op jit(solution)/shard_map/ppermute | solution.py:187
  86.7 2.3 %collective-permute-done.18.refs_4_ = bf16[1,40,1152]{2,1,0:T(8,128)(2,1)S(1)} collective-permute-done((bf16[1,40,1152]{2,1,0:T(8,128)(2,1)S(1)}, bf16[1,40,1152]{2,1,0:T(8,128)(2,1)S(1)}, u32[]{:S(2)}, u32[]{:S(2)}) %collective-permute-start.18) | collective-permute-done | bytes 92192 | tf_op jit(solution)/shard_map/ppermute | solution.py:187
  89.1 0.0 collective-permute-done.20.refs_6_
  89.1 0.0 collective-permute-done.17.refs_3_
  89.1 3.5 %collective-permute-done.21.refs_16_ = bf16[10,40,1152]{2,1,0:T(8,128)(2,1)S(1)} collective-permute-done((bf16[10,40,1152]{2,1,0:T(8,128)(2,1)S(1)}, bf16[10,40,1152]{2,1,0:T(8,128)(2,1)S(1)}, u32[]{:S(2)}, u32[]{:S(2)}) %collective-permute-start.21) | collective-permute-done | bytes 921632 | tf_op jit(solution)/shard_map/ppermute | solution.py:209
  92.6 0.0 copy-done
  92.6 2.4 %contract.1 = (f32[4,40,1280]{2,1,0:T(8,128)S(1)}, f32[4,40,1280]{2,1,0:T(8,128)S(1)}) custom-call(bf16[2,40,1152]{2,1,0:T(8,128)(2,1)S(1)} %copy-done, bf16[7,40,1152]{2,1,0:T(8,128)(2,1)S(1)} %collective-permute-done.6.refs_1_, bf16[5,40,1152]{2,1,0:T(8,128)(2,1)S(1)} %collective-permute-done.15.refs_2_, ...), custom_call_target="tpu_custom_call" | custom-call | flops 1887436800 | bytes 10000000 | tf_op jit(solution)/shard_map/contract/pallas_call | solution.py:277
  95.0 0.1 collective-permute-start.22
  95.1 2.3 %collective-permute-done.22 = f32[4,40,1280]{2,1,0:T(8,128)S(1)} collective-permute-done((f32[4,40,1280]{2,1,0:T(8,128)S(1)}, f32[4,40,1280]{2,1,0:T(8,128)S(1)}, u32[]{:S(2)}, u32[]{:S(2)}) %collective-permute-start.22) | collective-permute-done | bytes 819232 | tf_op jit(solution)/shard_map/ppermute | solution.py:187
  97.4 0.1 add_convert_fusion
  97.5 11.8 %all_to_all.10.in_ref = bf16[4,40,1280]{2,1,0:T(8,128)(2,1)} all-to-all(bf16[4,40,1280]{2,1,0:T(8,128)(2,1)S(1)} %add_convert_fusion), channel_id=1, replica_groups=mesh['z'=8,'y'=4,'x'=4,'core'=2] {'x'}, dimensions={0} | all-to-all | bytes 819200 | tf_op jit(solution)/shard_map/all_to_all | solution.py:351
  109.3 2.0 %pack.1 = f32[32,16,128]{2,1,0:T(8,128)} custom-call(bf16[4,40,1280]{2,1,0:T(8,128)(2,1)} %all_to_all.10.in_ref), custom_call_target="tpu_custom_call" | custom-call | tf_op jit(solution)/shard_map/pack/pallas_call | solution.py:310
  111.3 17.4 %all_to_all.11.in_ref = f32[32,16,128]{2,1,0:T(8,128)} all-to-all(f32[32,16,128]{2,1,0:T(8,128)} %pack.1), channel_id=1, replica_groups=mesh['z'=8,'y'=4,'x'=4,'core'=2] {'z','y'}, dimensions={0} | all-to-all | bytes 524288 | tf_op jit(solution)/shard_map/all_to_all | solution.py:352
  128.7 1.7 %finish.1 = f32[40,160]{1,0:T(8,128)} custom-call(f32[32,16,128]{2,1,0:T(8,128)} %all_to_all.11.in_ref), custom_call_target="tpu_custom_call" | custom-call | tf_op jit(solution)/shard_map/finish/pallas_call | solution.py:335
  (21 shorter events, 0.4 us)
Async XLA Ops:
  4.4 26.2 %copy-start.1 = (bf16[2,40,1152]{2,1,0:T(8,128)(2,1)S(1)}, bf16[2,40,1152]{2,1,0:T(8,128)(2,1)}, u32[]{:S(2)}) copy-start(bf16[2,40,1152]{2,1,0:T(8,128)(2,1)} %get-tuple-element.47) | copy-start | bytes 552964
  4.4 20.3 %collective-permute-start = (bf16[6,40,1152]{2,1,0:T(8,128)(2,1)}, bf16[6,40,1152]{2,1,0:T(8,128)(2,1)S(1)}, u32[]{:S(2)}, u32[]{:S(2)}) collective-permute-start(bf16[6,40,1152]{2,1,0:T(8,128)(2,1)} %get-tuple-element.34), channel_id=1, source_target_pairs={{0,32},{32,64},{64,96},{96,128},{128,160},{160,192},{192,224},{224... | collective-permute-start | bytes 1658888 | tf_op jit(solution)/shard_map/ppermute | solution.py:187
  6.4 20.8 %collective-permute-start.2 = (bf16[6,40,1152]{2,1,0:T(8,128)(2,1)}, bf16[6,40,1152]{2,1,0:T(8,128)(2,1)S(1)}, u32[]{:S(2)}, u32[]{:S(2)}) collective-permute-start(bf16[6,40,1152]{2,1,0:T(8,128)(2,1)} %get-tuple-element.36), channel_id=1, source_target_pairs={{0,224},{32,0},{64,32},{96,64},{128,96},{160,128},{192,160},{224,1... | collective-permute-start | bytes 1658888 | tf_op jit(solution)/shard_map/ppermute | solution.py:187
  10.5 16.7 %collective-permute-start.1 = (bf16[1,40,1152]{2,1,0:T(8,128)(2,1)}, bf16[1,40,1152]{2,1,0:T(8,128)(2,1)S(1)}, u32[]{:S(2)}, u32[]{:S(2)}) collective-permute-start(bf16[1,40,1152]{2,1,0:T(8,128)(2,1)} %get-tuple-element.35), channel_id=1, source_target_pairs={{0,64},{32,96},{64,128},{96,160},{128,192},{160,224},{192,0},{224,... | collective-permute-start | bytes 276488 | tf_op jit(solution)/shard_map/ppermute | solution.py:187
  10.5 16.8 %collective-permute-start.3 = (bf16[1,40,1152]{2,1,0:T(8,128)(2,1)}, bf16[1,40,1152]{2,1,0:T(8,128)(2,1)S(1)}, u32[]{:S(2)}, u32[]{:S(2)}) collective-permute-start(bf16[1,40,1152]{2,1,0:T(8,128)(2,1)} %get-tuple-element.37), channel_id=1, source_target_pairs={{0,192},{32,224},{64,0},{96,32},{128,64},{160,96},{192,128},{224,1... | collective-permute-start | bytes 276488 | tf_op jit(solution)/shard_map/ppermute | solution.py:187
  24.7 67.9 %copy-start = (bf16[2,40,1152]{2,1,0:T(8,128)(2,1)S(1)}, bf16[2,40,1152]{2,1,0:T(8,128)(2,1)}, u32[]{:S(2)}) copy-start(bf16[2,40,1152]{2,1,0:T(8,128)(2,1)} %get-tuple-element.33.refs_0_) | copy-start | bytes 552964
  27.4 12.2 %collective-permute-start.4 = (bf16[5,40,1152]{2,1,0:T(8,128)(2,1)S(1)}, bf16[5,40,1152]{2,1,0:T(8,128)(2,1)S(1)}, u32[]{:S(2)}, u32[]{:S(2)}) collective-permute-start(bf16[5,40,1152]{2,1,0:T(8,128)(2,1)S(1)} %pad_maximum_fusion), channel_id=1, source_target_pairs={{0,32},{32,64},{64,96},{96,128},{128,160},{160,192},{192,224},{224... | collective-permute-start | bytes 1382408 | tf_op jit(solution)/shard_map/ppermute | solution.py:187
  27.9 13.3 %collective-permute-start.5 = (bf16[5,40,1152]{2,1,0:T(8,128)(2,1)S(1)}, bf16[5,40,1152]{2,1,0:T(8,128)(2,1)S(1)}, u32[]{:S(2)}, u32[]{:S(2)}) collective-permute-start(bf16[5,40,1152]{2,1,0:T(8,128)(2,1)S(1)} %pad_maximum_fusion.1), channel_id=1, source_target_pairs={{0,224},{32,0},{64,32},{96,64},{128,96},{160,128},{192,160},{224,1... | collective-permute-start | bytes 1382408 | tf_op jit(solution)/shard_map/ppermute | solution.py:187
  30.8 14.4 %collective-permute-start.9 = (bf16[6,40,1152]{2,1,0:T(8,128)(2,1)S(1)}, bf16[6,40,1152]{2,1,0:T(8,128)(2,1)S(1)}, u32[]{:S(2)}, u32[]{:S(2)}) collective-permute-start(bf16[6,40,1152]{2,1,0:T(8,128)(2,1)S(1)} %constant_dynamic-update-slice_fusion.refs_9_), channel_id=1, source_target_pairs={{0,24},{8,0},{16,8},{24,16},{1,25},{9,1},{17,9},{25,17},{2,26},{10... | collective-permute-start | bytes 1658888 | tf_op jit(solution)/shard_map/ppermute | solution.py:187
  33.8 13.3 %collective-permute-start.8 = (bf16[6,40,1152]{2,1,0:T(8,128)(2,1)S(1)}, bf16[6,40,1152]{2,1,0:T(8,128)(2,1)S(1)}, u32[]{:S(2)}, u32[]{:S(2)}) collective-permute-start(bf16[6,40,1152]{2,1,0:T(8,128)(2,1)S(1)} %constant_dynamic-update-slice_fusion.refs_9_), channel_id=1, source_target_pairs={{0,8},{8,16},{16,24},{24,0},{1,9},{9,17},{17,25},{25,1},{2,10},{10... | collective-permute-start | bytes 1658888 | tf_op jit(solution)/shard_map/ppermute | solution.py:187
  41.2 12.3 %collective-permute-start.12 = (bf16[3,40,1152]{2,1,0:T(8,128)(2,1)S(1)}, bf16[3,40,1152]{2,1,0:T(8,128)(2,1)S(1)}, u32[]{:S(2)}, u32[]{:S(2)}) collective-permute-start(bf16[3,40,1152]{2,1,0:T(8,128)(2,1)S(1)} %slice.62), channel_id=1, source_target_pairs={{0,224},{32,0},{64,32},{96,64},{128,96},{160,128},{192,160},{224,1... | collective-permute-start | bytes 829448 | tf_op jit(solution)/shard_map/ppermute | solution.py:187
  42.7 10.8 %collective-permute-start.11 = (bf16[3,40,1152]{2,1,0:T(8,128)(2,1)S(1)}, bf16[3,40,1152]{2,1,0:T(8,128)(2,1)S(1)}, u32[]{:S(2)}, u32[]{:S(2)}) collective-permute-start(bf16[3,40,1152]{2,1,0:T(8,128)(2,1)S(1)} %slice.60), channel_id=1, source_target_pairs={{0,32},{32,64},{64,96},{96,128},{128,160},{160,192},{192,224},{224... | collective-permute-start | bytes 829448 | tf_op jit(solution)/shard_map/ppermute | solution.py:187
  43.3 19.9 %collective-permute-start.6 = (bf16[7,40,1152]{2,1,0:T(8,128)(2,1)}, bf16[7,40,1152]{2,1,0:T(8,128)(2,1)S(1)}, u32[]{:S(2)}, u32[]{:S(2)}) collective-permute-start(bf16[7,40,1152]{2,1,0:T(8,128)(2,1)} %get-tuple-element.45), channel_id=1, source_target_pairs={{0,32},{32,64},{64,96},{96,128},{128,160},{160,192},{192,224},{224... | collective-permute-start | bytes 1935368 | tf_op jit(solution)/shard_map/ppermute | solution.py:187
  45.1 18.1 %collective-permute-start.7 = (bf16[7,40,1152]{2,1,0:T(8,128)(2,1)}, bf16[7,40,1152]{2,1,0:T(8,128)(2,1)S(1)}, u32[]{:S(2)}, u32[]{:S(2)}) collective-permute-start(bf16[7,40,1152]{2,1,0:T(8,128)(2,1)} %get-tuple-element.46), channel_id=1, source_target_pairs={{0,224},{32,0},{64,32},{96,64},{128,96},{160,128},{192,160},{224,1... | collective-permute-start | bytes 1935368 | tf_op jit(solution)/shard_map/ppermute | solution.py:187
  47.2 15.8 %collective-permute-start.10 = (bf16[6,40,1152]{2,1,0:T(8,128)(2,1)S(1)}, bf16[6,40,1152]{2,1,0:T(8,128)(2,1)S(1)}, u32[]{:S(2)}, u32[]{:S(2)}) collective-permute-start(bf16[6,40,1152]{2,1,0:T(8,128)(2,1)S(1)} %broadcast_select_fusion.1), channel_id=1, source_target_pairs={{0,8},{1,25},{8,16},{9,1},{16,24},{17,9},{24,0},{25,17},{2,10},{3,... | collective-permute-start | bytes 1658888 | tf_op jit(solution)/shard_map/ppermute | solution.py:209
  53.5 21.8 %collective-permute-start.14 = (bf16[10,40,1152]{2,1,0:T(8,128)(2,1)S(1)}, bf16[10,40,1152]{2,1,0:T(8,128)(2,1)S(1)}, u32[]{:S(2)}, u32[]{:S(2)}) collective-permute-start(bf16[10,40,1152]{2,1,0:T(8,128)(2,1)S(1)} %slice_dynamic-update-slice_fusion.4.refs_13_), channel_id=1, source_target_pairs={{0,24},{8,0},{16,8},{24,16},{1,25},{9,1},{17,9},{25,17},{2,26},{10... | collective-permute-start | bytes 2764808 | tf_op jit(solution)/shard_map/ppermute | solution.py:187
  56.6 21.1 %collective-permute-start.13 = (bf16[10,40,1152]{2,1,0:T(8,128)(2,1)S(1)}, bf16[10,40,1152]{2,1,0:T(8,128)(2,1)S(1)}, u32[]{:S(2)}, u32[]{:S(2)}) collective-permute-start(bf16[10,40,1152]{2,1,0:T(8,128)(2,1)S(1)} %slice_dynamic-update-slice_fusion.4.refs_13_), channel_id=1, source_target_pairs={{0,8},{8,16},{16,24},{24,0},{1,9},{9,17},{17,25},{25,1},{2,10},{10... | collective-permute-start | bytes 2764808 | tf_op jit(solution)/shard_map/ppermute | solution.py:187
  63.3 9.1 %collective-permute-start.16 = (bf16[5,40,1152]{2,1,0:T(8,128)(2,1)S(1)}, bf16[5,40,1152]{2,1,0:T(8,128)(2,1)S(1)}, u32[]{:S(2)}, u32[]{:S(2)}) collective-permute-start(bf16[5,40,1152]{2,1,0:T(8,128)(2,1)S(1)} %slice.67), channel_id=1, source_target_pairs={{0,224},{32,0},{64,32},{96,64},{128,96},{160,128},{192,160},{224,1... | collective-permute-start | bytes 1382408 | tf_op jit(solution)/shard_map/ppermute | solution.py:187
  65.6 9.7 %collective-permute-start.15 = (bf16[5,40,1152]{2,1,0:T(8,128)(2,1)S(1)}, bf16[5,40,1152]{2,1,0:T(8,128)(2,1)S(1)}, u32[]{:S(2)}, u32[]{:S(2)}) collective-permute-start(bf16[5,40,1152]{2,1,0:T(8,128)(2,1)S(1)} %slice.66), channel_id=1, source_target_pairs={{0,32},{32,64},{64,96},{96,128},{128,160},{160,192},{192,224},{224... | collective-permute-start | bytes 1382408 | tf_op jit(solution)/shard_map/ppermute | solution.py:187
  77.8 14.7 %collective-permute-start.21 = (bf16[10,40,1152]{2,1,0:T(8,128)(2,1)S(1)}, bf16[10,40,1152]{2,1,0:T(8,128)(2,1)S(1)}, u32[]{:S(2)}, u32[]{:S(2)}) collective-permute-start(bf16[10,40,1152]{2,1,0:T(8,128)(2,1)S(1)} %broadcast_select_fusion), channel_id=1, source_target_pairs={{0,8},{1,25},{8,16},{9,1},{16,24},{17,9},{24,0},{25,17},{2,10},{3,... | collective-permute-start | bytes 2764808 | tf_op jit(solution)/shard_map/ppermute | solution.py:209
  78.0 11.1 %collective-permute-start.20 = (bf16[2,40,1152]{2,1,0:T(8,128)(2,1)S(1)}, bf16[2,40,1152]{2,1,0:T(8,128)(2,1)S(1)}, u32[]{:S(2)}, u32[]{:S(2)}) collective-permute-start(bf16[2,40,1152]{2,1,0:T(8,128)(2,1)S(1)} %slice.71), channel_id=1, source_target_pairs={{0,224},{32,0},{64,32},{96,64},{128,96},{160,128},{192,160},{224,1... | collective-permute-start | bytes 552968 | tf_op jit(solution)/shard_map/ppermute | solution.py:187
  79.2 9.9 %collective-permute-start.17 = (bf16[2,40,1152]{2,1,0:T(8,128)(2,1)S(1)}, bf16[2,40,1152]{2,1,0:T(8,128)(2,1)S(1)}, u32[]{:S(2)}, u32[]{:S(2)}) collective-permute-start(bf16[2,40,1152]{2,1,0:T(8,128)(2,1)S(1)} %slice.68), channel_id=1, source_target_pairs={{0,32},{32,64},{64,96},{96,128},{128,160},{160,192},{192,224},{224... | collective-permute-start | bytes 552968 | tf_op jit(solution)/shard_map/ppermute | solution.py:187
  80.1 6.6 %collective-permute-start.19 = (bf16[1,40,1152]{2,1,0:T(8,128)(2,1)S(1)}, bf16[1,40,1152]{2,1,0:T(8,128)(2,1)S(1)}, u32[]{:S(2)}, u32[]{:S(2)}) collective-permute-start(bf16[1,40,1152]{2,1,0:T(8,128)(2,1)S(1)} %slice.70), channel_id=1, source_target_pairs={{0,192},{32,224},{64,0},{96,32},{128,64},{160,96},{192,128},{224,1... | collective-permute-start | bytes 276488 | tf_op jit(solution)/shard_map/ppermute | solution.py:187
  81.9 7.2 %collective-permute-start.18 = (bf16[1,40,1152]{2,1,0:T(8,128)(2,1)S(1)}, bf16[1,40,1152]{2,1,0:T(8,128)(2,1)S(1)}, u32[]{:S(2)}, u32[]{:S(2)}) collective-permute-start(bf16[1,40,1152]{2,1,0:T(8,128)(2,1)S(1)} %slice.69), channel_id=1, source_target_pairs={{0,64},{32,96},{64,128},{96,160},{128,192},{160,224},{192,0},{224,... | collective-permute-start | bytes 276488 | tf_op jit(solution)/shard_map/ppermute | solution.py:187
  95.0 2.4 %collective-permute-start.22 = (f32[4,40,1280]{2,1,0:T(8,128)S(1)}, f32[4,40,1280]{2,1,0:T(8,128)S(1)}, u32[]{:S(2)}, u32[]{:S(2)}) collective-permute-start(f32[4,40,1280]{2,1,0:T(8,128)S(1)} %get-tuple-element.60), channel_id=1, source_target_pairs={{0,1},{1,0},{2,3},{3,2},{4,5},{5,4},{6,7},{7,6},{8,9},{9,8},{10,11... | collective-permute-start | bytes 2457608 | tf_op jit(solution)/shard_map/ppermute | solution.py:187

commit v5 on v4

--- a/solution.py
+++ b/solution.py
@@ -312,6 +312,7 @@
         out_shape=jax.ShapeDtypeStruct((NZ * NY, 16, LANES), F32),
         in_specs=[VMEM],
         out_specs=VMEM,
+        compiler_params=pltpu.CompilerParams(vmem_limit_bytes=8 * MIB),
         name="pack",
     )(value)
 
@@ -337,6 +338,7 @@
         out_shape=jax.ShapeDtypeStruct((LA, NY * LA), F32),
         in_specs=[VMEM],
         out_specs=VMEM,
+        compiler_params=pltpu.CompilerParams(vmem_limit_bytes=8 * MIB),
         name="finish",
     )(value)
 

time: 131 us -> 128 us (0.977)
  Pallas kernels: 20.6 us -> 18 us
    pallas_call x1, Pallas kernels: 1.98 us -> 0.27 us  [pack(): pl.pallas_call(pack_kernel, out_shape=jax.ShapeDtypeStruct((NZ * NY, 16,...]
where the time goes in v5:
time: 128 us; the launch traced here: 127 us
  waiting for transfers between devices  45.2 us (35%)
  starting transfers between devices  34.3 us (27%)
  blocking collectives  28.8 us (22%)
  Pallas kernels  18 us (14%)
    ppermute x21, waiting for transfers between devices, shift(): return lax.ppermute(value, axis, [(i, (i + by) % n) for i in range(n)])  35.4 us
    ppermute x21, starting transfers between devices, shift(): return lax.ppermute(value, axis, [(i, (i + by) % n) for i in range(n)])  33 us
    all_to_all x1, blocking collectives, local(): lax.all_to_all(pack(by_x), ('z', 'y'), split_axis=0, concat_axis=0, tiled...  17.1 us
    all_to_all x1, blocking collectives, local(): by_x = lax.all_to_all(parts, 'x', split_axis=0, concat_axis=0, tiled=True)  11.7 us
    pallas_call x1, Pallas kernels, products(): pl.pallas_call(product_kernel, out_shape=WHOLE, grid=(LA // STEPQ,), in_s...  10.1 us
    ppermute x2, waiting for transfers between devices, far_y(): return lax.ppermute(value, ('y', 'core'), pairs)  9.82 us
    pallas_call x1, Pallas kernels, prep(): pl.pallas_call(prep_kernel, out_shape=CHUNKS, in_specs=[SMEM, HBM], out_s...  4.42 us
  transfers between devices with their start and end apart: 23, of which 14 were waited for; matrix products, arithmetic and copies ran while one was open for 0% of the time, Pallas kernels for 8%

profile of v5, /device:TPU:2, one launch (start us, length us, event | category | flops | bytes accessed | tf_op | source)
XLA Modules:
  0.0 127.3 jit_solution(17782944634893786558)
XLA Ops:
  0.0 4.4 %prep.1 = (bf16[2,40,1152]{2,1,0:T(8,128)(2,1)}, bf16[6,40,1152]{2,1,0:T(8,128)(2,1)}, bf16[6,40,1152]{2,1,0:T(8,128)(2,1)}, bf16[1,40,1152]{2,1,0:T(8,128)(2,1)}, bf16[1,40,1152]{2,1,0:T(8,128)(2,1)}) custom-call(s32[6,6,20]{2,1,0:T(8,128)} %bitcast.1, bf16[40,384,384]{2,1,0:T(8,128)(2,1)} %basis_ref.3), custom_call_target="tpu_custom_call" | custom-call | flops 1000000 | bytes 3000000 | tf_op jit(solution)/shard_map/prep/pallas_call | solution.py:97
  4.4 0.0 copy-start.1
  4.4 2.0 %collective-permute-start = (bf16[6,40,1152]{2,1,0:T(8,128)(2,1)}, bf16[6,40,1152]{2,1,0:T(8,128)(2,1)S(1)}, u32[]{:S(2)}, u32[]{:S(2)}) collective-permute-start(bf16[6,40,1152]{2,1,0:T(8,128)(2,1)} %get-tuple-element.34), channel_id=1, source_target_pairs={{0,32},{32,64},{64,96},{96,128},{128,160},{160,192},{192,224},{224... | collective-permute-start | bytes 1658888 | tf_op jit(solution)/shard_map/ppermute | solution.py:187
  6.4 4.0 %collective-permute-start.2 = (bf16[6,40,1152]{2,1,0:T(8,128)(2,1)}, bf16[6,40,1152]{2,1,0:T(8,128)(2,1)S(1)}, u32[]{:S(2)}, u32[]{:S(2)}) collective-permute-start(bf16[6,40,1152]{2,1,0:T(8,128)(2,1)} %get-tuple-element.36), channel_id=1, source_target_pairs={{0,224},{32,0},{64,32},{96,64},{128,96},{160,128},{192,160},{224,1... | collective-permute-start | bytes 1658888 | tf_op jit(solution)/shard_map/ppermute | solution.py:187
  10.5 0.0 collective-permute-start.1
  10.5 4.1 %collective-permute-start.3 = (bf16[1,40,1152]{2,1,0:T(8,128)(2,1)}, bf16[1,40,1152]{2,1,0:T(8,128)(2,1)S(1)}, u32[]{:S(2)}, u32[]{:S(2)}) collective-permute-start(bf16[1,40,1152]{2,1,0:T(8,128)(2,1)} %get-tuple-element.37), channel_id=1, source_target_pairs={{0,192},{32,224},{64,0},{96,32},{128,64},{160,96},{192,128},{224,1... | collective-permute-start | bytes 276488 | tf_op jit(solution)/shard_map/ppermute | solution.py:187
  14.6 10.1 %products.1 = (bf16[2,40,1152]{2,1,0:T(8,128)(2,1)}, bf16[7,40,1152]{2,1,0:T(8,128)(2,1)}, bf16[7,40,1152]{2,1,0:T(8,128)(2,1)}) custom-call(s32[6,6,20]{2,1,0:T(8,128)} %bitcast.2, s32[6,6]{1,0:T(8,128)} %gpat_ref.1, bf16[40,384,384]{2,1,0:T(8,128)(2,1)} %basis_ref.3, bf16[384,384]{1,0:T(8,128)(2,1)} %occ_ref.1, bf16[384,384]{1,0:T(8,128)(2,1)} %vir_ref.1), custom_call_target="tpu_custom_call" | custom-call | flops 1132462080 | bytes 14000000 | tf_op jit(solution)/shard_map/products/pallas_call | solution.py:159
  24.7 0.0 copy-start
  24.7 0.0 collective-permute-done
  24.8 2.4 %collective-permute-done.1 = bf16[1,40,1152]{2,1,0:T(8,128)(2,1)S(1)} collective-permute-done((bf16[1,40,1152]{2,1,0:T(8,128)(2,1)}, bf16[1,40,1152]{2,1,0:T(8,128)(2,1)S(1)}, u32[]{:S(2)}, u32[]{:S(2)}) %collective-permute-start.1) | collective-permute-done | bytes 92192 | tf_op jit(solution)/shard_map/ppermute | solution.py:187
  27.1 0.1 pad_maximum_fusion
  27.2 0.0 collective-permute-done.2
  27.3 0.0 collective-permute-done.3
  27.3 0.1 pad_maximum_fusion.1
  27.4 0.5 collective-permute-start.4
  27.9 2.8 %collective-permute-start.5 = (bf16[5,40,1152]{2,1,0:T(8,128)(2,1)S(1)}, bf16[5,40,1152]{2,1,0:T(8,128)(2,1)S(1)}, u32[]{:S(2)}, u32[]{:S(2)}) collective-permute-start(bf16[5,40,1152]{2,1,0:T(8,128)(2,1)S(1)} %pad_maximum_fusion.1), channel_id=1, source_target_pairs={{0,224},{32,0},{64,32},{96,64},{128,96},{160,128},{192,160},{224,1... | collective-permute-start | bytes 1382408 | tf_op jit(solution)/shard_map/ppermute | solution.py:187
  30.7 0.0 copy-done.1
  30.8 3.1 %collective-permute-start.9 = (bf16[6,40,1152]{2,1,0:T(8,128)(2,1)S(1)}, bf16[6,40,1152]{2,1,0:T(8,128)(2,1)S(1)}, u32[]{:S(2)}, u32[]{:S(2)}) collective-permute-start(bf16[6,40,1152]{2,1,0:T(8,128)(2,1)S(1)} %constant_dynamic-update-slice_fusion.refs_9_), channel_id=1, source_target_pairs={{0,24},{8,0},{16,8},{24,16},{1,25},{9,1},{17,9},{25,17},{2,26},{10... | collective-permute-start | bytes 1658888 | tf_op jit(solution)/shard_map/ppermute | solution.py:187
  33.8 0.0 collective-permute-start.8
  33.8 5.7 %collective-permute-done.4 = bf16[5,40,1152]{2,1,0:T(8,128)(2,1)S(1)} collective-permute-done((bf16[5,40,1152]{2,1,0:T(8,128)(2,1)S(1)}, bf16[5,40,1152]{2,1,0:T(8,128)(2,1)S(1)}, u32[]{:S(2)}, u32[]{:S(2)}) %collective-permute-start.4) | collective-permute-done | bytes 460832 | tf_op jit(solution)/shard_map/ppermute | solution.py:187
  39.6 1.6 %collective-permute-done.5 = bf16[5,40,1152]{2,1,0:T(8,128)(2,1)S(1)} collective-permute-done((bf16[5,40,1152]{2,1,0:T(8,128)(2,1)S(1)}, bf16[5,40,1152]{2,1,0:T(8,128)(2,1)S(1)}, u32[]{:S(2)}, u32[]{:S(2)}) %collective-permute-start.5) | collective-permute-done | bytes 460832 | tf_op jit(solution)/shard_map/ppermute | solution.py:187
  41.2 1.5 %collective-permute-start.12 = (bf16[3,40,1152]{2,1,0:T(8,128)(2,1)S(1)}, bf16[3,40,1152]{2,1,0:T(8,128)(2,1)S(1)}, u32[]{:S(2)}, u32[]{:S(2)}) collective-permute-start(bf16[3,40,1152]{2,1,0:T(8,128)(2,1)S(1)} %slice.62), channel_id=1, source_target_pairs={{0,224},{32,0},{64,32},{96,64},{128,96},{160,128},{192,160},{224,1... | collective-permute-start | bytes 829448 | tf_op jit(solution)/shard_map/ppermute | solution.py:187
  42.7 0.6 collective-permute-start.11
  43.3 1.8 %collective-permute-start.6 = (bf16[7,40,1152]{2,1,0:T(8,128)(2,1)}, bf16[7,40,1152]{2,1,0:T(8,128)(2,1)S(1)}, u32[]{:S(2)}, u32[]{:S(2)}) collective-permute-start(bf16[7,40,1152]{2,1,0:T(8,128)(2,1)} %get-tuple-element.45), channel_id=1, source_target_pairs={{0,32},{32,64},{64,96},{96,128},{128,160},{160,192},{192,224},{224... | collective-permute-start | bytes 1935368 | tf_op jit(solution)/shard_map/ppermute | solution.py:187
  45.1 0.0 collective-permute-done.9.refs_11_
  45.1 1.6 %collective-permute-start.7 = (bf16[7,40,1152]{2,1,0:T(8,128)(2,1)}, bf16[7,40,1152]{2,1,0:T(8,128)(2,1)S(1)}, u32[]{:S(2)}, u32[]{:S(2)}) collective-permute-start(bf16[7,40,1152]{2,1,0:T(8,128)(2,1)} %get-tuple-element.46), channel_id=1, source_target_pairs={{0,224},{32,0},{64,32},{96,64},{128,96},{160,128},{192,160},{224,1... | collective-permute-start | bytes 1935368 | tf_op jit(solution)/shard_map/ppermute | solution.py:187
  46.7 0.4 collective-permute-done.8.refs_10_
  47.1 0.1 broadcast_select_fusion.1
  47.2 1.2 collective-permute-start.10
  48.4 5.0 %collective-permute-done.11 = bf16[3,40,1152]{2,1,0:T(8,128)(2,1)S(1)} collective-permute-done((bf16[3,40,1152]{2,1,0:T(8,128)(2,1)S(1)}, bf16[3,40,1152]{2,1,0:T(8,128)(2,1)S(1)}, u32[]{:S(2)}, u32[]{:S(2)}) %collective-permute-start.11) | collective-permute-done | bytes 276512 | tf_op jit(solution)/shard_map/ppermute | solution.py:187
  53.5 0.0 collective-permute-done.12
  53.5 3.1 %collective-permute-start.14 = (bf16[10,40,1152]{2,1,0:T(8,128)(2,1)S(1)}, bf16[10,40,1152]{2,1,0:T(8,128)(2,1)S(1)}, u32[]{:S(2)}, u32[]{:S(2)}) collective-permute-start(bf16[10,40,1152]{2,1,0:T(8,128)(2,1)S(1)} %slice_dynamic-update-slice_fusion.4.refs_13_), channel_id=1, source_target_pairs={{0,24},{8,0},{16,8},{24,16},{1,25},{9,1},{17,9},{25,17},{2,26},{10... | collective-permute-start | bytes 2764808 | tf_op jit(solution)/shard_map/ppermute | solution.py:187
  56.6 0.0 collective-permute-start.13
  56.6 6.3 %collective-permute-done.10.refs_12_ = bf16[6,40,1152]{2,1,0:T(8,128)(2,1)S(1)} collective-permute-done((bf16[6,40,1152]{2,1,0:T(8,128)(2,1)S(1)}, bf16[6,40,1152]{2,1,0:T(8,128)(2,1)S(1)}, u32[]{:S(2)}, u32[]{:S(2)}) %collective-permute-start.10) | collective-permute-done | bytes 552992 | tf_op jit(solution)/shard_map/ppermute | solution.py:209
  63.0 0.2 collective-permute-done.6.refs_1_
  63.2 0.0 collective-permute-done.7.refs_8_
  63.3 2.3 %collective-permute-start.16 = (bf16[5,40,1152]{2,1,0:T(8,128)(2,1)S(1)}, bf16[5,40,1152]{2,1,0:T(8,128)(2,1)S(1)}, u32[]{:S(2)}, u32[]{:S(2)}) collective-permute-start(bf16[5,40,1152]{2,1,0:T(8,128)(2,1)S(1)} %slice.67), channel_id=1, source_target_pairs={{0,224},{32,0},{64,32},{96,64},{128,96},{160,128},{192,160},{224,1... | collective-permute-start | bytes 1382408 | tf_op jit(solution)/shard_map/ppermute | solution.py:187
  65.6 0.4 collective-permute-start.15
  66.0 6.4 %collective-permute-done.16.refs_7_ = bf16[5,40,1152]{2,1,0:T(8,128)(2,1)S(1)} collective-permute-done((bf16[5,40,1152]{2,1,0:T(8,128)(2,1)S(1)}, bf16[5,40,1152]{2,1,0:T(8,128)(2,1)S(1)}, u32[]{:S(2)}, u32[]{:S(2)}) %collective-permute-start.16) | collective-permute-done | bytes 460832 | tf_op jit(solution)/shard_map/ppermute | solution.py:187
  72.4 2.9 %collective-permute-done.15.refs_2_ = bf16[5,40,1152]{2,1,0:T(8,128)(2,1)S(1)} collective-permute-done((bf16[5,40,1152]{2,1,0:T(8,128)(2,1)S(1)}, bf16[5,40,1152]{2,1,0:T(8,128)(2,1)S(1)}, u32[]{:S(2)}, u32[]{:S(2)}) %collective-permute-start.15) | collective-permute-done | bytes 460832 | tf_op jit(solution)/shard_map/ppermute | solution.py:187
  75.3 0.0 collective-permute-done.14.refs_15_
  75.3 2.4 %collective-permute-done.13.refs_14_ = bf16[10,40,1152]{2,1,0:T(8,128)(2,1)S(1)} collective-permute-done((bf16[10,40,1152]{2,1,0:T(8,128)(2,1)S(1)}, bf16[10,40,1152]{2,1,0:T(8,128)(2,1)S(1)}, u32[]{:S(2)}, u32[]{:S(2)}) %collective-permute-start.13) | collective-permute-done | bytes 921632 | tf_op jit(solution)/shard_map/ppermute | solution.py:187
  77.7 0.1 broadcast_select_fusion
  77.8 0.1 collective-permute-start.21
  78.0 1.2 collective-permute-start.20
  79.2 0.9 collective-permute-start.17
  80.1 1.8 %collective-permute-start.19 = (bf16[1,40,1152]{2,1,0:T(8,128)(2,1)S(1)}, bf16[1,40,1152]{2,1,0:T(8,128)(2,1)S(1)}, u32[]{:S(2)}, u32[]{:S(2)}) collective-permute-start(bf16[1,40,1152]{2,1,0:T(8,128)(2,1)S(1)} %slice.70), channel_id=1, source_target_pairs={{0,192},{32,224},{64,0},{96,32},{128,64},{160,96},{192,128},{224,1... | collective-permute-start | bytes 276488 | tf_op jit(solution)/shard_map/ppermute | solution.py:187
  81.9 1.2 collective-permute-start.18
  83.1 3.6 %collective-permute-done.19.refs_5_ = bf16[1,40,1152]{2,1,0:T(8,128)(2,1)S(1)} collective-permute-done((bf16[1,40,1152]{2,1,0:T(8,128)(2,1)S(1)}, bf16[1,40,1152]{2,1,0:T(8,128)(2,1)S(1)}, u32[]{:S(2)}, u32[]{:S(2)}) %collective-permute-start.19) | collective-permute-done | bytes 92192 | tf_op jit(solution)/shard_map/ppermute | solution.py:187
  86.7 2.3 %collective-permute-done.18.refs_4_ = bf16[1,40,1152]{2,1,0:T(8,128)(2,1)S(1)} collective-permute-done((bf16[1,40,1152]{2,1,0:T(8,128)(2,1)S(1)}, bf16[1,40,1152]{2,1,0:T(8,128)(2,1)S(1)}, u32[]{:S(2)}, u32[]{:S(2)}) %collective-permute-start.18) | collective-permute-done | bytes 92192 | tf_op jit(solution)/shard_map/ppermute | solution.py:187
  89.1 0.0 collective-permute-done.20.refs_6_
  89.1 0.0 collective-permute-done.17.refs_3_
  89.1 3.5 %collective-permute-done.21.refs_16_ = bf16[10,40,1152]{2,1,0:T(8,128)(2,1)S(1)} collective-permute-done((bf16[10,40,1152]{2,1,0:T(8,128)(2,1)S(1)}, bf16[10,40,1152]{2,1,0:T(8,128)(2,1)S(1)}, u32[]{:S(2)}, u32[]{:S(2)}) %collective-permute-start.21) | collective-permute-done | bytes 921632 | tf_op jit(solution)/shard_map/ppermute | solution.py:209
  92.6 0.0 copy-done
  92.6 2.4 %contract.1 = (f32[4,40,1280]{2,1,0:T(8,128)S(1)}, f32[4,40,1280]{2,1,0:T(8,128)S(1)}) custom-call(bf16[2,40,1152]{2,1,0:T(8,128)(2,1)S(1)} %copy-done, bf16[7,40,1152]{2,1,0:T(8,128)(2,1)S(1)} %collective-permute-done.6.refs_1_, bf16[5,40,1152]{2,1,0:T(8,128)(2,1)S(1)} %collective-permute-done.15.refs_2_, ...), custom_call_target="tpu_custom_call" | custom-call | flops 1887436800 | bytes 10000000 | tf_op jit(solution)/shard_map/contract/pallas_call | solution.py:277
  95.0 0.1 collective-permute-start.22
  95.1 2.3 %collective-permute-done.22 = f32[4,40,1280]{2,1,0:T(8,128)S(1)} collective-permute-done((f32[4,40,1280]{2,1,0:T(8,128)S(1)}, f32[4,40,1280]{2,1,0:T(8,128)S(1)}, u32[]{:S(2)}, u32[]{:S(2)}) %collective-permute-start.22) | collective-permute-done | bytes 819232 | tf_op jit(solution)/shard_map/ppermute | solution.py:187
  97.4 0.1 add_convert_fusion
  97.5 11.7 %all_to_all.10.in_ref = bf16[4,40,1280]{2,1,0:T(8,128)(2,1)S(1)} all-to-all(bf16[4,40,1280]{2,1,0:T(8,128)(2,1)S(1)} %add_convert_fusion), channel_id=1, replica_groups=mesh['z'=8,'y'=4,'x'=4,'core'=2] {'x'}, dimensions={0} | all-to-all | bytes 819200 | tf_op jit(solution)/shard_map/all_to_all | solution.py:353
  109.2 0.3 pack.1
  109.5 17.1 %all_to_all.11.in_ref = f32[32,16,128]{2,1,0:T(8,128)S(1)} all-to-all(f32[32,16,128]{2,1,0:T(8,128)S(1)} %pack.1), channel_id=1, replica_groups=mesh['z'=8,'y'=4,'x'=4,'core'=2] {'z','y'}, dimensions={0} | all-to-all | bytes 524288 | tf_op jit(solution)/shard_map/all_to_all | solution.py:354
  126.6 0.8 finish.1
  (21 shorter events, 0.4 us)
Async XLA Ops:
  4.4 26.2 %copy-start.1 = (bf16[2,40,1152]{2,1,0:T(8,128)(2,1)S(1)}, bf16[2,40,1152]{2,1,0:T(8,128)(2,1)}, u32[]{:S(2)}) copy-start(bf16[2,40,1152]{2,1,0:T(8,128)(2,1)} %get-tuple-element.47) | copy-start | bytes 552964
  4.4 20.3 %collective-permute-start = (bf16[6,40,1152]{2,1,0:T(8,128)(2,1)}, bf16[6,40,1152]{2,1,0:T(8,128)(2,1)S(1)}, u32[]{:S(2)}, u32[]{:S(2)}) collective-permute-start(bf16[6,40,1152]{2,1,0:T(8,128)(2,1)} %get-tuple-element.34), channel_id=1, source_target_pairs={{0,32},{32,64},{64,96},{96,128},{128,160},{160,192},{192,224},{224... | collective-permute-start | bytes 1658888 | tf_op jit(solution)/shard_map/ppermute | solution.py:187
  6.4 20.8 %collective-permute-start.2 = (bf16[6,40,1152]{2,1,0:T(8,128)(2,1)}, bf16[6,40,1152]{2,1,0:T(8,128)(2,1)S(1)}, u32[]{:S(2)}, u32[]{:S(2)}) collective-permute-start(bf16[6,40,1152]{2,1,0:T(8,128)(2,1)} %get-tuple-element.36), channel_id=1, source_target_pairs={{0,224},{32,0},{64,32},{96,64},{128,96},{160,128},{192,160},{224,1... | collective-permute-start | bytes 1658888 | tf_op jit(solution)/shard_map/ppermute | solution.py:187
  10.5 16.7 %collective-permute-start.1 = (bf16[1,40,1152]{2,1,0:T(8,128)(2,1)}, bf16[1,40,1152]{2,1,0:T(8,128)(2,1)S(1)}, u32[]{:S(2)}, u32[]{:S(2)}) collective-permute-start(bf16[1,40,1152]{2,1,0:T(8,128)(2,1)} %get-tuple-element.35), channel_id=1, source_target_pairs={{0,64},{32,96},{64,128},{96,160},{128,192},{160,224},{192,0},{224,... | collective-permute-start | bytes 276488 | tf_op jit(solution)/shard_map/ppermute | solution.py:187
  10.5 16.8 %collective-permute-start.3 = (bf16[1,40,1152]{2,1,0:T(8,128)(2,1)}, bf16[1,40,1152]{2,1,0:T(8,128)(2,1)S(1)}, u32[]{:S(2)}, u32[]{:S(2)}) collective-permute-start(bf16[1,40,1152]{2,1,0:T(8,128)(2,1)} %get-tuple-element.37), channel_id=1, source_target_pairs={{0,192},{32,224},{64,0},{96,32},{128,64},{160,96},{192,128},{224,1... | collective-permute-start | bytes 276488 | tf_op jit(solution)/shard_map/ppermute | solution.py:187
  24.7 67.8 %copy-start = (bf16[2,40,1152]{2,1,0:T(8,128)(2,1)S(1)}, bf16[2,40,1152]{2,1,0:T(8,128)(2,1)}, u32[]{:S(2)}) copy-start(bf16[2,40,1152]{2,1,0:T(8,128)(2,1)} %get-tuple-element.33.refs_0_) | copy-start | bytes 552964
  27.4 12.2 %collective-permute-start.4 = (bf16[5,40,1152]{2,1,0:T(8,128)(2,1)S(1)}, bf16[5,40,1152]{2,1,0:T(8,128)(2,1)S(1)}, u32[]{:S(2)}, u32[]{:S(2)}) collective-permute-start(bf16[5,40,1152]{2,1,0:T(8,128)(2,1)S(1)} %pad_maximum_fusion), channel_id=1, source_target_pairs={{0,32},{32,64},{64,96},{96,128},{128,160},{160,192},{192,224},{224... | collective-permute-start | bytes 1382408 | tf_op jit(solution)/shard_map/ppermute | solution.py:187
  27.9 13.3 %collective-permute-start.5 = (bf16[5,40,1152]{2,1,0:T(8,128)(2,1)S(1)}, bf16[5,40,1152]{2,1,0:T(8,128)(2,1)S(1)}, u32[]{:S(2)}, u32[]{:S(2)}) collective-permute-start(bf16[5,40,1152]{2,1,0:T(8,128)(2,1)S(1)} %pad_maximum_fusion.1), channel_id=1, source_target_pairs={{0,224},{32,0},{64,32},{96,64},{128,96},{160,128},{192,160},{224,1... | collective-permute-start | bytes 1382408 | tf_op jit(solution)/shard_map/ppermute | solution.py:187
  30.8 14.4 %collective-permute-start.9 = (bf16[6,40,1152]{2,1,0:T(8,128)(2,1)S(1)}, bf16[6,40,1152]{2,1,0:T(8,128)(2,1)S(1)}, u32[]{:S(2)}, u32[]{:S(2)}) collective-permute-start(bf16[6,40,1152]{2,1,0:T(8,128)(2,1)S(1)} %constant_dynamic-update-slice_fusion.refs_9_), channel_id=1, source_target_pairs={{0,24},{8,0},{16,8},{24,16},{1,25},{9,1},{17,9},{25,17},{2,26},{10... | collective-permute-start | bytes 1658888 | tf_op jit(solution)/shard_map/ppermute | solution.py:187
  33.8 13.3 %collective-permute-start.8 = (bf16[6,40,1152]{2,1,0:T(8,128)(2,1)S(1)}, bf16[6,40,1152]{2,1,0:T(8,128)(2,1)S(1)}, u32[]{:S(2)}, u32[]{:S(2)}) collective-permute-start(bf16[6,40,1152]{2,1,0:T(8,128)(2,1)S(1)} %constant_dynamic-update-slice_fusion.refs_9_), channel_id=1, source_target_pairs={{0,8},{8,16},{16,24},{24,0},{1,9},{9,17},{17,25},{25,1},{2,10},{10... | collective-permute-start | bytes 1658888 | tf_op jit(solution)/shard_map/ppermute | solution.py:187
  41.2 12.3 %collective-permute-start.12 = (bf16[3,40,1152]{2,1,0:T(8,128)(2,1)S(1)}, bf16[3,40,1152]{2,1,0:T(8,128)(2,1)S(1)}, u32[]{:S(2)}, u32[]{:S(2)}) collective-permute-start(bf16[3,40,1152]{2,1,0:T(8,128)(2,1)S(1)} %slice.62), channel_id=1, source_target_pairs={{0,224},{32,0},{64,32},{96,64},{128,96},{160,128},{192,160},{224,1... | collective-permute-start | bytes 829448 | tf_op jit(solution)/shard_map/ppermute | solution.py:187
  42.7 10.8 %collective-permute-start.11 = (bf16[3,40,1152]{2,1,0:T(8,128)(2,1)S(1)}, bf16[3,40,1152]{2,1,0:T(8,128)(2,1)S(1)}, u32[]{:S(2)}, u32[]{:S(2)}) collective-permute-start(bf16[3,40,1152]{2,1,0:T(8,128)(2,1)S(1)} %slice.60), channel_id=1, source_target_pairs={{0,32},{32,64},{64,96},{96,128},{128,160},{160,192},{192,224},{224... | collective-permute-start | bytes 829448 | tf_op jit(solution)/shard_map/ppermute | solution.py:187
  43.3 19.9 %collective-permute-start.6 = (bf16[7,40,1152]{2,1,0:T(8,128)(2,1)}, bf16[7,40,1152]{2,1,0:T(8,128)(2,1)S(1)}, u32[]{:S(2)}, u32[]{:S(2)}) collective-permute-start(bf16[7,40,1152]{2,1,0:T(8,128)(2,1)} %get-tuple-element.45), channel_id=1, source_target_pairs={{0,32},{32,64},{64,96},{96,128},{128,160},{160,192},{192,224},{224... | collective-permute-start | bytes 1935368 | tf_op jit(solution)/shard_map/ppermute | solution.py:187
  45.1 18.1 %collective-permute-start.7 = (bf16[7,40,1152]{2,1,0:T(8,128)(2,1)}, bf16[7,40,1152]{2,1,0:T(8,128)(2,1)S(1)}, u32[]{:S(2)}, u32[]{:S(2)}) collective-permute-start(bf16[7,40,1152]{2,1,0:T(8,128)(2,1)} %get-tuple-element.46), channel_id=1, source_target_pairs={{0,224},{32,0},{64,32},{96,64},{128,96},{160,128},{192,160},{224,1... | collective-permute-start | bytes 1935368 | tf_op jit(solution)/shard_map/ppermute | solution.py:187
  47.2 15.8 %collective-permute-start.10 = (bf16[6,40,1152]{2,1,0:T(8,128)(2,1)S(1)}, bf16[6,40,1152]{2,1,0:T(8,128)(2,1)S(1)}, u32[]{:S(2)}, u32[]{:S(2)}) collective-permute-start(bf16[6,40,1152]{2,1,0:T(8,128)(2,1)S(1)} %broadcast_select_fusion.1), channel_id=1, source_target_pairs={{0,8},{1,25},{8,16},{9,1},{16,24},{17,9},{24,0},{25,17},{2,10},{3,... | collective-permute-start | bytes 1658888 | tf_op jit(solution)/shard_map/ppermute | solution.py:209
  53.5 21.7 %collective-permute-start.14 = (bf16[10,40,1152]{2,1,0:T(8,128)(2,1)S(1)}, bf16[10,40,1152]{2,1,0:T(8,128)(2,1)S(1)}, u32[]{:S(2)}, u32[]{:S(2)}) collective-permute-start(bf16[10,40,1152]{2,1,0:T(8,128)(2,1)S(1)} %slice_dynamic-update-slice_fusion.4.refs_13_), channel_id=1, source_target_pairs={{0,24},{8,0},{16,8},{24,16},{1,25},{9,1},{17,9},{25,17},{2,26},{10... | collective-permute-start | bytes 2764808 | tf_op jit(solution)/shard_map/ppermute | solution.py:187
  56.6 21.1 %collective-permute-start.13 = (bf16[10,40,1152]{2,1,0:T(8,128)(2,1)S(1)}, bf16[10,40,1152]{2,1,0:T(8,128)(2,1)S(1)}, u32[]{:S(2)}, u32[]{:S(2)}) collective-permute-start(bf16[10,40,1152]{2,1,0:T(8,128)(2,1)S(1)} %slice_dynamic-update-slice_fusion.4.refs_13_), channel_id=1, source_target_pairs={{0,8},{8,16},{16,24},{24,0},{1,9},{9,17},{17,25},{25,1},{2,10},{10... | collective-permute-start | bytes 2764808 | tf_op jit(solution)/shard_map/ppermute | solution.py:187
  63.3 9.1 %collective-permute-start.16 = (bf16[5,40,1152]{2,1,0:T(8,128)(2,1)S(1)}, bf16[5,40,1152]{2,1,0:T(8,128)(2,1)S(1)}, u32[]{:S(2)}, u32[]{:S(2)}) collective-permute-start(bf16[5,40,1152]{2,1,0:T(8,128)(2,1)S(1)} %slice.67), channel_id=1, source_target_pairs={{0,224},{32,0},{64,32},{96,64},{128,96},{160,128},{192,160},{224,1... | collective-permute-start | bytes 1382408 | tf_op jit(solution)/shard_map/ppermute | solution.py:187
  65.6 9.7 %collective-permute-start.15 = (bf16[5,40,1152]{2,1,0:T(8,128)(2,1)S(1)}, bf16[5,40,1152]{2,1,0:T(8,128)(2,1)S(1)}, u32[]{:S(2)}, u32[]{:S(2)}) collective-permute-start(bf16[5,40,1152]{2,1,0:T(8,128)(2,1)S(1)} %slice.66), channel_id=1, source_target_pairs={{0,32},{32,64},{64,96},{96,128},{128,160},{160,192},{192,224},{224... | collective-permute-start | bytes 1382408 | tf_op jit(solution)/shard_map/ppermute | solution.py:187
  77.8 14.7 %collective-permute-start.21 = (bf16[10,40,1152]{2,1,0:T(8,128)(2,1)S(1)}, bf16[10,40,1152]{2,1,0:T(8,128)(2,1)S(1)}, u32[]{:S(2)}, u32[]{:S(2)}) collective-permute-start(bf16[10,40,1152]{2,1,0:T(8,128)(2,1)S(1)} %broadcast_select_fusion), channel_id=1, source_target_pairs={{0,8},{1,25},{8,16},{9,1},{16,24},{17,9},{24,0},{25,17},{2,10},{3,... | collective-permute-start | bytes 2764808 | tf_op jit(solution)/shard_map/ppermute | solution.py:209
  78.0 11.1 %collective-permute-start.20 = (bf16[2,40,1152]{2,1,0:T(8,128)(2,1)S(1)}, bf16[2,40,1152]{2,1,0:T(8,128)(2,1)S(1)}, u32[]{:S(2)}, u32[]{:S(2)}) collective-permute-start(bf16[2,40,1152]{2,1,0:T(8,128)(2,1)S(1)} %slice.71), channel_id=1, source_target_pairs={{0,224},{32,0},{64,32},{96,64},{128,96},{160,128},{192,160},{224,1... | collective-permute-start | bytes 552968 | tf_op jit(solution)/shard_map/ppermute | solution.py:187
  79.2 9.8 %collective-permute-start.17 = (bf16[2,40,1152]{2,1,0:T(8,128)(2,1)S(1)}, bf16[2,40,1152]{2,1,0:T(8,128)(2,1)S(1)}, u32[]{:S(2)}, u32[]{:S(2)}) collective-permute-start(bf16[2,40,1152]{2,1,0:T(8,128)(2,1)S(1)} %slice.68), channel_id=1, source_target_pairs={{0,32},{32,64},{64,96},{96,128},{128,160},{160,192},{192,224},{224... | collective-permute-start | bytes 552968 | tf_op jit(solution)/shard_map/ppermute | solution.py:187
  80.1 6.6 %collective-permute-start.19 = (bf16[1,40,1152]{2,1,0:T(8,128)(2,1)S(1)}, bf16[1,40,1152]{2,1,0:T(8,128)(2,1)S(1)}, u32[]{:S(2)}, u32[]{:S(2)}) collective-permute-start(bf16[1,40,1152]{2,1,0:T(8,128)(2,1)S(1)} %slice.70), channel_id=1, source_target_pairs={{0,192},{32,224},{64,0},{96,32},{128,64},{160,96},{192,128},{224,1... | collective-permute-start | bytes 276488 | tf_op jit(solution)/shard_map/ppermute | solution.py:187
  81.9 7.2 %collective-permute-start.18 = (bf16[1,40,1152]{2,1,0:T(8,128)(2,1)S(1)}, bf16[1,40,1152]{2,1,0:T(8,128)(2,1)S(1)}, u32[]{:S(2)}, u32[]{:S(2)}) collective-permute-start(bf16[1,40,1152]{2,1,0:T(8,128)(2,1)S(1)} %slice.69), channel_id=1, source_target_pairs={{0,64},{32,96},{64,128},{96,160},{128,192},{160,224},{192,0},{224,... | collective-permute-start | bytes 276488 | tf_op jit(solution)/shard_map/ppermute | solution.py:187
  95.0 2.4 %collective-permute-start.22 = (f32[4,40,1280]{2,1,0:T(8,128)S(1)}, f32[4,40,1280]{2,1,0:T(8,128)S(1)}, u32[]{:S(2)}, u32[]{:S(2)}) collective-permute-start(f32[4,40,1280]{2,1,0:T(8,128)S(1)} %get-tuple-element.60), channel_id=1, source_target_pairs={{0,1},{1,0},{2,3},{3,2},{4,5},{5,4},{6,7},{7,6},{8,9},{9,8},{10,11... | collective-permute-start | bytes 2457608 | tf_op jit(solution)/shard_map/ppermute | solution.py:187

commit v6 on v5

--- a/solution.py
+++ b/solution.py
@@ -302,14 +302,13 @@
         upper = jnp.concatenate([oct8[0], oct8[1], oct8[2], jnp.zeros((8, 8), F32)], axis=1)
         lower = jnp.concatenate([oct8[3], oct8[4], jnp.zeros((8, 48), F32)], axis=1)
         dest = lax.rem(z - d + NZ, NZ) * NY + lax.rem(y - e + NY, NY)
-        out_ref[dest, 0:8, :] = upper
-        out_ref[dest, 8:16, :] = lower
+        out_ref[dest] = jnp.concatenate([upper, lower], axis=0).astype(BF16)
 
 
 def pack(value):
     return pl.pallas_call(
         pack_kernel,
-        out_shape=jax.ShapeDtypeStruct((NZ * NY, 16, LANES), F32),
+        out_shape=jax.ShapeDtypeStruct((NZ * NY, 16, LANES), BF16),
         in_specs=[VMEM],
         out_specs=VMEM,
         compiler_params=pltpu.CompilerParams(vmem_limit_bytes=8 * MIB),
@@ -320,9 +319,9 @@
 def finish_kernel(in_ref, out_ref):
     parts = []
     for y in range(NY):
-        total = in_ref[y]
+        total = in_ref[y].astype(F32)
         for z in range(1, NZ):
-            total = total + in_ref[z * NY + y]
+            total = total + in_ref[z * NY + y].astype(F32)
         for o in range(5):
             lo = (o % 3) * LA
             parts.append(total[8 * (o // 3) : 8 * (o // 3) + 8, lo : lo + LA])

time: 128 us -> 126 us (0.984)
  blocking collectives: 28.8 us -> 27.1 us
    all_to_all x1, blocking collectives: 17.1 us -> 15.3 us  [local(): lax.all_to_all(pack(by_x), ('z', 'y'), split_axis=0, concat_axis=0, tiled...]
where the time goes in v6:
time: 126 us
  waiting for transfers between devices  45.2 us (36%)
  starting transfers between devices  34.3 us (27%)
  blocking collectives  27.1 us (22%)
  Pallas kernels  17.9 us (14%)
    ppermute x21, waiting for transfers between devices, shift(): return lax.ppermute(value, axis, [(i, (i + by) % n) for i in range(n)])  35.4 us
    ppermute x21, starting transfers between devices, shift(): return lax.ppermute(value, axis, [(i, (i + by) % n) for i in range(n)])  33 us
    all_to_all x1, blocking collectives, local(): lax.all_to_all(pack(by_x), ('z', 'y'), split_axis=0, concat_axis=0, tiled...  15.3 us
    all_to_all x1, blocking collectives, local(): by_x = lax.all_to_all(parts, 'x', split_axis=0, concat_axis=0, tiled=True)  11.7 us
    pallas_call x1, Pallas kernels, products(): pl.pallas_call(product_kernel, out_shape=WHOLE, grid=(LA // STEPQ,), in_s...  10.1 us
    ppermute x2, waiting for transfers between devices, far_y(): return lax.ppermute(value, ('y', 'core'), pairs)  9.82 us
    pallas_call x1, Pallas kernels, prep(): pl.pallas_call(prep_kernel, out_shape=CHUNKS, in_specs=[SMEM, HBM], out_s...  4.42 us
  transfers between devices with their start and end apart: 23, of which 14 were waited for; matrix products, arithmetic and copies ran while one was open for 0% of the time, Pallas kernels for 8%

profile of v6, /device:TPU:2, one launch (start us, length us, event | category | flops | bytes accessed | tf_op | source)
XLA Modules:
  0.0 125.5 jit_solution(17604144334920581615)
XLA Ops:
  0.0 4.4 %prep.1 = (bf16[2,40,1152]{2,1,0:T(8,128)(2,1)}, bf16[6,40,1152]{2,1,0:T(8,128)(2,1)}, bf16[6,40,1152]{2,1,0:T(8,128)(2,1)}, bf16[1,40,1152]{2,1,0:T(8,128)(2,1)}, bf16[1,40,1152]{2,1,0:T(8,128)(2,1)}) custom-call(s32[6,6,20]{2,1,0:T(8,128)} %bitcast.1, bf16[40,384,384]{2,1,0:T(8,128)(2,1)} %basis_ref.3), custom_call_target="tpu_custom_call" | custom-call | flops 1000000 | bytes 3000000 | tf_op jit(solution)/shard_map/prep/pallas_call | solution.py:97
  4.4 0.0 copy-start.1
  4.4 2.0 %collective-permute-start = (bf16[6,40,1152]{2,1,0:T(8,128)(2,1)}, bf16[6,40,1152]{2,1,0:T(8,128)(2,1)S(1)}, u32[]{:S(2)}, u32[]{:S(2)}) collective-permute-start(bf16[6,40,1152]{2,1,0:T(8,128)(2,1)} %get-tuple-element.34), channel_id=1, source_target_pairs={{0,32},{32,64},{64,96},{96,128},{128,160},{160,192},{192,224},{224... | collective-permute-start | bytes 1658888 | tf_op jit(solution)/shard_map/ppermute | solution.py:187
  6.4 4.0 %collective-permute-start.2 = (bf16[6,40,1152]{2,1,0:T(8,128)(2,1)}, bf16[6,40,1152]{2,1,0:T(8,128)(2,1)S(1)}, u32[]{:S(2)}, u32[]{:S(2)}) collective-permute-start(bf16[6,40,1152]{2,1,0:T(8,128)(2,1)} %get-tuple-element.36), channel_id=1, source_target_pairs={{0,224},{32,0},{64,32},{96,64},{128,96},{160,128},{192,160},{224,1... | collective-permute-start | bytes 1658888 | tf_op jit(solution)/shard_map/ppermute | solution.py:187
  10.5 0.0 collective-permute-start.1
  10.5 4.1 %collective-permute-start.3 = (bf16[1,40,1152]{2,1,0:T(8,128)(2,1)}, bf16[1,40,1152]{2,1,0:T(8,128)(2,1)S(1)}, u32[]{:S(2)}, u32[]{:S(2)}) collective-permute-start(bf16[1,40,1152]{2,1,0:T(8,128)(2,1)} %get-tuple-element.37), channel_id=1, source_target_pairs={{0,192},{32,224},{64,0},{96,32},{128,64},{160,96},{192,128},{224,1... | collective-permute-start | bytes 276488 | tf_op jit(solution)/shard_map/ppermute | solution.py:187
  14.6 10.1 %products.1 = (bf16[2,40,1152]{2,1,0:T(8,128)(2,1)}, bf16[7,40,1152]{2,1,0:T(8,128)(2,1)}, bf16[7,40,1152]{2,1,0:T(8,128)(2,1)}) custom-call(s32[6,6,20]{2,1,0:T(8,128)} %bitcast.2, s32[6,6]{1,0:T(8,128)} %gpat_ref.1, bf16[40,384,384]{2,1,0:T(8,128)(2,1)} %basis_ref.3, bf16[384,384]{1,0:T(8,128)(2,1)} %occ_ref.1, bf16[384,384]{1,0:T(8,128)(2,1)} %vir_ref.1), custom_call_target="tpu_custom_call" | custom-call | flops 1132462080 | bytes 14000000 | tf_op jit(solution)/shard_map/products/pallas_call | solution.py:159
  24.7 0.0 copy-start
  24.7 0.0 collective-permute-done
  24.8 2.4 %collective-permute-done.1 = bf16[1,40,1152]{2,1,0:T(8,128)(2,1)S(1)} collective-permute-done((bf16[1,40,1152]{2,1,0:T(8,128)(2,1)}, bf16[1,40,1152]{2,1,0:T(8,128)(2,1)S(1)}, u32[]{:S(2)}, u32[]{:S(2)}) %collective-permute-start.1) | collective-permute-done | bytes 92192 | tf_op jit(solution)/shard_map/ppermute | solution.py:187
  27.1 0.1 pad_maximum_fusion
  27.2 0.0 collective-permute-done.2
  27.3 0.0 collective-permute-done.3
  27.3 0.1 pad_maximum_fusion.1
  27.4 0.5 collective-permute-start.4
  27.9 2.8 %collective-permute-start.5 = (bf16[5,40,1152]{2,1,0:T(8,128)(2,1)S(1)}, bf16[5,40,1152]{2,1,0:T(8,128)(2,1)S(1)}, u32[]{:S(2)}, u32[]{:S(2)}) collective-permute-start(bf16[5,40,1152]{2,1,0:T(8,128)(2,1)S(1)} %pad_maximum_fusion.1), channel_id=1, source_target_pairs={{0,224},{32,0},{64,32},{96,64},{128,96},{160,128},{192,160},{224,1... | collective-permute-start | bytes 1382408 | tf_op jit(solution)/shard_map/ppermute | solution.py:187
  30.7 0.0 copy-done.1
  30.8 3.1 %collective-permute-start.9 = (bf16[6,40,1152]{2,1,0:T(8,128)(2,1)S(1)}, bf16[6,40,1152]{2,1,0:T(8,128)(2,1)S(1)}, u32[]{:S(2)}, u32[]{:S(2)}) collective-permute-start(bf16[6,40,1152]{2,1,0:T(8,128)(2,1)S(1)} %constant_dynamic-update-slice_fusion.refs_9_), channel_id=1, source_target_pairs={{0,24},{8,0},{16,8},{24,16},{1,25},{9,1},{17,9},{25,17},{2,26},{10... | collective-permute-start | bytes 1658888 | tf_op jit(solution)/shard_map/ppermute | solution.py:187
  33.8 0.0 collective-permute-start.8
  33.8 5.7 %collective-permute-done.4 = bf16[5,40,1152]{2,1,0:T(8,128)(2,1)S(1)} collective-permute-done((bf16[5,40,1152]{2,1,0:T(8,128)(2,1)S(1)}, bf16[5,40,1152]{2,1,0:T(8,128)(2,1)S(1)}, u32[]{:S(2)}, u32[]{:S(2)}) %collective-permute-start.4) | collective-permute-done | bytes 460832 | tf_op jit(solution)/shard_map/ppermute | solution.py:187
  39.6 1.6 %collective-permute-done.5 = bf16[5,40,1152]{2,1,0:T(8,128)(2,1)S(1)} collective-permute-done((bf16[5,40,1152]{2,1,0:T(8,128)(2,1)S(1)}, bf16[5,40,1152]{2,1,0:T(8,128)(2,1)S(1)}, u32[]{:S(2)}, u32[]{:S(2)}) %collective-permute-start.5) | collective-permute-done | bytes 460832 | tf_op jit(solution)/shard_map/ppermute | solution.py:187
  41.2 1.5 %collective-permute-start.12 = (bf16[3,40,1152]{2,1,0:T(8,128)(2,1)S(1)}, bf16[3,40,1152]{2,1,0:T(8,128)(2,1)S(1)}, u32[]{:S(2)}, u32[]{:S(2)}) collective-permute-start(bf16[3,40,1152]{2,1,0:T(8,128)(2,1)S(1)} %slice.62), channel_id=1, source_target_pairs={{0,224},{32,0},{64,32},{96,64},{128,96},{160,128},{192,160},{224,1... | collective-permute-start | bytes 829448 | tf_op jit(solution)/shard_map/ppermute | solution.py:187
  42.7 0.6 collective-permute-start.11
  43.3 1.8 %collective-permute-start.6 = (bf16[7,40,1152]{2,1,0:T(8,128)(2,1)}, bf16[7,40,1152]{2,1,0:T(8,128)(2,1)S(1)}, u32[]{:S(2)}, u32[]{:S(2)}) collective-permute-start(bf16[7,40,1152]{2,1,0:T(8,128)(2,1)} %get-tuple-element.45), channel_id=1, source_target_pairs={{0,32},{32,64},{64,96},{96,128},{128,160},{160,192},{192,224},{224... | collective-permute-start | bytes 1935368 | tf_op jit(solution)/shard_map/ppermute | solution.py:187
  45.1 0.0 collective-permute-done.9.refs_11_
  45.1 1.6 %collective-permute-start.7 = (bf16[7,40,1152]{2,1,0:T(8,128)(2,1)}, bf16[7,40,1152]{2,1,0:T(8,128)(2,1)S(1)}, u32[]{:S(2)}, u32[]{:S(2)}) collective-permute-start(bf16[7,40,1152]{2,1,0:T(8,128)(2,1)} %get-tuple-element.46), channel_id=1, source_target_pairs={{0,224},{32,0},{64,32},{96,64},{128,96},{160,128},{192,160},{224,1... | collective-permute-start | bytes 1935368 | tf_op jit(solution)/shard_map/ppermute | solution.py:187
  46.7 0.4 collective-permute-done.8.refs_10_
  47.1 0.1 broadcast_select_fusion.1
  47.2 1.2 collective-permute-start.10
  48.4 5.0 %collective-permute-done.11 = bf16[3,40,1152]{2,1,0:T(8,128)(2,1)S(1)} collective-permute-done((bf16[3,40,1152]{2,1,0:T(8,128)(2,1)S(1)}, bf16[3,40,1152]{2,1,0:T(8,128)(2,1)S(1)}, u32[]{:S(2)}, u32[]{:S(2)}) %collective-permute-start.11) | collective-permute-done | bytes 276512 | tf_op jit(solution)/shard_map/ppermute | solution.py:187
  53.5 0.0 collective-permute-done.12
  53.5 3.1 %collective-permute-start.14 = (bf16[10,40,1152]{2,1,0:T(8,128)(2,1)S(1)}, bf16[10,40,1152]{2,1,0:T(8,128)(2,1)S(1)}, u32[]{:S(2)}, u32[]{:S(2)}) collective-permute-start(bf16[10,40,1152]{2,1,0:T(8,128)(2,1)S(1)} %slice_dynamic-update-slice_fusion.4.refs_13_), channel_id=1, source_target_pairs={{0,24},{8,0},{16,8},{24,16},{1,25},{9,1},{17,9},{25,17},{2,26},{10... | collective-permute-start | bytes 2764808 | tf_op jit(solution)/shard_map/ppermute | solution.py:187
  56.6 0.0 collective-permute-start.13
  56.6 6.3 %collective-permute-done.10.refs_12_ = bf16[6,40,1152]{2,1,0:T(8,128)(2,1)S(1)} collective-permute-done((bf16[6,40,1152]{2,1,0:T(8,128)(2,1)S(1)}, bf16[6,40,1152]{2,1,0:T(8,128)(2,1)S(1)}, u32[]{:S(2)}, u32[]{:S(2)}) %collective-permute-start.10) | collective-permute-done | bytes 552992 | tf_op jit(solution)/shard_map/ppermute | solution.py:209
  63.0 0.2 collective-permute-done.6.refs_1_
  63.2 0.0 collective-permute-done.7.refs_8_
  63.3 2.3 %collective-permute-start.16 = (bf16[5,40,1152]{2,1,0:T(8,128)(2,1)S(1)}, bf16[5,40,1152]{2,1,0:T(8,128)(2,1)S(1)}, u32[]{:S(2)}, u32[]{:S(2)}) collective-permute-start(bf16[5,40,1152]{2,1,0:T(8,128)(2,1)S(1)} %slice.67), channel_id=1, source_target_pairs={{0,224},{32,0},{64,32},{96,64},{128,96},{160,128},{192,160},{224,1... | collective-permute-start | bytes 1382408 | tf_op jit(solution)/shard_map/ppermute | solution.py:187
  65.6 0.4 collective-permute-start.15
  66.0 6.4 %collective-permute-done.16.refs_7_ = bf16[5,40,1152]{2,1,0:T(8,128)(2,1)S(1)} collective-permute-done((bf16[5,40,1152]{2,1,0:T(8,128)(2,1)S(1)}, bf16[5,40,1152]{2,1,0:T(8,128)(2,1)S(1)}, u32[]{:S(2)}, u32[]{:S(2)}) %collective-permute-start.16) | collective-permute-done | bytes 460832 | tf_op jit(solution)/shard_map/ppermute | solution.py:187
  72.4 2.9 %collective-permute-done.15.refs_2_ = bf16[5,40,1152]{2,1,0:T(8,128)(2,1)S(1)} collective-permute-done((bf16[5,40,1152]{2,1,0:T(8,128)(2,1)S(1)}, bf16[5,40,1152]{2,1,0:T(8,128)(2,1)S(1)}, u32[]{:S(2)}, u32[]{:S(2)}) %collective-permute-start.15) | collective-permute-done | bytes 460832 | tf_op jit(solution)/shard_map/ppermute | solution.py:187
  75.3 0.0 collective-permute-done.14.refs_15_
  75.3 2.4 %collective-permute-done.13.refs_14_ = bf16[10,40,1152]{2,1,0:T(8,128)(2,1)S(1)} collective-permute-done((bf16[10,40,1152]{2,1,0:T(8,128)(2,1)S(1)}, bf16[10,40,1152]{2,1,0:T(8,128)(2,1)S(1)}, u32[]{:S(2)}, u32[]{:S(2)}) %collective-permute-start.13) | collective-permute-done | bytes 921632 | tf_op jit(solution)/shard_map/ppermute | solution.py:187
  77.7 0.1 broadcast_select_fusion
  77.8 0.1 collective-permute-start.21
  78.0 1.2 collective-permute-start.20
  79.2 0.9 collective-permute-start.17
  80.1 1.8 %collective-permute-start.19 = (bf16[1,40,1152]{2,1,0:T(8,128)(2,1)S(1)}, bf16[1,40,1152]{2,1,0:T(8,128)(2,1)S(1)}, u32[]{:S(2)}, u32[]{:S(2)}) collective-permute-start(bf16[1,40,1152]{2,1,0:T(8,128)(2,1)S(1)} %slice.70), channel_id=1, source_target_pairs={{0,192},{32,224},{64,0},{96,32},{128,64},{160,96},{192,128},{224,1... | collective-permute-start | bytes 276488 | tf_op jit(solution)/shard_map/ppermute | solution.py:187
  81.9 1.2 collective-permute-start.18
  83.1 3.6 %collective-permute-done.19.refs_5_ = bf16[1,40,1152]{2,1,0:T(8,128)(2,1)S(1)} collective-permute-done((bf16[1,40,1152]{2,1,0:T(8,128)(2,1)S(1)}, bf16[1,40,1152]{2,1,0:T(8,128)(2,1)S(1)}, u32[]{:S(2)}, u32[]{:S(2)}) %collective-permute-start.19) | collective-permute-done | bytes 92192 | tf_op jit(solution)/shard_map/ppermute | solution.py:187
  86.7 2.3 %collective-permute-done.18.refs_4_ = bf16[1,40,1152]{2,1,0:T(8,128)(2,1)S(1)} collective-permute-done((bf16[1,40,1152]{2,1,0:T(8,128)(2,1)S(1)}, bf16[1,40,1152]{2,1,0:T(8,128)(2,1)S(1)}, u32[]{:S(2)}, u32[]{:S(2)}) %collective-permute-start.18) | collective-permute-done | bytes 92192 | tf_op jit(solution)/shard_map/ppermute | solution.py:187
  89.1 0.0 collective-permute-done.20.refs_6_
  89.1 0.0 collective-permute-done.17.refs_3_
  89.1 3.5 %collective-permute-done.21.refs_16_ = bf16[10,40,1152]{2,1,0:T(8,128)(2,1)S(1)} collective-permute-done((bf16[10,40,1152]{2,1,0:T(8,128)(2,1)S(1)}, bf16[10,40,1152]{2,1,0:T(8,128)(2,1)S(1)}, u32[]{:S(2)}, u32[]{:S(2)}) %collective-permute-start.21) | collective-permute-done | bytes 921632 | tf_op jit(solution)/shard_map/ppermute | solution.py:209
  92.6 0.0 copy-done
  92.6 2.4 %contract.1 = (f32[4,40,1280]{2,1,0:T(8,128)S(1)}, f32[4,40,1280]{2,1,0:T(8,128)S(1)}) custom-call(bf16[2,40,1152]{2,1,0:T(8,128)(2,1)S(1)} %copy-done, bf16[7,40,1152]{2,1,0:T(8,128)(2,1)S(1)} %collective-permute-done.6.refs_1_, bf16[5,40,1152]{2,1,0:T(8,128)(2,1)S(1)} %collective-permute-done.15.refs_2_, ...), custom_call_target="tpu_custom_call" | custom-call | flops 1887436800 | bytes 10000000 | tf_op jit(solution)/shard_map/contract/pallas_call | solution.py:277
  95.0 0.1 collective-permute-start.22
  95.1 2.3 %collective-permute-done.22 = f32[4,40,1280]{2,1,0:T(8,128)S(1)} collective-permute-done((f32[4,40,1280]{2,1,0:T(8,128)S(1)}, f32[4,40,1280]{2,1,0:T(8,128)S(1)}, u32[]{:S(2)}, u32[]{:S(2)}) %collective-permute-start.22) | collective-permute-done | bytes 819232 | tf_op jit(solution)/shard_map/ppermute | solution.py:187
  97.4 0.1 add_convert_fusion
  97.5 11.7 %all_to_all.10.in_ref = bf16[4,40,1280]{2,1,0:T(8,128)(2,1)S(1)} all-to-all(bf16[4,40,1280]{2,1,0:T(8,128)(2,1)S(1)} %add_convert_fusion), channel_id=1, replica_groups=mesh['z'=8,'y'=4,'x'=4,'core'=2] {'x'}, dimensions={0} | all-to-all | bytes 819200 | tf_op jit(solution)/shard_map/all_to_all | solution.py:352
  109.2 0.2 pack.1
  109.4 15.3 %all_to_all.11.in_ref = bf16[32,16,128]{2,1,0:T(8,128)(2,1)S(1)} all-to-all(bf16[32,16,128]{2,1,0:T(8,128)(2,1)S(1)} %pack.1), channel_id=1, replica_groups=mesh['z'=8,'y'=4,'x'=4,'core'=2] {'z','y'}, dimensions={0} | all-to-all | bytes 262144 | tf_op jit(solution)/shard_map/all_to_all | solution.py:353
  124.7 0.8 finish.1
  (21 shorter events, 0.4 us)
Async XLA Ops:
  4.4 26.2 %copy-start.1 = (bf16[2,40,1152]{2,1,0:T(8,128)(2,1)S(1)}, bf16[2,40,1152]{2,1,0:T(8,128)(2,1)}, u32[]{:S(2)}) copy-start(bf16[2,40,1152]{2,1,0:T(8,128)(2,1)} %get-tuple-element.47) | copy-start | bytes 552964
  4.4 20.3 %collective-permute-start = (bf16[6,40,1152]{2,1,0:T(8,128)(2,1)}, bf16[6,40,1152]{2,1,0:T(8,128)(2,1)S(1)}, u32[]{:S(2)}, u32[]{:S(2)}) collective-permute-start(bf16[6,40,1152]{2,1,0:T(8,128)(2,1)} %get-tuple-element.34), channel_id=1, source_target_pairs={{0,32},{32,64},{64,96},{96,128},{128,160},{160,192},{192,224},{224... | collective-permute-start | bytes 1658888 | tf_op jit(solution)/shard_map/ppermute | solution.py:187
  6.4 20.8 %collective-permute-start.2 = (bf16[6,40,1152]{2,1,0:T(8,128)(2,1)}, bf16[6,40,1152]{2,1,0:T(8,128)(2,1)S(1)}, u32[]{:S(2)}, u32[]{:S(2)}) collective-permute-start(bf16[6,40,1152]{2,1,0:T(8,128)(2,1)} %get-tuple-element.36), channel_id=1, source_target_pairs={{0,224},{32,0},{64,32},{96,64},{128,96},{160,128},{192,160},{224,1... | collective-permute-start | bytes 1658888 | tf_op jit(solution)/shard_map/ppermute | solution.py:187
  10.5 16.7 %collective-permute-start.1 = (bf16[1,40,1152]{2,1,0:T(8,128)(2,1)}, bf16[1,40,1152]{2,1,0:T(8,128)(2,1)S(1)}, u32[]{:S(2)}, u32[]{:S(2)}) collective-permute-start(bf16[1,40,1152]{2,1,0:T(8,128)(2,1)} %get-tuple-element.35), channel_id=1, source_target_pairs={{0,64},{32,96},{64,128},{96,160},{128,192},{160,224},{192,0},{224,... | collective-permute-start | bytes 276488 | tf_op jit(solution)/shard_map/ppermute | solution.py:187
  10.5 16.8 %collective-permute-start.3 = (bf16[1,40,1152]{2,1,0:T(8,128)(2,1)}, bf16[1,40,1152]{2,1,0:T(8,128)(2,1)S(1)}, u32[]{:S(2)}, u32[]{:S(2)}) collective-permute-start(bf16[1,40,1152]{2,1,0:T(8,128)(2,1)} %get-tuple-element.37), channel_id=1, source_target_pairs={{0,192},{32,224},{64,0},{96,32},{128,64},{160,96},{192,128},{224,1... | collective-permute-start | bytes 276488 | tf_op jit(solution)/shard_map/ppermute | solution.py:187
  24.7 67.8 %copy-start = (bf16[2,40,1152]{2,1,0:T(8,128)(2,1)S(1)}, bf16[2,40,1152]{2,1,0:T(8,128)(2,1)}, u32[]{:S(2)}) copy-start(bf16[2,40,1152]{2,1,0:T(8,128)(2,1)} %get-tuple-element.33.refs_0_) | copy-start | bytes 552964
  27.4 12.2 %collective-permute-start.4 = (bf16[5,40,1152]{2,1,0:T(8,128)(2,1)S(1)}, bf16[5,40,1152]{2,1,0:T(8,128)(2,1)S(1)}, u32[]{:S(2)}, u32[]{:S(2)}) collective-permute-start(bf16[5,40,1152]{2,1,0:T(8,128)(2,1)S(1)} %pad_maximum_fusion), channel_id=1, source_target_pairs={{0,32},{32,64},{64,96},{96,128},{128,160},{160,192},{192,224},{224... | collective-permute-start | bytes 1382408 | tf_op jit(solution)/shard_map/ppermute | solution.py:187
  27.9 13.3 %collective-permute-start.5 = (bf16[5,40,1152]{2,1,0:T(8,128)(2,1)S(1)}, bf16[5,40,1152]{2,1,0:T(8,128)(2,1)S(1)}, u32[]{:S(2)}, u32[]{:S(2)}) collective-permute-start(bf16[5,40,1152]{2,1,0:T(8,128)(2,1)S(1)} %pad_maximum_fusion.1), channel_id=1, source_target_pairs={{0,224},{32,0},{64,32},{96,64},{128,96},{160,128},{192,160},{224,1... | collective-permute-start | bytes 1382408 | tf_op jit(solution)/shard_map/ppermute | solution.py:187
  30.8 14.4 %collective-permute-start.9 = (bf16[6,40,1152]{2,1,0:T(8,128)(2,1)S(1)}, bf16[6,40,1152]{2,1,0:T(8,128)(2,1)S(1)}, u32[]{:S(2)}, u32[]{:S(2)}) collective-permute-start(bf16[6,40,1152]{2,1,0:T(8,128)(2,1)S(1)} %constant_dynamic-update-slice_fusion.refs_9_), channel_id=1, source_target_pairs={{0,24},{8,0},{16,8},{24,16},{1,25},{9,1},{17,9},{25,17},{2,26},{10... | collective-permute-start | bytes 1658888 | tf_op jit(solution)/shard_map/ppermute | solution.py:187
  33.8 13.3 %collective-permute-start.8 = (bf16[6,40,1152]{2,1,0:T(8,128)(2,1)S(1)}, bf16[6,40,1152]{2,1,0:T(8,128)(2,1)S(1)}, u32[]{:S(2)}, u32[]{:S(2)}) collective-permute-start(bf16[6,40,1152]{2,1,0:T(8,128)(2,1)S(1)} %constant_dynamic-update-slice_fusion.refs_9_), channel_id=1, source_target_pairs={{0,8},{8,16},{16,24},{24,0},{1,9},{9,17},{17,25},{25,1},{2,10},{10... | collective-permute-start | bytes 1658888 | tf_op jit(solution)/shard_map/ppermute | solution.py:187
  41.2 12.3 %collective-permute-start.12 = (bf16[3,40,1152]{2,1,0:T(8,128)(2,1)S(1)}, bf16[3,40,1152]{2,1,0:T(8,128)(2,1)S(1)}, u32[]{:S(2)}, u32[]{:S(2)}) collective-permute-start(bf16[3,40,1152]{2,1,0:T(8,128)(2,1)S(1)} %slice.62), channel_id=1, source_target_pairs={{0,224},{32,0},{64,32},{96,64},{128,96},{160,128},{192,160},{224,1... | collective-permute-start | bytes 829448 | tf_op jit(solution)/shard_map/ppermute | solution.py:187
  42.7 10.8 %collective-permute-start.11 = (bf16[3,40,1152]{2,1,0:T(8,128)(2,1)S(1)}, bf16[3,40,1152]{2,1,0:T(8,128)(2,1)S(1)}, u32[]{:S(2)}, u32[]{:S(2)}) collective-permute-start(bf16[3,40,1152]{2,1,0:T(8,128)(2,1)S(1)} %slice.60), channel_id=1, source_target_pairs={{0,32},{32,64},{64,96},{96,128},{128,160},{160,192},{192,224},{224... | collective-permute-start | bytes 829448 | tf_op jit(solution)/shard_map/ppermute | solution.py:187
  43.3 19.9 %collective-permute-start.6 = (bf16[7,40,1152]{2,1,0:T(8,128)(2,1)}, bf16[7,40,1152]{2,1,0:T(8,128)(2,1)S(1)}, u32[]{:S(2)}, u32[]{:S(2)}) collective-permute-start(bf16[7,40,1152]{2,1,0:T(8,128)(2,1)} %get-tuple-element.45), channel_id=1, source_target_pairs={{0,32},{32,64},{64,96},{96,128},{128,160},{160,192},{192,224},{224... | collective-permute-start | bytes 1935368 | tf_op jit(solution)/shard_map/ppermute | solution.py:187
  45.1 18.1 %collective-permute-start.7 = (bf16[7,40,1152]{2,1,0:T(8,128)(2,1)}, bf16[7,40,1152]{2,1,0:T(8,128)(2,1)S(1)}, u32[]{:S(2)}, u32[]{:S(2)}) collective-permute-start(bf16[7,40,1152]{2,1,0:T(8,128)(2,1)} %get-tuple-element.46), channel_id=1, source_target_pairs={{0,224},{32,0},{64,32},{96,64},{128,96},{160,128},{192,160},{224,1... | collective-permute-start | bytes 1935368 | tf_op jit(solution)/shard_map/ppermute | solution.py:187
  47.2 15.8 %collective-permute-start.10 = (bf16[6,40,1152]{2,1,0:T(8,128)(2,1)S(1)}, bf16[6,40,1152]{2,1,0:T(8,128)(2,1)S(1)}, u32[]{:S(2)}, u32[]{:S(2)}) collective-permute-start(bf16[6,40,1152]{2,1,0:T(8,128)(2,1)S(1)} %broadcast_select_fusion.1), channel_id=1, source_target_pairs={{0,8},{1,25},{8,16},{9,1},{16,24},{17,9},{24,0},{25,17},{2,10},{3,... | collective-permute-start | bytes 1658888 | tf_op jit(solution)/shard_map/ppermute | solution.py:209
  53.5 21.7 %collective-permute-start.14 = (bf16[10,40,1152]{2,1,0:T(8,128)(2,1)S(1)}, bf16[10,40,1152]{2,1,0:T(8,128)(2,1)S(1)}, u32[]{:S(2)}, u32[]{:S(2)}) collective-permute-start(bf16[10,40,1152]{2,1,0:T(8,128)(2,1)S(1)} %slice_dynamic-update-slice_fusion.4.refs_13_), channel_id=1, source_target_pairs={{0,24},{8,0},{16,8},{24,16},{1,25},{9,1},{17,9},{25,17},{2,26},{10... | collective-permute-start | bytes 2764808 | tf_op jit(solution)/shard_map/ppermute | solution.py:187
  56.6 21.1 %collective-permute-start.13 = (bf16[10,40,1152]{2,1,0:T(8,128)(2,1)S(1)}, bf16[10,40,1152]{2,1,0:T(8,128)(2,1)S(1)}, u32[]{:S(2)}, u32[]{:S(2)}) collective-permute-start(bf16[10,40,1152]{2,1,0:T(8,128)(2,1)S(1)} %slice_dynamic-update-slice_fusion.4.refs_13_), channel_id=1, source_target_pairs={{0,8},{8,16},{16,24},{24,0},{1,9},{9,17},{17,25},{25,1},{2,10},{10... | collective-permute-start | bytes 2764808 | tf_op jit(solution)/shard_map/ppermute | solution.py:187
  63.3 9.1 %collective-permute-start.16 = (bf16[5,40,1152]{2,1,0:T(8,128)(2,1)S(1)}, bf16[5,40,1152]{2,1,0:T(8,128)(2,1)S(1)}, u32[]{:S(2)}, u32[]{:S(2)}) collective-permute-start(bf16[5,40,1152]{2,1,0:T(8,128)(2,1)S(1)} %slice.67), channel_id=1, source_target_pairs={{0,224},{32,0},{64,32},{96,64},{128,96},{160,128},{192,160},{224,1... | collective-permute-start | bytes 1382408 | tf_op jit(solution)/shard_map/ppermute | solution.py:187
  65.6 9.7 %collective-permute-start.15 = (bf16[5,40,1152]{2,1,0:T(8,128)(2,1)S(1)}, bf16[5,40,1152]{2,1,0:T(8,128)(2,1)S(1)}, u32[]{:S(2)}, u32[]{:S(2)}) collective-permute-start(bf16[5,40,1152]{2,1,0:T(8,128)(2,1)S(1)} %slice.66), channel_id=1, source_target_pairs={{0,32},{32,64},{64,96},{96,128},{128,160},{160,192},{192,224},{224... | collective-permute-start | bytes 1382408 | tf_op jit(solution)/shard_map/ppermute | solution.py:187
  77.8 14.7 %collective-permute-start.21 = (bf16[10,40,1152]{2,1,0:T(8,128)(2,1)S(1)}, bf16[10,40,1152]{2,1,0:T(8,128)(2,1)S(1)}, u32[]{:S(2)}, u32[]{:S(2)}) collective-permute-start(bf16[10,40,1152]{2,1,0:T(8,128)(2,1)S(1)} %broadcast_select_fusion), channel_id=1, source_target_pairs={{0,8},{1,25},{8,16},{9,1},{16,24},{17,9},{24,0},{25,17},{2,10},{3,... | collective-permute-start | bytes 2764808 | tf_op jit(solution)/shard_map/ppermute | solution.py:209
  78.0 11.1 %collective-permute-start.20 = (bf16[2,40,1152]{2,1,0:T(8,128)(2,1)S(1)}, bf16[2,40,1152]{2,1,0:T(8,128)(2,1)S(1)}, u32[]{:S(2)}, u32[]{:S(2)}) collective-permute-start(bf16[2,40,1152]{2,1,0:T(8,128)(2,1)S(1)} %slice.71), channel_id=1, source_target_pairs={{0,224},{32,0},{64,32},{96,64},{128,96},{160,128},{192,160},{224,1... | collective-permute-start | bytes 552968 | tf_op jit(solution)/shard_map/ppermute | solution.py:187
  79.2 9.8 %collective-permute-start.17 = (bf16[2,40,1152]{2,1,0:T(8,128)(2,1)S(1)}, bf16[2,40,1152]{2,1,0:T(8,128)(2,1)S(1)}, u32[]{:S(2)}, u32[]{:S(2)}) collective-permute-start(bf16[2,40,1152]{2,1,0:T(8,128)(2,1)S(1)} %slice.68), channel_id=1, source_target_pairs={{0,32},{32,64},{64,96},{96,128},{128,160},{160,192},{192,224},{224... | collective-permute-start | bytes 552968 | tf_op jit(solution)/shard_map/ppermute | solution.py:187
  80.1 6.6 %collective-permute-start.19 = (bf16[1,40,1152]{2,1,0:T(8,128)(2,1)S(1)}, bf16[1,40,1152]{2,1,0:T(8,128)(2,1)S(1)}, u32[]{:S(2)}, u32[]{:S(2)}) collective-permute-start(bf16[1,40,1152]{2,1,0:T(8,128)(2,1)S(1)} %slice.70), channel_id=1, source_target_pairs={{0,192},{32,224},{64,0},{96,32},{128,64},{160,96},{192,128},{224,1... | collective-permute-start | bytes 276488 | tf_op jit(solution)/shard_map/ppermute | solution.py:187
  81.9 7.2 %collective-permute-start.18 = (bf16[1,40,1152]{2,1,0:T(8,128)(2,1)S(1)}, bf16[1,40,1152]{2,1,0:T(8,128)(2,1)S(1)}, u32[]{:S(2)}, u32[]{:S(2)}) collective-permute-start(bf16[1,40,1152]{2,1,0:T(8,128)(2,1)S(1)} %slice.69), channel_id=1, source_target_pairs={{0,64},{32,96},{64,128},{96,160},{128,192},{160,224},{192,0},{224,... | collective-permute-start | bytes 276488 | tf_op jit(solution)/shard_map/ppermute | solution.py:187
  95.0 2.4 %collective-permute-start.22 = (f32[4,40,1280]{2,1,0:T(8,128)S(1)}, f32[4,40,1280]{2,1,0:T(8,128)S(1)}, u32[]{:S(2)}, u32[]{:S(2)}) collective-permute-start(f32[4,40,1280]{2,1,0:T(8,128)S(1)} %get-tuple-element.60), channel_id=1, source_target_pairs={{0,1},{1,0},{2,3},{3,2},{4,5},{5,4},{6,7},{7,6},{8,9},{9,8},{10,11... | collective-permute-start | bytes 2457608 | tf_op jit(solution)/shard_map/ppermute | solution.py:187
